TPU v7x, 32 devices: a whole 2x2x4 slice. The times are simulated.
32 devices in a mesh: shard: 2 (over x), context: 4 (over y, core), tensor: 4 (over z).
Axes of the slice: x: 2, y: 2, z: 4, core: 2. Of those that a mesh axis runs over, the one named last changes fastest.
Arguments:
- clip_input: bfloat16 [4, 2, 8, 196, 768], P(None, 'shard', 'tensor', 'context'), may hold values from -6 to 6
- clip_slot: int32 [4, 2], P(None, 'shard'), may hold values from 0 to 1, as said below
- norm_gain: bfloat16 [3, 768], P(None, 'shard'), may hold values from 0.25 to 1.75
- norm_shift: bfloat16 [3, 768], P(None, 'shard'), may hold values from -2 to 2
- attention_in: bfloat16 [2, 768, 3, 768], P(None, 'shard', None, 'tensor'), may hold values from -0.21875 to 0.21875
- attention_bias: bfloat16 [2, 2, 12, 64], P(None, None, 'tensor', 'shard'), may hold values from -2 to 2
- attention_out: bfloat16 [2, 768, 768], P(None, 'tensor', 'shard'), may hold values from -0.625 to 0.625
- branch_bias: bfloat16 [4, 768], P(None, 'shard'), may hold values from -2 to 2
- temporal_fc: bfloat16 [768, 768], P('shard'), may hold values from -0.21875 to 0.21875
- hidden_in: bfloat16 [768, 3072], P('shard', 'tensor'), may hold values from -0.21875 to 0.21875
- hidden_bias: bfloat16 [24, 128], P('tensor', 'shard'), may hold values from -2 to 2
- hidden_out: bfloat16 [3072, 768], P('tensor', 'shard'), may hold values from -0.109375 to 0.109375
- output_grad: bfloat16 [4, 2, 8, 196, 768], P(None, 'shard', 'tensor', 'context'), may hold values from -6 to 6
Outputs:
- layer_out: bfloat16 [4, 2, 8, 196, 768], P(None, 'shard', 'tensor', 'context')
- input_grad: bfloat16 [4, 2, 8, 196, 768], P(None, 'shard', 'tensor', 'context')
- norm_gain_grad: float32 [3, 768], P(None, 'shard')
- norm_shift_grad: float32 [3, 768], P(None, 'shard')
- attention_in_grad: float32 [2, 768, 3, 768], P(None, 'shard', None, 'tensor')
- attention_bias_grad: float32 [2, 2, 12, 64], P(None, None, 'tensor', 'shard')
- attention_out_grad: float32 [2, 768, 768], P(None, 'tensor', 'shard')
- branch_bias_grad: float32 [4, 768], P(None, 'shard')
- temporal_fc_grad: float32 [768, 768], P('shard')
- hidden_in_grad: float32 [768, 3072], P('shard', 'tensor')
- hidden_bias_grad: float32 [24, 128], P('tensor', 'shard')
- hidden_out_grad: float32 [3072, 768], P('tensor', 'shard')
Inputs may be any that keep to these rules, and one draw needn't show every extreme that they name: `clip_slot`: in micro-batch 0 every slot holds a clip; in every later micro-batch exactly 1 of the 2 slots do, which ones drawn from the seed.
All inputs are finite; a program needn't handle non-finite values.
Results may differ from a plain program's by a relative error of at most 0.03.
Values may be sent and summed in bfloat16 or wider, within the bound.
No kernel may reach another device: no remote copies, remote signals or barrier semaphores. Data moves between devices by JAX's collectives and lax.ppermute only.
A program may use at most 128 MiB of HBM per device.

v0:
```python
from functools import partial

import jax
import jax.numpy as jnp
from jax import lax
from jax.sharding import PartitionSpec as P

HEAD_DIM = 64


EPS = 1e-06
SQRT_HALF = 0.7071067811865476
INV_ROOT_TAU = 0.3989422804014327
TEMPORAL = ("iphd,jphd->phij", "phij,jphd->iphd", "phij,iphd->jphd")
SPATIAL = ("fqhd,fkhd->fhqk", "fhqk,fkhd->fqhd", "fhqk,fqhd->fkhd")


def normalize(values, gain, shift):
    centred = values - jnp.mean(values, -1, keepdims=True)
    inverse = lax.rsqrt(jnp.mean(centred * centred, -1, keepdims=True) + EPS)
    unit = centred * inverse
    return ((unit * gain + shift).astype(jnp.bfloat16), unit, inverse)


def normalize_back(grad, unit, inverse, gain):
    scaled = grad * gain
    inner = (
        scaled
        - jnp.mean(scaled, -1, keepdims=True)
        - unit * jnp.mean(scaled * unit, -1, keepdims=True)
    )
    return (inverse * inner, jnp.sum(grad * unit, axis=(0, 1)), jnp.sum(grad, axis=(0, 1)))


def gelu(values):
    return 0.5 * values * (1.0 + lax.erf(values * SQRT_HALF))


def gelu_slope(values):
    return (
        0.5 * (1.0 + lax.erf(values * SQRT_HALF))
        + values * jnp.exp(-0.5 * values * values) * INV_ROOT_TAU
    )


def attend(query, key, value, forms, scale):
    scores = jnp.einsum(forms[0], query, key, preferred_element_type=jnp.float32) * scale
    top = jnp.max(scores, -1, keepdims=True)
    weights = jnp.exp(scores - top)
    total = jnp.sum(weights, -1, keepdims=True)
    probs = (weights / total).astype(jnp.bfloat16)
    mixed = jnp.einsum(forms[1], probs, value, preferred_element_type=jnp.float32)
    return (mixed.astype(jnp.bfloat16), top + jnp.log(total))


def attend_back(query, key, value, logsum, out_grad, forms, scale):
    scores = jnp.einsum(forms[0], query, key, preferred_element_type=jnp.float32) * scale
    probs = jnp.exp(scores - logsum)
    value_grad = jnp.einsum(
        forms[2], probs.astype(jnp.bfloat16), out_grad, preferred_element_type=jnp.float32
    )
    prob_grad = jnp.einsum(forms[0], out_grad, value, preferred_element_type=jnp.float32)
    inner = jnp.sum(probs * prob_grad, -1, keepdims=True)
    score_grad = (probs * (prob_grad - inner)).astype(jnp.bfloat16)
    query_grad = jnp.einsum(forms[1], score_grad, key, preferred_element_type=jnp.float32) * scale
    key_grad = jnp.einsum(forms[2], score_grad, query, preferred_element_type=jnp.float32) * scale
    return (query_grad, key_grad, value_grad)


def project_in(piece, first, weight, pair):
    shift = jnp.stack([pair[0], jnp.zeros_like(pair[0]), pair[1]]).astype(jnp.float32)
    mixed = jnp.einsum("fpd,dcw->fpcw", piece, weight, preferred_element_type=jnp.float32)
    return (piece, (mixed + shift).astype(jnp.bfloat16))


def expand(piece, first, weight, shift):
    return (
        piece,
        jnp.einsum("fpd,dk->fpk", piece, weight, preferred_element_type=jnp.float32) + shift,
    )


def retract(piece, first, weight):
    return (piece, jnp.einsum("fpd,kd->fpk", piece, weight, preferred_element_type=jnp.float32))


def project_out(first, count, mixed, weight):
    return jnp.einsum("fpk,kd->fpd", mixed, weight, preferred_element_type=jnp.float32)


def project_back(first, count, grads, weight):
    return jnp.einsum("fpk,dk->fpd", grads, weight, preferred_element_type=jnp.float32)


def gather_rows(rows_low, project):
    return project(lax.all_gather(rows_low, "tensor", axis=0, tiled=True), jnp.int32(0))


def gather_grad_rows(rows_low, project):
    return project(lax.all_gather(rows_low, "tensor", axis=0, tiled=True), jnp.int32(0))


def sum_branch(term, count):
    return lax.psum_scatter(
        term(jnp.int32(0), count * lax.axis_size("tensor")).astype(jnp.bfloat16),
        "tensor",
        scatter_dimension=0,
        tiled=True,
    ).astype(jnp.float32)


def sum_input_grad(term, count):
    return lax.psum_scatter(
        term(jnp.int32(0), count * lax.axis_size("tensor")).astype(jnp.bfloat16),
        "tensor",
        scatter_dimension=0,
        tiled=True,
    ).astype(jnp.float32)


def token_sum(values):
    return jnp.sum(values.astype(jnp.float32), axis=(0, 1))


def qkv_backward(seen, weight, query_grad, key_grad, value_grad, local_frames):
    frames, places = (query_grad.shape[0], query_grad.shape[1])
    width = weight.shape[2]
    stacked = jnp.stack(
        [
            query_grad.reshape(frames, places, width),
            key_grad.reshape(frames, places, width),
            value_grad.reshape(frames, places, width),
        ],
        2,
    ).astype(jnp.bfloat16)
    weight_grad = jnp.einsum("fpd,fpcw->dcw", seen, stacked, preferred_element_type=jnp.float32)
    sums = token_sum(stacked)
    flat_grad = stacked.reshape(frames, places, 3 * width)
    flat_weight = weight.reshape(weight.shape[0], 3 * width)
    normed_grad = sum_input_grad(
        partial(project_back, grads=flat_grad, weight=flat_weight), local_frames
    )
    return (weight_grad, jnp.stack([sums[0], sums[2]]), normed_grad)


def layer_pass(weights, clip, live, cotangent):
    gains, shifts, qkv_w, qv_bias, proj_w, branch, fc_w, up_w, up_bias, down_w = weights
    local_frames = clip.shape[0]
    heads = qv_bias.shape[2]
    width = heads * HEAD_DIM
    scale = HEAD_DIM ** (-0.5)
    gains = gains.astype(jnp.float32)
    shifts = shifts.astype(jnp.float32)
    branch = branch.astype(jnp.float32)
    pairs = qv_bias.reshape(2, 2, width)
    up_shift = up_bias.reshape(-1).astype(jnp.float32)
    start = clip.astype(jnp.float32)
    normed_a, unit_a, inverse_a = normalize(start, gains[0], shifts[0])
    seen_a, qkv_a = gather_rows(normed_a, partial(project_in, weight=qkv_w[0], pair=pairs[0]))
    shaped_a = qkv_a.reshape(qkv_a.shape[:3] + (heads, HEAD_DIM))
    mixed_a, logsum_a = attend(
        shaped_a[:, :, 0], shaped_a[:, :, 1], shaped_a[:, :, 2], TEMPORAL, scale
    )
    flat_a = mixed_a.reshape(mixed_a.shape[0], mixed_a.shape[1], width)
    temporal_low = (
        sum_branch(partial(project_out, mixed=flat_a, weight=proj_w[0]), local_frames) + branch[0]
    ).astype(jnp.bfloat16)
    after_a = (
        start
        + jnp.einsum("fpk,kd->fpd", temporal_low, fc_w, preferred_element_type=jnp.float32)
        + branch[1]
    )
    normed_b, unit_b, inverse_b = normalize(after_a, gains[1], shifts[1])
    seen_b, qkv_b = gather_rows(normed_b, partial(project_in, weight=qkv_w[1], pair=pairs[1]))
    frames, places = (qkv_b.shape[0], qkv_b.shape[1])
    keys_b, values_b = (
        lax.all_gather(qkv_b[:, :, 1], "context", axis=1, tiled=True),
        lax.all_gather(qkv_b[:, :, 2], "context", axis=1, tiled=True),
    )
    all_places = keys_b.shape[1]
    keys_b = keys_b.reshape(frames, all_places, heads, HEAD_DIM)
    values_b = values_b.reshape(frames, all_places, heads, HEAD_DIM)
    query_b = qkv_b[:, :, 0].reshape(frames, places, heads, HEAD_DIM)
    mixed_b, logsum_b = attend(query_b, keys_b, values_b, SPATIAL, scale)
    flat_b = mixed_b.reshape(frames, places, width)
    after_b = (
        after_a
        + sum_branch(partial(project_out, mixed=flat_b, weight=proj_w[1]), local_frames)
        + branch[2]
    )
    normed_c, unit_c, inverse_c = normalize(after_b, gains[2], shifts[2])
    seen_c, hidden_c = gather_rows(normed_c, partial(expand, weight=up_w, shift=up_shift))
    active_c = gelu(hidden_c).astype(jnp.bfloat16)
    result = (
        after_b
        + sum_branch(partial(project_out, mixed=active_c, weight=down_w), local_frames)
        + branch[3]
    )
    mask = live.astype(jnp.float32)
    layer_rows = (mask * result).astype(jnp.bfloat16)
    grad = mask * cotangent.astype(jnp.float32)
    low_c = grad.astype(jnp.bfloat16)
    seen_grad_c, active_grad = gather_grad_rows(low_c, partial(retract, weight=down_w))
    down_grad = jnp.einsum("fpk,fpd->kd", active_c, seen_grad_c, preferred_element_type=jnp.float32)
    hidden_grad = (active_grad * gelu_slope(hidden_c)).astype(jnp.bfloat16)
    up_grad = jnp.einsum("fpd,fpk->dk", seen_c, hidden_grad, preferred_element_type=jnp.float32)
    up_bias_grad = token_sum(hidden_grad)
    normed_grad_c = sum_input_grad(
        partial(project_back, grads=hidden_grad, weight=up_w), local_frames
    )
    back_c, gain_c, shift_c = normalize_back(normed_grad_c, unit_c, inverse_c, gains[2])
    branch_grad_3 = token_sum(low_c)
    grad = grad + back_c
    low_b = grad.astype(jnp.bfloat16)
    seen_grad_b, mixed_grad_b = gather_grad_rows(low_b, partial(retract, weight=proj_w[1]))
    proj_grad_b = jnp.einsum("fpk,fpd->kd", flat_b, seen_grad_b, preferred_element_type=jnp.float32)
    branch_grad_2 = token_sum(low_b)
    mixed_grad_b = mixed_grad_b.astype(jnp.bfloat16).reshape(frames, places, heads, HEAD_DIM)
    query_grad_b, key_grad_b, value_grad_b = attend_back(
        query_b, keys_b, values_b, logsum_b, mixed_grad_b, SPATIAL, scale
    )
    key_grad_b, value_grad_b = (
        lax.psum_scatter(
            key_grad_b.reshape(frames, all_places, width).astype(jnp.bfloat16),
            "context",
            scatter_dimension=1,
            tiled=True,
        ).astype(jnp.float32),
        lax.psum_scatter(
            value_grad_b.reshape(frames, all_places, width).astype(jnp.bfloat16),
            "context",
            scatter_dimension=1,
            tiled=True,
        ).astype(jnp.float32),
    )
    qkv_grad_b, pair_grad_b, normed_grad_b = qkv_backward(
        seen_b, qkv_w[1], query_grad_b, key_grad_b, value_grad_b, local_frames
    )
    back_b, gain_b, shift_b = normalize_back(normed_grad_b, unit_b, inverse_b, gains[1])
    grad = grad + back_b
    low_fc = grad.astype(jnp.bfloat16)
    fc_grad = jnp.einsum("fpk,fpd->kd", temporal_low, low_fc, preferred_element_type=jnp.float32)
    branch_grad_1 = token_sum(low_fc)
    temporal_grad = jnp.einsum(
        "fpd,kd->fpk", low_fc, fc_w, preferred_element_type=jnp.float32
    ).astype(jnp.bfloat16)
    branch_grad_0 = token_sum(temporal_grad)
    seen_grad_a, mixed_grad_a = gather_grad_rows(temporal_grad, partial(retract, weight=proj_w[0]))
    proj_grad_a = jnp.einsum("fpk,fpd->kd", flat_a, seen_grad_a, preferred_element_type=jnp.float32)
    mixed_grad_a = mixed_grad_a.astype(jnp.bfloat16).reshape(
        shaped_a.shape[0], shaped_a.shape[1], heads, HEAD_DIM
    )
    query_grad_a, key_grad_a, value_grad_a = attend_back(
        shaped_a[:, :, 0],
        shaped_a[:, :, 1],
        shaped_a[:, :, 2],
        logsum_a,
        mixed_grad_a,
        TEMPORAL,
        scale,
    )
    qkv_grad_a, pair_grad_a, normed_grad_a = qkv_backward(
        seen_a, qkv_w[0], query_grad_a, key_grad_a, value_grad_a, local_frames
    )
    back_a, gain_a, shift_a = normalize_back(normed_grad_a, unit_a, inverse_a, gains[0])
    grad = grad + back_a
    input_rows = grad.astype(jnp.bfloat16)
    grads = (
        jnp.stack([gain_a, gain_b, gain_c]),
        jnp.stack([shift_a, shift_b, shift_c]),
        jnp.stack([qkv_grad_a, qkv_grad_b]),
        jnp.stack([pair_grad_a, pair_grad_b]).reshape(2, 2, heads, HEAD_DIM),
        jnp.stack([proj_grad_a, proj_grad_b]),
        jnp.stack([branch_grad_0, branch_grad_1, branch_grad_2, branch_grad_3]),
        fc_grad,
        up_grad,
        up_bias_grad.reshape(up_bias.shape),
        down_grad,
    )
    return (layer_rows, input_rows, grads)


def body(
    clip_input,
    clip_slot,
    norm_gain,
    norm_shift,
    attention_in,
    attention_bias,
    attention_out,
    branch_bias,
    temporal_fc,
    hidden_in,
    hidden_bias,
    hidden_out,
    output_grad,
):
    shards = (
        norm_gain,
        norm_shift,
        attention_in,
        attention_bias,
        attention_out,
        branch_bias,
        temporal_fc,
        hidden_in,
        hidden_bias,
        hidden_out,
    )
    along = (1, 1, 1, 3, 2, 1, 0, 0, 1, 1)
    groups = lax.axis_size("shard")
    zeros = tuple(
        (
            jnp.zeros(
                tuple(
                    (
                        extent * groups if index == dim else extent
                        for index, extent in enumerate(item.shape)
                    )
                ),
                jnp.float32,
            )
            for item, dim in zip(shards, along)
        )
    )

    def micro(totals, batch):
        clip, live, cotangent = batch
        weights = (
            lax.all_gather(shards[0], "shard", axis=1, tiled=True),
            lax.all_gather(shards[1], "shard", axis=1, tiled=True),
            lax.all_gather(shards[2], "shard", axis=1, tiled=True),
            lax.all_gather(shards[3], "shard", axis=3, tiled=True),
            lax.all_gather(shards[4], "shard", axis=2, tiled=True),
            lax.all_gather(shards[5], "shard", axis=1, tiled=True),
            lax.all_gather(shards[6], "shard", axis=0, tiled=True),
            lax.all_gather(shards[7], "shard", axis=0, tiled=True),
            lax.all_gather(shards[8], "shard", axis=1, tiled=True),
            lax.all_gather(shards[9], "shard", axis=1, tiled=True),
        )
        layer_rows, input_rows, grads = layer_pass(weights, clip, live, cotangent)
        totals = jax.tree.map(lambda first, second: first + second, totals, grads)
        return (totals, (layer_rows, input_rows))

    totals, (layer_rows, input_rows) = lax.scan(
        micro, zeros, (clip_input[:, 0], clip_slot[:, 0], output_grad[:, 0])
    )
    pieces = (
        lax.psum_scatter(
            totals[0].astype(jnp.bfloat16), "shard", scatter_dimension=1, tiled=True
        ).astype(jnp.float32),
        lax.psum_scatter(
            totals[1].astype(jnp.bfloat16), "shard", scatter_dimension=1, tiled=True
        ).astype(jnp.float32),
        lax.psum_scatter(
            totals[2].astype(jnp.bfloat16), "shard", scatter_dimension=1, tiled=True
        ).astype(jnp.float32),
        lax.psum_scatter(
            totals[3].astype(jnp.bfloat16), "shard", scatter_dimension=3, tiled=True
        ).astype(jnp.float32),
        lax.psum_scatter(
            totals[4].astype(jnp.bfloat16), "shard", scatter_dimension=2, tiled=True
        ).astype(jnp.float32),
        lax.psum_scatter(
            totals[5].astype(jnp.bfloat16), "shard", scatter_dimension=1, tiled=True
        ).astype(jnp.float32),
        lax.psum_scatter(
            totals[6].astype(jnp.bfloat16), "shard", scatter_dimension=0, tiled=True
        ).astype(jnp.float32),
        lax.psum_scatter(
            totals[7].astype(jnp.bfloat16), "shard", scatter_dimension=0, tiled=True
        ).astype(jnp.float32),
        lax.psum_scatter(
            totals[8].astype(jnp.bfloat16), "shard", scatter_dimension=1, tiled=True
        ).astype(jnp.float32),
        lax.psum_scatter(
            totals[9].astype(jnp.bfloat16), "shard", scatter_dimension=1, tiled=True
        ).astype(jnp.float32),
    )
    (
        gain_grad,
        shift_grad,
        qkv_grad,
        pair_grad,
        proj_grad,
        branch_grad,
        fc_grad,
        up_grad,
        up_bias_grad,
        down_grad,
    ) = pieces
    gain_grad, shift_grad, branch_grad, fc_grad = (
        lax.psum(gain_grad.astype(jnp.bfloat16), ("context", "tensor")).astype(jnp.float32),
        lax.psum(shift_grad.astype(jnp.bfloat16), ("context", "tensor")).astype(jnp.float32),
        lax.psum(branch_grad.astype(jnp.bfloat16), ("context", "tensor")).astype(jnp.float32),
        lax.psum(fc_grad.astype(jnp.bfloat16), ("context", "tensor")).astype(jnp.float32),
    )
    qkv_grad, pair_grad, proj_grad, up_grad, up_bias_grad, down_grad = (
        lax.psum(qkv_grad.astype(jnp.bfloat16), "context").astype(jnp.float32),
        lax.psum(pair_grad.astype(jnp.bfloat16), "context").astype(jnp.float32),
        lax.psum(proj_grad.astype(jnp.bfloat16), "context").astype(jnp.float32),
        lax.psum(up_grad.astype(jnp.bfloat16), "context").astype(jnp.float32),
        lax.psum(up_bias_grad.astype(jnp.bfloat16), "context").astype(jnp.float32),
        lax.psum(down_grad.astype(jnp.bfloat16), "context").astype(jnp.float32),
    )
    return (
        layer_rows[:, None],
        input_rows[:, None],
        gain_grad,
        shift_grad,
        qkv_grad,
        pair_grad,
        proj_grad,
        branch_grad,
        fc_grad,
        up_grad,
        up_bias_grad,
        down_grad,
    )


def solution(mesh):
    placed = (
        P(None, "shard", "tensor", "context", None),
        P(None, "shard"),
        P(None, "shard"),
        P(None, "shard"),
        P(None, "shard", None, "tensor"),
        P(None, None, "tensor", "shard"),
        P(None, "tensor", "shard"),
        P(None, "shard"),
        P("shard", None),
        P("shard", "tensor"),
        P("tensor", "shard"),
        P("tensor", "shard"),
        P(None, "shard", "tensor", "context", None),
    )
    return jax.shard_map(
        body,
        mesh=mesh,
        in_specs=placed,
        out_specs=(
            P(None, "shard", "tensor", "context", None),
            P(None, "shard", "tensor", "context", None),
            P(None, "shard"),
            P(None, "shard"),
            P(None, "shard", None, "tensor"),
            P(None, None, "tensor", "shard"),
            P(None, "tensor", "shard"),
            P(None, "shard"),
            P("shard", None),
            P("shard", "tensor"),
            P("tensor", "shard"),
            P("tensor", "shard"),
        ),
        check_vma=False,
    )
```

profile of v0, /device:TPU:0, one launch (start us, length us, event | category | flops | bytes accessed | tf_op | source)
XLA Modules:
  0.0 2072.7 jit_solution(15062299218756334080)
XLA Ops:
  11.3 1708.6 %while.33 = (s32[]{:T(128)}, f32[3,768]{1,0:T(4,128)}, f32[3,768]{1,0:T(4,128)}, f32[2,768,3,192]{1,3,2,0:T(8,128)}, f32[2,2,3,64]{3,2,1,0:T(4,128)}, /*index=5*...) while((s32[]{:T(128)}, f32[3,768]{1,0:T(4,128)}, ...), condition=%wide.region_40.41_spmd.clone, body=%wide.region_0.40_spmd.clone.sunk | while | flops 6112532480 | bytes 269198592 | solution.py:345
  71.1 25.5 %reduce-scatter.55.cloned.1.call-done = bf16[2,49,768]{2,1,0:T(8,128)(2,1)} async-done(((bf16[8,49,768]{2,1,0:T(8,128)(2,1)}), bf16[2,49,768]{2,1,0:T(8,128)(2,1)}) %reduce-scatter.55.cloned.1.call-update) | async-done | bytes 150544 | tf_op jit(solution)/shard_map/while/body/eval_jaxpr/reduce_scatter | solution.py:104
  154.0 22.8 %all_gather.95 = bf16[8,49,768]{2,1,0:T(8,128)(2,1)} all-gather(bf16[2,49,768]{2,1,0:T(8,128)(2,1)S(1)} %get-tuple-element.744), channel_id=1, replica_groups=mesh['shard'=2,'context'=4,'tensor'=4] {'tensor'}, dimensions={0}, use_global_device_ids=true | all-gather | bytes 752640 | tf_op jit(solution)/shard_map/while/body/eval_jaxpr/all_gather | solution.py:100
  252.2 21.4 %reduce-scatter.61.cloned.1.call-done = bf16[2,49,768]{2,1,0:T(8,128)(2,1)} async-done(((bf16[8,49,768]{2,1,0:T(8,128)(2,1)}), bf16[2,49,768]{2,1,0:T(8,128)(2,1)}) %reduce-scatter.61.cloned.1.call-update) | async-done | bytes 150544 | tf_op jit(solution)/shard_map/while/body/eval_jaxpr/reduce_scatter | solution.py:104
  328.1 25.4 %reduce-scatter.63.cloned.1.call-done = bf16[8,49,192]{2,0,1:T(8,128)(2,1)} async-done(((bf16[8,196,192]{2,0,1:T(8,128)(2,1)}), bf16[8,49,192]{2,0,1:T(8,128)(2,1)}) %reduce-scatter.63.cloned.1.call-update) | async-done | bytes 150544 | tf_op jit(solution)/shard_map/while/body/eval_jaxpr/reduce_scatter | solution.py:229
  496.2 25.4 %reduce-scatter.55.cloned.1.call-done = bf16[2,49,768]{2,1,0:T(8,128)(2,1)} async-done(((bf16[8,49,768]{2,1,0:T(8,128)(2,1)}), bf16[2,49,768]{2,1,0:T(8,128)(2,1)}) %reduce-scatter.55.cloned.1.call-update) | async-done | bytes 150544 | tf_op jit(solution)/shard_map/while/body/eval_jaxpr/reduce_scatter | solution.py:104
  579.0 22.8 %all_gather.95 = bf16[8,49,768]{2,1,0:T(8,128)(2,1)} all-gather(bf16[2,49,768]{2,1,0:T(8,128)(2,1)S(1)} %get-tuple-element.744), channel_id=1, replica_groups=mesh['shard'=2,'context'=4,'tensor'=4] {'tensor'}, dimensions={0}, use_global_device_ids=true | all-gather | bytes 752640 | tf_op jit(solution)/shard_map/while/body/eval_jaxpr/all_gather | solution.py:100
  677.1 21.2 %reduce-scatter.61.cloned.1.call-done = bf16[2,49,768]{2,1,0:T(8,128)(2,1)} async-done(((bf16[8,49,768]{2,1,0:T(8,128)(2,1)}), bf16[2,49,768]{2,1,0:T(8,128)(2,1)}) %reduce-scatter.61.cloned.1.call-update) | async-done | bytes 150544 | tf_op jit(solution)/shard_map/while/body/eval_jaxpr/reduce_scatter | solution.py:104
  752.8 25.5 %reduce-scatter.63.cloned.1.call-done = bf16[8,49,192]{2,0,1:T(8,128)(2,1)} async-done(((bf16[8,196,192]{2,0,1:T(8,128)(2,1)}), bf16[8,49,192]{2,0,1:T(8,128)(2,1)}) %reduce-scatter.63.cloned.1.call-update) | async-done | bytes 150544 | tf_op jit(solution)/shard_map/while/body/eval_jaxpr/reduce_scatter | solution.py:229
  921.2 25.4 %reduce-scatter.55.cloned.1.call-done = bf16[2,49,768]{2,1,0:T(8,128)(2,1)} async-done(((bf16[8,49,768]{2,1,0:T(8,128)(2,1)}), bf16[2,49,768]{2,1,0:T(8,128)(2,1)}) %reduce-scatter.55.cloned.1.call-update) | async-done | bytes 150544 | tf_op jit(solution)/shard_map/while/body/eval_jaxpr/reduce_scatter | solution.py:104
  1003.7 23.0 %all_gather.95 = bf16[8,49,768]{2,1,0:T(8,128)(2,1)} all-gather(bf16[2,49,768]{2,1,0:T(8,128)(2,1)S(1)} %get-tuple-element.744), channel_id=1, replica_groups=mesh['shard'=2,'context'=4,'tensor'=4] {'tensor'}, dimensions={0}, use_global_device_ids=true | all-gather | bytes 752640 | tf_op jit(solution)/shard_map/while/body/eval_jaxpr/all_gather | solution.py:100
  1050.5 20.0 all-gather.23.cloned.1.call-done
  1102.1 21.4 %reduce-scatter.61.cloned.1.call-done = bf16[2,49,768]{2,1,0:T(8,128)(2,1)} async-done(((bf16[8,49,768]{2,1,0:T(8,128)(2,1)}), bf16[2,49,768]{2,1,0:T(8,128)(2,1)}) %reduce-scatter.61.cloned.1.call-update) | async-done | bytes 150544 | tf_op jit(solution)/shard_map/while/body/eval_jaxpr/reduce_scatter | solution.py:104
  1178.1 25.6 %reduce-scatter.63.cloned.1.call-done = bf16[8,49,192]{2,0,1:T(8,128)(2,1)} async-done(((bf16[8,196,192]{2,0,1:T(8,128)(2,1)}), bf16[8,49,192]{2,0,1:T(8,128)(2,1)}) %reduce-scatter.63.cloned.1.call-update) | async-done | bytes 150544 | tf_op jit(solution)/shard_map/while/body/eval_jaxpr/reduce_scatter | solution.py:229
  1346.1 25.4 %reduce-scatter.55.cloned.1.call-done = bf16[2,49,768]{2,1,0:T(8,128)(2,1)} async-done(((bf16[8,49,768]{2,1,0:T(8,128)(2,1)}), bf16[2,49,768]{2,1,0:T(8,128)(2,1)}) %reduce-scatter.55.cloned.1.call-update) | async-done | bytes 150544 | tf_op jit(solution)/shard_map/while/body/eval_jaxpr/reduce_scatter | solution.py:104
  1429.1 22.5 %all_gather.95 = bf16[8,49,768]{2,1,0:T(8,128)(2,1)} all-gather(bf16[2,49,768]{2,1,0:T(8,128)(2,1)S(1)} %get-tuple-element.744), channel_id=1, replica_groups=mesh['shard'=2,'context'=4,'tensor'=4] {'tensor'}, dimensions={0}, use_global_device_ids=true | all-gather | bytes 752640 | tf_op jit(solution)/shard_map/while/body/eval_jaxpr/all_gather | solution.py:100
  1475.2 20.2 all-gather.23.cloned.1.call-done
  1527.1 21.3 %reduce-scatter.61.cloned.1.call-done = bf16[2,49,768]{2,1,0:T(8,128)(2,1)} async-done(((bf16[8,49,768]{2,1,0:T(8,128)(2,1)}), bf16[2,49,768]{2,1,0:T(8,128)(2,1)}) %reduce-scatter.61.cloned.1.call-update) | async-done | bytes 150544 | tf_op jit(solution)/shard_map/while/body/eval_jaxpr/reduce_scatter | solution.py:104
  1603.0 25.4 %reduce-scatter.63.cloned.1.call-done = bf16[8,49,192]{2,0,1:T(8,128)(2,1)} async-done(((bf16[8,196,192]{2,0,1:T(8,128)(2,1)}), bf16[8,49,192]{2,0,1:T(8,128)(2,1)}) %reduce-scatter.63.cloned.1.call-update) | async-done | bytes 150544 | tf_op jit(solution)/shard_map/while/body/eval_jaxpr/reduce_scatter | solution.py:229
  1764.2 21.9 %reduce-scatter.53.cloned.1.call-done = bf16[384,768]{1,0:T(8,128)(2,1)} async-done(((bf16[768,768]{1,0:T(8,128)(2,1)}), bf16[384,768]{1,0:T(8,128)(2,1)}) %reduce-scatter.53.cloned.1.call-update) | async-done | bytes 589840
  1788.3 29.0 %reduce-scatter.43.cloned.1.call-done = bf16[384,1152]{1,0:T(8,128)(2,1)} async-done(((bf16[768,1152]{1,0:T(8,128)(2,1)}), bf16[384,1152]{1,0:T(8,128)(2,1)}) %reduce-scatter.43.cloned.1.call-update) | async-done | bytes 884752
  1906.2 35.0 %all-reduce = (bf16[3,384]{1,0:T(4,128)(2,1)S(1)}, bf16[3,384]{1,0:T(4,128)(2,1)S(1)}, bf16[4,384]{1,0:T(4,128)(2,1)S(1)}) all-reduce(bf16[3,384]{1,0:T(4,128)(2,1)S(1)} %copy.207, bf16[3,384]{1,0:T(4,128)(2,1)S(1)} %copy.209, bf16[4,384]{1,0:T(4,128)(2,1)S(1)} %copy.217), channel_id=1, replica_groups=mesh['shard'=2,'context'=4,'tensor'=4] {'context','tensor'}, use_global_device_ids=true, to_apply=%region_42.43 | all-reduce | flops 3840 | bytes 15360 | tf_op jit(solution)/shard_map/psum | solution.py:393
  1943.0 57.7 %all-reduce.6.cloned.1.call-done = bf16[384,768]{1,0:T(8,128)(2,1)} async-done(((bf16[384,768]{1,0:T(8,128)(2,1)}), bf16[384,768]{1,0:T(8,128)(2,1)}) %all-reduce.6.cloned.1.call-update) | async-done | bytes 589840 | tf_op jit(solution)/shard_map/psum | solution.py:396
  2002.9 56.7 %all-reduce.8.cloned.1.call-done = (bf16[2,384,3,192]{1,3,2,0:T(8,128)(2,1)}, bf16[2,192,384]{2,1,0:T(8,128)(2,1)}, bf16[384,768]{1,0:T(8,128)(2,1)}, bf16[768,384]{1,0:T(8,128)(2,1)}) async-done(((bf16[2,384,3,192]{1,3,2,0:T(8,128)(2,1)}, bf16[2,192,384]{2,1,0:T(8,128)(2,1)}, bf16[384,768]{1,0:T(8,128)(2,1)}, bf16[768,384]{1,0:T(8,128)(2,1)}), (bf16[2,384,3,192]{1,3,2,0:T(8,128)(2,1)}, ...) | async-done | bytes 2359312 | tf_op jit(solution)/shard_map/psum | solution.py:399
  (1597 shorter events, 1422.0 us)
Async XLA Ops:
  12.8 83.9 %reduce-scatter.55.cloned.1.call-start = ((), (), s32[]{:S(2)}) async-start(), calls=%async_computation.32 | async-start | bytes 860160 | tf_op jit(solution)/shard_map/while/body/eval_jaxpr/reduce_scatter | solution.py:104
  62.0 114.8 %reduce-scatter.57.cloned.1.call-start = ((), (), s32[]{:S(2)}) async-start(), calls=%async_computation.33 | async-start | bytes 860160 | tf_op jit(solution)/shard_map/while/body/eval_jaxpr/reduce_scatter | solution.py:104
  146.1 103.1 %reduce-scatter.59.cloned.1.call-start = ((), (), s32[]{:S(2)}) async-start(), calls=%async_computation.36 | async-start | bytes 860160 | tf_op jit(solution)/shard_map/while/body/eval_jaxpr/reduce_scatter | solution.py:113
  229.7 97.4 %reduce-scatter.65.cloned.1.call-start = ((), (), s32[]{:S(2)}) async-start(), calls=%async_computation.39 | async-start | bytes 1003520 | tf_op jit(solution)/shard_map/while/body/eval_jaxpr/reduce_scatter | solution.py:223
  440.8 80.8 %reduce-scatter.55.cloned.1.call-start = ((), (), s32[]{:S(2)}) async-start(), calls=%async_computation.32 | async-start | bytes 860160 | tf_op jit(solution)/shard_map/while/body/eval_jaxpr/reduce_scatter | solution.py:104
  487.5 114.3 %reduce-scatter.57.cloned.1.call-start = ((), (), s32[]{:S(2)}) async-start(), calls=%async_computation.33 | async-start | bytes 860160 | tf_op jit(solution)/shard_map/while/body/eval_jaxpr/reduce_scatter | solution.py:104
  571.1 103.1 %reduce-scatter.59.cloned.1.call-start = ((), (), s32[]{:S(2)}) async-start(), calls=%async_computation.36 | async-start | bytes 860160 | tf_op jit(solution)/shard_map/while/body/eval_jaxpr/reduce_scatter | solution.py:113
  654.6 97.3 %reduce-scatter.65.cloned.1.call-start = ((), (), s32[]{:S(2)}) async-start(), calls=%async_computation.39 | async-start | bytes 1003520 | tf_op jit(solution)/shard_map/while/body/eval_jaxpr/reduce_scatter | solution.py:223
  865.8 80.7 %reduce-scatter.55.cloned.1.call-start = ((), (), s32[]{:S(2)}) async-start(), calls=%async_computation.32 | async-start | bytes 860160 | tf_op jit(solution)/shard_map/while/body/eval_jaxpr/reduce_scatter | solution.py:104
  912.5 114.2 %reduce-scatter.57.cloned.1.call-start = ((), (), s32[]{:S(2)}) async-start(), calls=%async_computation.33 | async-start | bytes 860160 | tf_op jit(solution)/shard_map/while/body/eval_jaxpr/reduce_scatter | solution.py:104
  995.8 103.4 %reduce-scatter.59.cloned.1.call-start = ((), (), s32[]{:S(2)}) async-start(), calls=%async_computation.36 | async-start | bytes 860160 | tf_op jit(solution)/shard_map/while/body/eval_jaxpr/reduce_scatter | solution.py:113
  1079.6 97.5 %reduce-scatter.65.cloned.1.call-start = ((), (), s32[]{:S(2)}) async-start(), calls=%async_computation.39 | async-start | bytes 1003520 | tf_op jit(solution)/shard_map/while/body/eval_jaxpr/reduce_scatter | solution.py:223
  1337.7 113.9 %reduce-scatter.57.cloned.1.call-start = ((), (), s32[]{:S(2)}) async-start(), calls=%async_computation.33 | async-start | bytes 860160 | tf_op jit(solution)/shard_map/while/body/eval_jaxpr/reduce_scatter | solution.py:104
  1421.2 103.0 %reduce-scatter.59.cloned.1.call-start = ((), (), s32[]{:S(2)}) async-start(), calls=%async_computation.36 | async-start | bytes 860160 | tf_op jit(solution)/shard_map/while/body/eval_jaxpr/reduce_scatter | solution.py:113
  1504.6 97.4 %reduce-scatter.65.cloned.1.call-start = ((), (), s32[]{:S(2)}) async-start(), calls=%async_computation.39 | async-start | bytes 1003520 | tf_op jit(solution)/shard_map/while/body/eval_jaxpr/reduce_scatter | solution.py:223
  1730.2 87.1 %reduce-scatter.43.cloned.1.call-start = ((), (), s32[]{:S(2)}) async-start(), calls=%async_computation.23 | async-start | bytes 2654208
  1742.2 99.6 %reduce-scatter.37.cloned.1.call-start = ((), (), s32[]{:S(2)}) async-start(), calls=%async_computation.20 | async-start | bytes 1769472 | tf_op jit(solution)/shard_map/reduce_scatter | solution.py:370
  1745.2 108.8 %reduce-scatter.51.cloned.1.call-start = ((), (), s32[]{:S(2)}) async-start(), calls=%async_computation.27 | async-start | bytes 49152
  1746.0 119.8 %reduce-scatter.45.cloned.1.call-start = ((), (), s32[]{:S(2)}) async-start(), calls=%async_computation.24 | async-start | bytes 24576
  1747.0 131.9 %reduce-scatter.41.cloned.1.call-start = ((), (), s32[]{:S(2)}) async-start(), calls=%async_computation.22 | async-start | bytes 294912
  1747.9 144.1 %reduce-scatter.39.cloned.1.call-start = ((), (), s32[]{:S(2)}) async-start(), calls=%async_computation.21 | async-start | bytes 294912
  1748.9 156.3 %reduce-scatter.49.cloned.1.call-start = ((), (), s32[]{:S(2)}) async-start(), calls=%async_computation.26 | async-start | bytes 294912
  1749.9 250.8 %all-reduce.6.cloned.1.call-start = ((), (), s32[]{:S(2)}) async-start(), calls=%async_computation.19 | async-start | bytes 1179648 | tf_op jit(solution)/shard_map/psum | solution.py:396
  1750.4 309.2 %all-reduce.8.cloned.1.call-start = ((), (), s32[]{:S(2)}) async-start(), calls=%async_computation.29 | async-start | bytes 4718592 | tf_op jit(solution)/shard_map/psum | solution.py:399
  (409 other events, 5553.1 us)
Sparse Core Ops, SparseCore 0:
  13.8 33.1 all-gather.18
  145.0 25.8 reduce-scatter.56
  172.4 23.7 all-gather.20
  197.7 22.7 all-gather.22
  304.0 23.0 reduce-scatter.64
  330.1 23.3 reduce-scatter.62
  442.0 30.2 all-gather.18
  570.0 25.8 reduce-scatter.56
  597.4 23.7 all-gather.20
  622.6 22.7 all-gather.22
  728.8 23.0 reduce-scatter.64
  755.0 23.3 reduce-scatter.62
  867.0 30.0 all-gather.18
  994.6 26.2 reduce-scatter.56
  1022.6 23.5 all-gather.20
  1154.0 23.0 reduce-scatter.64
  1180.2 23.3 reduce-scatter.62
  1291.9 29.3 all-gather.18
  1322.9 23.1 all-gather.16
  1419.8 25.5 reduce-scatter.56
  1447.0 23.9 all-gather.20
  1472.6 22.7 all-gather.22
  1578.9 23.0 reduce-scatter.64
  1605.0 23.3 reduce-scatter.62
  (24 shorter events, 533.6 us)
Sparse Core Ops, SparseCore 1:
  1723.2 20.5 reduce-scatter.34
  1746.6 15.2 reduce-scatter.46
  1764.5 21.6 reduce-scatter.52
  1789.1 28.1 reduce-scatter.42
  1820.1 21.6 reduce-scatter.36
  1844.1 9.7 reduce-scatter.50
  1856.0 9.7 reduce-scatter.44
  1868.0 10.8 reduce-scatter.40
  1881.1 10.8 reduce-scatter.38
  1894.3 10.8 reduce-scatter.48
  1908.9 91.8 all-reduce.5
  2004.6 54.9 all-reduce.7
where the time goes:
time: 2100 us; the launch traced here: 2070 us
  waiting for transfers between devices  864 us (41%)
  blocking collectives  662 us (32%)
  matrix products  207 us (10%)
  local copies, waits for them, and re-layouts  193 us (9%)
  other arithmetic  115 us (5%)
    all_gather x12, blocking collectives, gather_grad_rows(): lax.all_gather(rows_low, 'tensor', axis=0, tiled=True)  226 us
    all_gather x12, blocking collectives, gather_rows(): lax.all_gather(rows_low, 'tensor', axis=0, tiled=True)  203 us
    reduce_scatter x12, waiting for transfers between devices, sum_input_grad(): lax.psum_scatter(term(jnp.int32(0), count * lax.axis_size('tensor')).asty...  192 us
    reduce_scatter x12, waiting for transfers between devices, sum_branch(): lax.psum_scatter(term(jnp.int32(0), count * lax.axis_size('tensor')).asty...  187 us
    unnamed x20, waiting for transfers between devices  115 us
    reduce_scatter x4, waiting for transfers between devices, layer_pass(): lax.psum_scatter(value_grad_b.reshape(frames, all_places, width).astype(j...  102 us
    all_gather x4, waiting for transfers between devices, micro(): lax.all_gather(shards[9], 'shard', axis=1, tiled=True)  79.8 us
    psum x1, waiting for transfers between devices, body(): lax.psum(fc_grad.astype(jnp.bfloat16), ('context', 'tensor'))  57.7 us
  transfers between devices with their start and end apart: 60, of which 47 were waited for; matrix products, arithmetic and copies ran while one was open for 13% of the time, Pallas kernels for 0%

commit v1 on v0

v1 whole, which is shorter than its diff:
```python
import jax
import jax.numpy as jnp
from jax import lax
from jax.sharding import PartitionSpec as P

HEAD_DIM = 64
EPS = 1e-06
SQRT_HALF = 0.7071067811865476
INV_ROOT_TAU = 0.3989422804014327
LOW = jnp.bfloat16
F32 = jnp.float32


def dot(form, first, second):
    return jnp.einsum(form, first, second, preferred_element_type=F32)


def hop(values, axis, step):
    count = lax.axis_size(axis)
    return lax.ppermute(values, axis, [(i, i ^ step) for i in range(count)])


def pick(values, index, axis=0):
    return lax.dynamic_index_in_dim(values, index, axis, keepdims=False)


def ordered(parts, me, axis=0):
    shape = list(parts[0].shape)
    shape.insert(axis, len(parts))
    out = jnp.zeros(shape, parts[0].dtype)
    for j, part in enumerate(parts):
        out = lax.dynamic_update_index_in_dim(out, part, me ^ j, axis)
    return out


def swap_halves(values):
    half = values.shape[-1] // 2
    return jnp.concatenate([values[..., half:], values[..., :half]], -1)


class Place:
    def __init__(self):
        self.shard = lax.axis_index("shard")
        self.context = lax.axis_index("context")
        self.tensor = lax.axis_index("tensor")
        self.paired = lax.axis_size("shard") == 2

    def relative(self, values):
        if not self.paired:
            return values
        return jnp.where(self.shard == 0, values, swap_halves(values))

    def beside(self, values):
        return swap_halves(hop(values, "shard", 1))


def gather_columns(place, part):
    if place.paired:
        return jnp.concatenate([part, hop(part, "shard", 1)], -1)
    return lax.all_gather(part, "shard", axis=part.ndim - 1, tiled=True)


def scatter_columns(place, total):
    if place.paired:
        half = total.shape[-1] // 2
        mine = total[..., :half].astype(F32) + hop(total[..., half:], "shard", 1).astype(F32)
        return mine.astype(LOW)
    return lax.psum_scatter(total, "shard", scatter_dimension=total.ndim - 1, tiled=True)


def gather_blocks(place, block, short):
    def spread(mine):
        ranks = lax.axis_size("tensor")
        blocks = [mine] + [hop(mine, "tensor", k) for k in range(1, ranks)]
        return jnp.stack([gather_columns(place, item) for item in blocks])

    first = spread(pick(block, place.context))
    if short:
        second = spread(pick(block, place.context ^ 2))
    else:
        second = hop(first, "context", 2)
    return [first, hop(first, "context", 1), second, hop(second, "context", 1)]


def reduce_blocks(place, pieces, short):
    def add(*terms):
        total = terms[0].astype(F32)
        for term in terms[1:]:
            total = total + term.astype(F32)
        return total.astype(LOW)

    def collapse(total):
        mine = scatter_columns(place, total)
        return add(*[mine[0]] + [hop(mine[k], "tensor", k) for k in range(1, mine.shape[0])])

    first = add(pieces[0], hop(pieces[1], "context", 1))
    second = add(pieces[2], hop(pieces[3], "context", 1))
    if short:
        first, second = collapse(first), collapse(second)
        first, second = add(first, hop(second, "context", 2)), add(second, hop(first, "context", 2))
    else:
        first = collapse(add(first, hop(second, "context", 2)))
        second = hop(first, "context", 2)
    parts = [first, hop(first, "context", 1), second, hop(second, "context", 1)]
    return ordered(parts, place.context).astype(F32)


def unit_of(values):
    centred = values - jnp.mean(values, -1, keepdims=True)
    inverse = lax.rsqrt(jnp.mean(centred * centred, -1, keepdims=True) + EPS)
    return (centred * inverse, inverse)


def norm_back(grad, unit, inverse, gain):
    scaled = grad * gain
    inner = (
        scaled
        - jnp.mean(scaled, -1, keepdims=True)
        - unit * jnp.mean(scaled * unit, -1, keepdims=True)
    )
    return (inverse * inner, jnp.sum(grad * unit, 0), jnp.sum(grad, 0))


def gelu_both(values):
    half = 0.5 * (1.0 + lax.erf(values * SQRT_HALF))
    return (values * half, half + values * jnp.exp(-0.5 * values * values) * INV_ROOT_TAU)


def attend(query, key, value, allowed):
    scores = dot("bqd,bkd->bqk", query, key) * HEAD_DIM ** (-0.5)
    if allowed is not None:
        scores = jnp.where(allowed, scores, -jnp.inf)
    weights = jnp.exp(scores - jnp.max(scores, -1, keepdims=True))
    probs = weights / jnp.sum(weights, -1, keepdims=True)
    mixed = dot("bqk,bkd->bqd", probs.astype(LOW), value)
    return (mixed.astype(LOW), probs)


def attend_back(query, key, value, probs, grad):
    value_grad = dot("bqk,bqd->bkd", probs.astype(LOW), grad)
    prob_grad = dot("bqd,bkd->bqk", grad, value)
    inner = jnp.sum(probs * prob_grad, -1, keepdims=True)
    score_grad = (probs * (prob_grad - inner)).astype(LOW)
    scale = HEAD_DIM ** (-0.5)
    query_grad = dot("bqk,bkd->bqd", score_grad, key) * scale
    key_grad = dot("bqk,bqd->bkd", score_grad, query) * scale
    return (query_grad.astype(LOW), key_grad.astype(LOW), value_grad.astype(LOW))


class Tokens:
    def __init__(self, place, clips, live):
        self.place = place
        self.batches, self.frames, self.places = clips.shape[:3]
        self.ranks = lax.axis_size("tensor")
        self.whole = 1 if place.paired else self.batches
        self.split = self.batches - self.whole
        self.live = live
        self.room_whole = -(-self.whole * self.places // self.ranks)
        self.room_split = -(-self.split * self.places // (2 * self.ranks))
        self.room = self.room_whole + self.room_split
        if self.split:
            self.mine = live[self.whole :] > 0
            flat = jnp.repeat(self.mine, self.places)
            flat = jnp.pad(flat, (0, 2 * self.ranks * self.room_split - flat.shape[0]))
            self.mine_flat = pick(flat.reshape(2, -1), place.shard)

    def frame_rows(self, clips):
        place = self.place
        width = clips.shape[-1]
        rows = clips[: self.whole].reshape(-1, self.places, width)
        if self.split:
            later = clips[self.whole :]
            other = hop(pick(later, 1 - place.shard, 1), "shard", 1)
            chosen = jnp.where(self.mine[:, None, None], pick(later, place.shard, 1), other)
            rows = jnp.concatenate([rows, chosen])
        return place.relative(rows)

    def natural_rows(self, rows):
        place = self.place
        rows = place.relative(rows)
        first = self.whole * self.frames
        width = rows.shape[-1]
        out = rows[:first].reshape(self.whole, self.frames, self.places, width)
        if self.split:
            mine = rows[first:]
            other = hop(mine, "shard", 1)
            zero = jnp.zeros((), rows.dtype)
            pair = jnp.where(
                place.shard == 0, jnp.stack([mine, other], 1), jnp.stack([other, mine], 1)
            )
            out = jnp.concatenate([out, jnp.where(self.mine[:, None, None, None], pair, zero)])
        return out

    def scatter_places(self, whole, split):
        width = whole.shape[-1]
        frames, ranks = self.frames, self.ranks
        whole = jnp.pad(whole, ((0, 0), (0, ranks * self.room_whole - whole.shape[1]), (0, 0)))
        rows = whole.reshape(frames, ranks, self.room_whole, width)
        if self.split:
            split = split.reshape(frames, ranks, self.room_split, width)
            rows = jnp.concatenate([rows, split], 2)
        me = self.place.tensor
        return jnp.stack(
            [pick(rows, me, 1)]
            + [hop(pick(rows, me ^ k, 1), "tensor", k) for k in range(1, ranks)]
        )

    def gather_places(self, rows):
        width = rows.shape[-1]
        parts = [rows[0]] + [hop(rows[k], "tensor", k) for k in range(1, self.ranks)]
        rows = ordered(parts, self.place.tensor, 1)
        whole = rows[:, :, : self.room_whole].reshape(self.frames, -1, width)
        whole = whole[:, : self.whole * self.places]
        split = rows[:, :, self.room_whole :].reshape(self.frames, -1, width)
        return (whole, split)

    def natural_to_places(self, clips):
        width = clips.shape[-1]
        place = self.place

        def flat(part, room):
            part = jnp.swapaxes(part, 0, 1).reshape(self.frames, -1, width)
            return jnp.pad(part, ((0, 0), (0, room - part.shape[1]), (0, 0)))

        whole = flat(clips[: self.whole], self.whole * self.places)
        split = None
        if self.split:
            later = flat(clips[self.whole :], 2 * self.ranks * self.room_split)
            later = later.reshape(self.frames, 2, -1, width)
            other = hop(pick(later, 1 - place.shard, 1), "shard", 1)
            split = jnp.where(self.mine_flat[:, None], pick(later, place.shard, 1), other)
        return place.relative(self.scatter_places(whole, split))

    def frames_to_places(self, rows):
        place = self.place
        width = rows.shape[-1]
        first = self.whole * self.frames
        whole = rows[:first].reshape(self.whole, self.frames, self.places, width)
        whole = jnp.swapaxes(whole, 0, 1).reshape(self.frames, -1, width)
        split = None
        if self.split:
            flat = rows[first:].reshape(-1, width)
            flat = jnp.pad(flat, ((0, 2 * self.ranks * self.room_split - flat.shape[0]), (0, 0)))
            flat = flat.reshape(2, -1, width)
            mine = pick(flat, place.shard)
            other = place.beside(pick(flat, 1 - place.shard))
            split = jnp.where(
                place.shard == 0, jnp.stack([mine, other]), jnp.stack([other, mine])
            )
        return self.scatter_places(whole, split)

    def places_to_frames(self, rows):
        place = self.place
        width = rows.shape[-1]
        whole, split = self.gather_places(rows)
        whole = jnp.swapaxes(whole.reshape(self.frames, self.whole, self.places, width), 0, 1)
        out = whole.reshape(-1, self.places, width)
        if self.split:
            mine = pick(split, place.shard)
            other = place.beside(pick(split, 1 - place.shard))
            flat = jnp.where(
                place.shard == 0, jnp.concatenate([mine, other]), jnp.concatenate([other, mine])
            )
            flat = flat[: self.split * self.places].reshape(self.split, self.places, width)
            out = jnp.concatenate([out, flat])
        return out


def body(
    clip_input,
    clip_slot,
    norm_gain,
    norm_shift,
    attention_in,
    attention_bias,
    attention_out,
    branch_bias,
    temporal_fc,
    hidden_in,
    hidden_bias,
    hidden_out,
    output_grad,
):
    place = Place()
    shards, quarters, ranks = (lax.axis_size(name) for name in ("shard", "context", "tensor"))
    clips, cotangents, live = clip_input[:, 0], output_grad[:, 0], clip_slot[:, 0]
    tokens = Tokens(place, clips, live)
    columns = attention_in.shape[1]
    width = columns * shards
    group = attention_in.shape[3]
    heads = group // HEAD_DIM
    hidden = hidden_in.shape[1]
    context = place.context

    def in_block(weight):
        block = jnp.transpose(weight, (1, 2, 0)).reshape(3, quarters, group // quarters, columns)
        return jnp.swapaxes(block, 0, 1)

    def quartered(block):
        return block.reshape(quarters, -1, block.shape[-1])

    vectors = jnp.concatenate(
        [norm_gain, norm_shift, branch_bias, attention_bias.reshape(-1, columns)]
        + [hidden_bias.reshape(-1, columns)]
    )
    vectors = lax.all_gather(lax.all_gather(vectors, "tensor"), "shard")
    rows = vectors[:, place.tensor].astype(F32)
    along = jnp.swapaxes(rows[:, :10], 0, 1).reshape(10, width)
    along = place.relative(along)
    gains, shifts, branch = along[:3], along[3:6], along[6:10]
    hops = place.tensor ^ jnp.arange(ranks)
    own = jnp.take(vectors, hops, axis=1).astype(F32)
    last = 10 + attention_bias.size // columns
    pairs = own[:, :, 10:last].reshape((shards, ranks) + attention_bias.shape)
    pairs = jnp.transpose(pairs, (2, 3, 1, 4, 0, 5)).reshape(2, 2, ranks, group)
    up_shift = own[:, :, last:].reshape((shards, ranks) + hidden_bias.shape)
    up_shift = jnp.transpose(up_shift, (1, 2, 0, 3)).reshape(ranks, quarters, -1)

    def assemble_in(pieces):
        whole = ordered(pieces, context, 2)
        return whole.reshape(ranks, 3 * group, width)

    def assemble_out(pieces):
        return ordered(pieces, context, 1).reshape(ranks, group, width)

    in_a = assemble_in(gather_blocks(place, in_block(attention_in[0]), False))
    out_a = assemble_out(gather_blocks(place, quartered(attention_out[0]), False))
    fc_rows = gather_columns(place, temporal_fc.T).T
    fc = place.relative(fc_rows)
    in_b = assemble_in(gather_blocks(place, in_block(attention_in[1]), False))
    out_b = assemble_out(gather_blocks(place, quartered(attention_out[1]), False))
    up = gather_blocks(place, quartered(hidden_in.T), False)
    down = gather_blocks(place, quartered(hidden_out), True)
    up = [item.reshape(-1, width) for item in up]
    down = [item.reshape(-1, width) for item in down]
    up_bias = [pick(up_shift, context ^ j, 1).reshape(-1) for j in range(quarters)]

    def project(normed, weight, pair):
        shift = jnp.stack([pair[0], jnp.zeros_like(pair[0]), pair[1]], 1).reshape(ranks, 1, -1)
        return (dot("td,knd->ktn", normed, weight) + shift).astype(LOW)

    start_p = tokens.natural_to_places(clips).astype(F32).reshape(-1, width)
    start = tokens.frame_rows(clips)
    units, places = start.shape[:2]
    start = start.astype(F32).reshape(-1, width)
    grad = tokens.frame_rows(cotangents * live[:, None, None, None].astype(LOW))
    grad = grad.reshape(-1, width)
    unit_a, inverse_a = unit_of(start_p)
    normed_a = (unit_a * gains[0] + shifts[0]).astype(LOW)
    count_p = start_p.shape[0]
    qkv_a = project(normed_a, in_a, pairs[0]).reshape(ranks, count_p, 3, heads, HEAD_DIM)
    qkv_a = jnp.transpose(qkv_a, (2, 0, 3, 1, 4)).reshape(3, ranks * heads, count_p, HEAD_DIM)
    spot = jnp.arange(count_p) % tokens.room
    allowed = spot[:, None] == spot[None]
    mixed_a, probs_a = attend(qkv_a[0], qkv_a[1], qkv_a[2], allowed)

    def side_by_side(values):
        values = values.reshape(ranks, heads, values.shape[1], HEAD_DIM)
        return jnp.swapaxes(values, 1, 2).reshape(ranks, values.shape[2], group)

    flat_a = side_by_side(mixed_a)
    temporal_p = (dot("ktn,knd->td", flat_a, out_a) + branch[0]).astype(LOW)
    temporal = tokens.places_to_frames(temporal_p.reshape(ranks, tokens.frames, -1, width))
    temporal = temporal.reshape(-1, width)
    after_a = start + dot("tk,kd->td", temporal, fc) + branch[1]

    unit_b, inverse_b = unit_of(after_a)
    normed_b = (unit_b * gains[1] + shifts[1]).astype(LOW)
    qkv_b = project(normed_b, in_b, pairs[1])

    def to_groups(values):
        return [pick(values, context)] + [
            hop(pick(values, context ^ j), "context", j) for j in range(1, quarters)
        ]

    def from_groups(parts):
        parts = [parts[0]] + [hop(parts[j], "context", j) for j in range(1, quarters)]
        return ordered(parts, context)

    def frame_heads(parts, kinds):
        values = jnp.stack(parts).reshape(quarters, units, places, kinds, heads, HEAD_DIM)
        values = jnp.transpose(values, (3, 1, 4, 0, 2, 5))
        return values.reshape(kinds, units * heads, quarters * places, HEAD_DIM)

    def frame_rows(values, kinds):
        values = values.reshape(kinds, units, heads, quarters, places, HEAD_DIM)
        values = jnp.transpose(values, (3, 1, 4, 0, 2, 5))
        return values.reshape(quarters, units * places, kinds * group)

    q_b, k_b, v_b = frame_heads(to_groups(qkv_b), 3)
    mixed_b, probs_b = attend(q_b, k_b, v_b, None)
    flat_b = from_groups(frame_rows(mixed_b[None], 1))
    after_b = after_a + dot("ktn,knd->td", flat_b, out_b) + branch[2]

    unit_c, inverse_c = unit_of(after_b)
    normed_c = (unit_c * gains[2] + shifts[2]).astype(LOW)
    result = after_b + branch[3]
    back = jnp.zeros_like(result)
    down_grad, up_grad, up_bias_grad = [], [], []
    for j in range(quarters):
        hidden_c = dot("td,kd->tk", normed_c, up[j]) + up_bias[j]
        active, slope = gelu_both(hidden_c)
        active = active.astype(LOW)
        result = result + dot("tk,kd->td", active, down[j])
        down_grad.append(dot("tk,td->kd", active, grad).astype(LOW).reshape(ranks, -1, width))
        hidden_grad = (dot("td,kd->tk", grad, down[j]) * slope).astype(LOW)
        up_grad.append(
            dot("tk,td->kd", hidden_grad, normed_c).astype(LOW).reshape(ranks, -1, width)
        )
        up_bias_grad.append(jnp.sum(hidden_grad.astype(F32), 0))
        back = back + dot("tk,kd->td", hidden_grad, up[j])
    layer_rows = result.astype(LOW).reshape(units, places, width)
    layer_out = tokens.natural_rows(layer_rows)
    layer_out = layer_out * live[:, None, None, None].astype(LOW)
    down_total = reduce_blocks(place, down_grad, True)
    up_total = reduce_blocks(place, up_grad, False)

    branch_3 = jnp.sum(grad.astype(F32), 0)
    back, gain_c, shift_c = norm_back(back, unit_c, inverse_c, gains[2])
    grad = grad.astype(F32) + back

    low_b = grad.astype(LOW)
    branch_2 = jnp.sum(low_b.astype(F32), 0)
    mixed_grad_b = dot("td,knd->ktn", low_b, out_b).astype(LOW)
    out_grad_b = dot("ktn,td->knd", flat_b, low_b).astype(LOW)
    (mixed_grad_b,) = frame_heads(to_groups(mixed_grad_b), 1)
    qkv_grad_b = attend_back(q_b, k_b, v_b, probs_b, mixed_grad_b)
    qkv_grad_b = from_groups(frame_rows(jnp.stack(qkv_grad_b), 3))

    def split_quarters(values, axis):
        return [pick(values, context ^ j, axis) for j in range(quarters)]

    def reduce_out(total):
        parts = split_quarters(total.reshape(ranks, quarters, -1, width), 1)
        return reduce_blocks(place, parts, False).reshape(group, columns)

    def reduce_in(total):
        parts = split_quarters(total.reshape(ranks, 3, quarters, -1, width), 2)
        total = reduce_blocks(place, parts, False)
        return jnp.transpose(total, (3, 1, 0, 2)).reshape(columns, 3, group)

    in_grad_b = dot("ktn,td->knd", qkv_grad_b, normed_b).astype(LOW)
    pair_b = jnp.sum(qkv_grad_b.astype(F32), 1).reshape(ranks, 3, group)
    back, gain_b, shift_b = norm_back(
        dot("ktn,knd->td", qkv_grad_b, in_b), unit_b, inverse_b, gains[1]
    )
    grad = grad + back

    low_fc = grad.astype(LOW)
    branch_1 = jnp.sum(low_fc.astype(F32), 0)
    fc_grad = dot("tk,td->kd", temporal, low_fc)
    temporal_grad = dot("td,kd->tk", low_fc, fc).astype(LOW)
    branch_0 = jnp.sum(temporal_grad.astype(F32), 0)
    temporal_grad = tokens.frames_to_places(temporal_grad.reshape(units, places, width))
    temporal_grad = temporal_grad.reshape(-1, width)
    out_grad_a = dot("ktn,td->knd", flat_a, temporal_grad).astype(LOW)
    mixed_grad_a = dot("td,knd->ktn", temporal_grad, out_a).astype(LOW)
    mixed_grad_a = mixed_grad_a.reshape(ranks, count_p, heads, HEAD_DIM)
    mixed_grad_a = jnp.swapaxes(mixed_grad_a, 1, 2).reshape(-1, count_p, HEAD_DIM)
    qkv_grad_a = attend_back(qkv_a[0], qkv_a[1], qkv_a[2], probs_a, mixed_grad_a)
    qkv_grad_a = jnp.concatenate([side_by_side(item) for item in qkv_grad_a], -1)
    in_grad_a = dot("ktn,td->knd", qkv_grad_a, normed_a).astype(LOW)
    pair_a = jnp.sum(qkv_grad_a.astype(F32), 1).reshape(ranks, 3, group)
    back, gain_a, shift_a = norm_back(
        dot("ktn,knd->td", qkv_grad_a, in_a), unit_a, inverse_a, gains[0]
    )
    back = tokens.places_to_frames(
        back.astype(LOW).reshape(ranks, tokens.frames, -1, width)
    ).reshape(-1, width)
    input_rows = (grad + back.astype(F32)).astype(LOW).reshape(units, places, width)
    input_grad = tokens.natural_rows(input_rows)

    in_total = jnp.stack([reduce_in(in_grad_a), reduce_in(in_grad_b)])
    out_total = jnp.stack([reduce_out(out_grad_a), reduce_out(out_grad_b)])
    fc_grad = place.relative(fc_grad).astype(LOW)
    fc_total = lax.psum(scatter_columns(place, fc_grad.T).T, ("context", "tensor")).astype(F32)

    along = jnp.stack(
        [gain_a, gain_b, gain_c, shift_a, shift_b, shift_c, branch_0, branch_1, branch_2, branch_3]
    )
    along = place.relative(along).reshape(-1)
    inner = jnp.stack([pair_a, pair_b])[:, :, ::2]
    inner = ordered([inner[:, k] for k in range(ranks)], place.tensor).reshape(-1)
    outer = ordered([item.reshape(ranks, -1) for item in up_bias_grad], context, 1)
    outer = ordered([outer[k] for k in range(ranks)], place.tensor).reshape(-1)
    sums = lax.psum(jnp.concatenate([along, inner, outer]), ("shard", "context", "tensor"))
    along, inner, outer = jnp.split(sums, [along.size, along.size + inner.size])
    along = lax.dynamic_slice_in_dim(along.reshape(10, width), place.shard * columns, columns, 1)
    inner = pick(inner.reshape(ranks, 2, 2, heads, HEAD_DIM), place.tensor)
    piece = HEAD_DIM // shards
    inner = lax.dynamic_slice_in_dim(inner, place.shard * piece, piece, 3)
    outer = pick(outer.reshape(ranks, -1, shards, hidden_bias.shape[1]), place.tensor)
    outer = pick(outer, place.shard, 1)
    return (
        layer_out[:, None],
        input_grad[:, None],
        along[:3],
        along[3:6],
        in_total,
        inner,
        out_total,
        along[6:],
        fc_total,
        up_total.reshape(hidden, columns).T,
        outer,
        down_total.reshape(hidden, columns),
    )


def solution(mesh):
    rows = P(None, "shard", "tensor", "context", None)
    weights = (
        P(None, "shard"),
        P(None, "shard"),
        P(None, "shard", None, "tensor"),
        P(None, None, "tensor", "shard"),
        P(None, "tensor", "shard"),
        P(None, "shard"),
        P("shard", None),
        P("shard", "tensor"),
        P("tensor", "shard"),
        P("tensor", "shard"),
    )
    return jax.shard_map(
        body,
        mesh=mesh,
        in_specs=(rows, P(None, "shard")) + weights + (rows,),
        out_specs=(rows, rows) + weights,
        check_vma=False,
    )
```

time: 2100 us -> 965 us (0.46)
  blocking collectives: 662 us -> 57 us
  waiting for transfers between devices: 864 us -> 282 us
  starting transfers between devices: 2.56 us -> 158 us
  matrix products: 207 us -> 99.2 us
  local copies, waits for them, and re-layouts: 193 us -> 241 us
    all_gather x56 -> x2, blocking collectives: 620 us -> 18 us  [body(): vectors = lax.all_gather(lax.all_gather(vectors, 'tensor'), 'shard')]
    reduce_scatter x34 -> x0, waiting for transfers between devices: 529 us -> none  [the longest x12 192 us: sum_input_grad(): lax.psum_scatter(term(jnp.int32(0), count * lax.axis_size('tensor')).asty...]
    ppermute x0 -> x164, waiting for transfers between devices: none -> 236 us  [hop(): return lax.ppermute(values, axis, [(i, i ^ step) for i in range(count)])]
    ppermute x0 -> x164, starting transfers between devices: none -> 158 us  [hop(): return lax.ppermute(values, axis, [(i, i ^ step) for i in range(count)])]
    unnamed x20 -> x1, waiting for transfers between devices: 115 us -> 0.02 us
    dot_general x132 -> x49, matrix products: 207 us -> 91.8 us  [dot(): return jnp.einsum(form, first, second, preferred_element_type=F32)]
    all_gather x16 -> x0, waiting for transfers between devices: 94.5 us -> none  [the longest x4 79.8 us: micro(): lax.all_gather(shards[9], 'shard', axis=1, tiled=True)]
    psum x2 -> x1, waiting for transfers between devices: 114 us -> 46 us  [body(): lax.psum(scatter_columns(place, fc_grad.T).T, ('context', 'tensor'))]
  transfers between devices with their start and end apart: 60 -> 165, of which waited for: 47 -> 56; matrix products, arithmetic and copies ran while one was open for 13% -> 42% of each run, Pallas kernels for 0% -> 0%
where the time goes in v1:
time: 965 us; the launch traced here: 957 us
  waiting for transfers between devices  282 us (29%)
  local copies, waits for them, and re-layouts  241 us (25%)
  starting transfers between devices  158 us (16%)
  other arithmetic  102 us (11%)
  matrix products  99.2 us (10%)
  blocking collectives  57 us (6%)
  between operations  17.7 us (2%)
    ppermute x164, waiting for transfers between devices, hop(): return lax.ppermute(values, axis, [(i, i ^ step) for i in range(count)])  236 us
    ppermute x164, starting transfers between devices, hop(): return lax.ppermute(values, axis, [(i, i ^ step) for i in range(count)])  158 us
    dot_general x49, matrix products, dot(): return jnp.einsum(form, first, second, preferred_element_type=F32)  91.8 us
    psum x1, waiting for transfers between devices, body(): lax.psum(scatter_columns(place, fc_grad.T).T, ('context', 'tensor'))  46 us
    psum x1, blocking collectives, body(): lax.psum(jnp.concatenate([along, inner, outer]), ('shard', 'context', 'te...  38.9 us
    dynamic_update_slice x57, local copies, waits for them, and re-layouts, ordered(): out = lax.dynamic_update_index_in_dim(out, part, me ^ j, axis)  24.8 us
    slice x8, local copies, waits for them, and re-layouts, from_groups(): parts[j]  24.1 us
    another operation x35, other arithmetic, spread(): return jnp.stack([gather_columns(place, item) for item in blocks])  19.5 us
  transfers between devices with their start and end apart: 165, of which 56 were waited for; matrix products, arithmetic and copies ran while one was open for 42% of the time, Pallas kernels for 0%

profile of v1, /device:TPU:0, one launch (start us, length us, event | category | flops | bytes accessed | tf_op | source)
XLA Modules:
  0.0 957.2 jit_solution(6862684863875663504)
XLA Ops:
  8.6 5.1 collective-permute-start.6
  22.2 13.1 %all-gather.2 = bf16[4,12,384]{2,1,0:T(8,128)(2,1)S(1)} all-gather(bf16[1,12,384]{2,1,0:T(8,128)(2,1)S(1)} %bitcast.884), channel_id=2, replica_groups=mesh['shard'=2,'context'=4,'tensor'=4] {'tensor'}, dimensions={0}, use_global_device_ids=true | all-gather | bytes 46080 | tf_op jit(solution)/shard_map/all_gather | solution.py:306
  35.2 5.0 all-gather.1
  201.3 9.3 collective-permute-done.79
  238.6 35.4 %collective-permute-done.54 = bf16[4,48,768]{2,1,0:T(8,128)(2,1)} collective-permute-done((bf16[4,48,768]{2,1,0:T(8,128)(2,1)}, bf16[4,48,768]{2,1,0:T(8,128)(2,1)}, u32[]{:S(2)}, u32[]{:S(2)}) %collective-permute-start.54) | collective-permute-done | bytes 294944 | tf_op jit(solution)/shard_map/ppermute | solution.py:20
  281.7 4.6 fusion.171
  296.8 6.2 collective-permute-done.27
  330.2 5.4 collective-permute-done.41
  348.5 4.2 copy.586
  475.8 6.1 fusion.149
  485.7 4.4 copy.624
  492.3 4.4 copy.626
  575.8 5.4 multiply_reduce_fusion.3
  590.1 38.9 %psum.14 = f32[13824]{0:T(1024)} all-reduce(f32[13824]{0:T(1024)} %pad_maximum_fusion.23), channel_id=1, replica_groups=mesh['shard'=2,'context'=4,'tensor'=4] {'shard','context','tensor'}, use_global_device_ids=true, to_apply=%region_34.35 | all-reduce | flops 13824 | bytes 110592 | tf_op jit(solution)/shard_map/psum | solution.py:486
  677.1 10.5 %collective-permute-done.97 = bf16[76,768]{1,0:T(8,128)(2,1)S(1)} collective-permute-done((bf16[76,768]{1,0:T(8,128)(2,1)S(1)}, bf16[76,768]{1,0:T(8,128)(2,1)S(1)}, u32[]{:S(2)}, u32[]{:S(2)}) %collective-permute-start.97) | collective-permute-done | bytes 116768 | tf_op jit(solution)/shard_map/ppermute | solution.py:20
  712.7 5.8 collective-permute-done.98
  728.5 6.1 collective-permute-done.121
  755.8 46.0 %all-reduce.7.cloned.1.call-done = bf16[384,768]{0,1:T(8,128)(2,1)} async-done(((bf16[384,768]{0,1:T(8,128)(2,1)}), bf16[384,768]{0,1:T(8,128)(2,1)}) %all-reduce.7.cloned.1.call-update) | async-done | bytes 589840 | tf_op jit(solution)/shard_map/psum | solution.py:476
  819.4 9.3 collective-permute-done.158
  842.4 20.7 %collective-permute-done.162 = bf16[192,384]{1,0:T(8,128)(2,1)S(1)} collective-permute-done((bf16[192,384]{1,0:T(8,128)(2,1)S(1)}, bf16[192,384]{1,0:T(8,128)(2,1)S(1)}, u32[]{:S(2)}, u32[]{:S(2)}) %collective-permute-start.162) | collective-permute-done | bytes 147488 | tf_op jit(solution)/shard_map/ppermute | solution.py:20
  869.2 16.4 %collective-permute-done.101 = bf16[4,3,48,768]{3,2,1,0:T(8,128)(2,1)S(1)} collective-permute-done((bf16[4,3,48,768]{3,2,1,0:T(8,128)(2,1)S(1)}, bf16[4,3,48,768]{3,2,1,0:T(8,128)(2,1)S(1)}, u32[]{:S(2)}, u32[]{:S(2)}) %collective-permute-start.101) | collective-permute-done | bytes 884768 | tf_op jit(solution)/shard_map/ppermute | solution.py:20
  892.2 16.9 %collective-permute-done.142 = bf16[4,192,768]{2,1,0:T(8,128)(2,1)S(1)} collective-permute-done((bf16[4,192,768]{2,1,0:T(8,128)(2,1)S(1)}, bf16[4,192,768]{2,1,0:T(8,128)(2,1)S(1)}, u32[]{:S(2)}, u32[]{:S(2)}) %collective-permute-start.142) | collective-permute-done | bytes 1179680 | tf_op jit(solution)/shard_map/ppermute | solution.py:20
  930.5 4.2 collective-permute-done.146
  934.6 6.0 collective-permute-done.145
  (1146 shorter events, 650.0 us)
Async XLA Ops:
  7.2 794.6 %all-reduce.7.cloned.1.call-start = ((), (), s32[]{:S(2)}) async-start(), calls=%async_computation | async-start | bytes 1179648 | tf_op jit(solution)/shard_map/psum | solution.py:476
  8.6 96.2 %collective-permute-start.6 = (bf16[3,48,384]{2,1,0:T(8,128)(2,1)S(1)}, bf16[3,48,384]{2,1,0:T(8,128)(2,1)}, u32[]{:S(2)}, u32[]{:S(2)}) collective-permute-start(bf16[3,48,384]{2,1,0:T(8,128)(2,1)S(1)} %dynamic-slice_bitcast_fusion.18), channel_id=1, source_target_pairs={{0,3},{1,2},{2,1},{3,0},{4,7},{5,6},{6,5},{7,4},{8,11},{9,10},{10,... | collective-permute-start | bytes 331784 | tf_op jit(solution)/shard_map/ppermute | solution.py:20
  13.7 94.5 %collective-permute-start.4 = (bf16[3,48,384]{2,1,0:T(8,128)(2,1)S(1)}, bf16[3,48,384]{2,1,0:T(8,128)(2,1)}, u32[]{:S(2)}, u32[]{:S(2)}) collective-permute-start(bf16[3,48,384]{2,1,0:T(8,128)(2,1)S(1)} %dynamic-slice_bitcast_fusion.18), channel_id=1, source_target_pairs={{0,2},{1,3},{2,0},{3,1},{4,6},{5,7},{6,4},{7,5},{8,10},{9,11},{10,... | collective-permute-start | bytes 331784 | tf_op jit(solution)/shard_map/ppermute | solution.py:20
  13.7 99.6 %collective-permute-start.2 = (bf16[3,48,384]{2,1,0:T(8,128)(2,1)S(1)}, bf16[3,48,384]{2,1,0:T(8,128)(2,1)}, u32[]{:S(2)}, u32[]{:S(2)}) collective-permute-start(bf16[3,48,384]{2,1,0:T(8,128)(2,1)S(1)} %dynamic-slice_bitcast_fusion.18), channel_id=1, source_target_pairs={{0,1},{1,0},{2,3},{3,2},{4,5},{5,4},{6,7},{7,6},{8,9},{9,8},{10,11... | collective-permute-start | bytes 331784 | tf_op jit(solution)/shard_map/ppermute | solution.py:20
  113.3 62.7 %collective-permute-start.61 = (bf16[192,384]{1,0:T(8,128)(2,1)}, bf16[192,384]{1,0:T(8,128)(2,1)}, u32[]{:S(2)}, u32[]{:S(2)}) collective-permute-start(bf16[192,384]{1,0:T(8,128)(2,1)} %dynamic-slice_bitcast_fusion.15), channel_id=1, source_target_pairs={{0,3},{1,2},{2,1},{3,0},{4,7},{5,6},{6,5},{7,4},{8,11},{9,10},{10,... | collective-permute-start | bytes 442376 | tf_op jit(solution)/shard_map/ppermute | solution.py:20
  119.5 56.7 %collective-permute-start.59 = (bf16[192,384]{1,0:T(8,128)(2,1)}, bf16[192,384]{1,0:T(8,128)(2,1)}, u32[]{:S(2)}, u32[]{:S(2)}) collective-permute-start(bf16[192,384]{1,0:T(8,128)(2,1)} %dynamic-slice_bitcast_fusion.15), channel_id=1, source_target_pairs={{0,2},{1,3},{2,0},{3,1},{4,6},{5,7},{6,4},{7,5},{8,10},{9,11},{10,... | collective-permute-start | bytes 442376 | tf_op jit(solution)/shard_map/ppermute | solution.py:20
  127.2 54.1 %collective-permute-start.57 = (bf16[192,384]{1,0:T(8,128)(2,1)}, bf16[192,384]{1,0:T(8,128)(2,1)}, u32[]{:S(2)}, u32[]{:S(2)}) collective-permute-start(bf16[192,384]{1,0:T(8,128)(2,1)} %dynamic-slice_bitcast_fusion.15), channel_id=1, source_target_pairs={{0,1},{1,0},{2,3},{3,2},{4,5},{5,4},{6,7},{7,6},{8,9},{9,8},{10,11... | collective-permute-start | bytes 442376 | tf_op jit(solution)/shard_map/ppermute | solution.py:20
  221.5 52.5 %collective-permute-start.8 = (bf16[4,3,48,768]{3,2,1,0:T(8,128)(2,1)}, bf16[4,3,48,768]{3,2,1,0:T(8,128)(2,1)}, u32[]{:S(2)}, u32[]{:S(2)}) collective-permute-start(bf16[4,3,48,768]{3,2,1,0:T(8,128)(2,1)} %pad_maximum_fusion.6), channel_id=1, source_target_pairs={{0,4},{4,0},{8,12},{12,8},{1,5},{5,1},{9,13},{13,9},{2,6},{6,2},{1... | collective-permute-start | bytes 2654216 | tf_op jit(solution)/shard_map/ppermute | solution.py:20
  226.3 48.2 %collective-permute-start.9 = (bf16[4,3,48,768]{3,2,1,0:T(8,128)(2,1)}, bf16[4,3,48,768]{3,2,1,0:T(8,128)(2,1)S(1)}, u32[]{:S(2)}, u32[]{:S(2)}) collective-permute-start(bf16[4,3,48,768]{3,2,1,0:T(8,128)(2,1)} %pad_maximum_fusion.6), channel_id=1, source_target_pairs={{0,8},{4,12},{8,0},{12,4},{1,9},{5,13},{9,1},{13,5},{2,10},{6,14},... | collective-permute-start | bytes 2654216 | tf_op jit(solution)/shard_map/ppermute | solution.py:20
  273.9 124.9 %collective-permute-start.70 = (bf16[4,192,768]{2,1,0:T(8,128)(2,1)}, bf16[4,192,768]{2,1,0:T(8,128)(2,1)}, u32[]{:S(2)}, u32[]{:S(2)}) collective-permute-start(bf16[4,192,768]{2,1,0:T(8,128)(2,1)} %pad_maximum_fusion), channel_id=1, source_target_pairs={{0,4},{4,0},{8,12},{12,8},{1,5},{5,1},{9,13},{13,9},{2,6},{6,2},{1... | collective-permute-start | bytes 3538952 | tf_op jit(solution)/shard_map/ppermute | solution.py:20
  273.9 48.9 %collective-permute-start.55 = (bf16[4,48,768]{2,1,0:T(8,128)(2,1)}, bf16[4,48,768]{2,1,0:T(8,128)(2,1)}, u32[]{:S(2)}, u32[]{:S(2)}) collective-permute-start(bf16[4,48,768]{2,1,0:T(8,128)(2,1)} %collective-permute-done.54), channel_id=1, source_target_pairs={{0,4},{4,0},{8,12},{12,8},{1,5},{5,1},{9,13},{13,9},{2,6},{6,2},{1... | collective-permute-start | bytes 884744 | tf_op jit(solution)/shard_map/ppermute | solution.py:20
  322.9 59.6 %collective-permute-start.72 = (bf16[4,192,768]{2,1,0:T(8,128)(2,1)}, bf16[4,192,768]{2,1,0:T(8,128)(2,1)}, u32[]{:S(2)}, u32[]{:S(2)}) collective-permute-start(bf16[4,192,768]{2,1,0:T(8,128)(2,1)} %pad_maximum_fusion), channel_id=1, source_target_pairs={{0,8},{4,12},{8,0},{12,4},{1,9},{5,13},{9,1},{13,5},{2,10},{6,14},... | collective-permute-start | bytes 3538952 | tf_op jit(solution)/shard_map/ppermute | solution.py:20
  447.6 57.4 %collective-permute-start.82 = (bf16[3,49,768]{2,0,1:T(4,128)(2,1)}, bf16[3,49,768]{2,0,1:T(4,128)(2,1)}, u32[]{:S(2)}, u32[]{:S(2)}) collective-permute-start(bf16[3,49,768]{2,0,1:T(4,128)(2,1)} %get-tuple-element.170), channel_id=1, source_target_pairs={{0,16},{16,0},{1,17},{17,1},{2,18},{18,2},{3,19},{19,3},{4,20},{20... | collective-permute-start | bytes 677384 | tf_op jit(solution)/shard_map/ppermute | solution.py:20
  452.2 56.5 %collective-permute-start.130 = (bf16[4,48,768]{2,1,0:T(8,128)(2,1)}, bf16[4,48,768]{2,1,0:T(8,128)(2,1)}, u32[]{:S(2)}, u32[]{:S(2)}) collective-permute-start(bf16[4,48,768]{2,1,0:T(8,128)(2,1)} %get-tuple-element.151), channel_id=1, source_target_pairs={{0,4},{4,0},{8,12},{12,8},{1,5},{5,1},{9,13},{13,9},{2,6},{6,2},{1... | collective-permute-start | bytes 884744 | tf_op jit(solution)/shard_map/ppermute | solution.py:20
  452.2 93.2 %collective-permute-start.129 = (bf16[4,48,768]{2,1,0:T(8,128)(2,1)}, bf16[4,48,768]{2,1,0:T(8,128)(2,1)}, u32[]{:S(2)}, u32[]{:S(2)}) collective-permute-start(bf16[4,48,768]{2,1,0:T(8,128)(2,1)} %get-tuple-element.150), channel_id=1, source_target_pairs={{0,4},{4,0},{8,12},{12,8},{1,5},{5,1},{9,13},{13,9},{2,6},{6,2},{1... | collective-permute-start | bytes 884744 | tf_op jit(solution)/shard_map/ppermute | solution.py:20
  508.6 216.4 %collective-permute-start.141 = (bf16[4,192,768]{2,1,0:T(8,128)(2,1)}, bf16[4,192,768]{2,1,0:T(8,128)(2,1)}, u32[]{:S(2)}, u32[]{:S(2)}) collective-permute-start(bf16[4,192,768]{2,1,0:T(8,128)(2,1)} %bitcast.294), channel_id=1, source_target_pairs={{0,4},{4,0},{8,12},{12,8},{1,5},{5,1},{9,13},{13,9},{2,6},{6,2},{1... | collective-permute-start | bytes 3538952 | tf_op jit(solution)/shard_map/ppermute | solution.py:20
  510.7 226.6 %collective-permute-start.155 = (bf16[4,192,768]{2,1,0:T(8,128)(2,1)}, bf16[4,192,768]{2,1,0:T(8,128)(2,1)}, u32[]{:S(2)}, u32[]{:S(2)}) collective-permute-start(bf16[4,192,768]{2,1,0:T(8,128)(2,1)} %bitcast.312), channel_id=1, source_target_pairs={{0,4},{4,0},{8,12},{12,8},{1,5},{5,1},{9,13},{13,9},{2,6},{6,2},{1... | collective-permute-start | bytes 3538952 | tf_op jit(solution)/shard_map/ppermute | solution.py:20
  552.4 113.5 %collective-permute-start.132 = (bf16[4,48,384]{2,1,0:T(8,128)(2,1)}, bf16[4,48,384]{2,1,0:T(8,128)(2,1)}, u32[]{:S(2)}, u32[]{:S(2)}) collective-permute-start(bf16[4,48,384]{2,1,0:T(8,128)(2,1)} %slice.773), channel_id=1, source_target_pairs={{0,16},{16,0},{1,17},{17,1},{2,18},{18,2},{3,19},{19,3},{4,20},{20... | collective-permute-start | bytes 442376 | tf_op jit(solution)/shard_map/ppermute | solution.py:20
  728.3 110.8 %collective-permute-start.100 = (bf16[4,3,48,768]{3,2,1,0:T(8,128)(2,1)}, bf16[4,3,48,768]{3,2,1,0:T(8,128)(2,1)}, u32[]{:S(2)}, u32[]{:S(2)}) collective-permute-start(bf16[4,3,48,768]{3,2,1,0:T(8,128)(2,1)} %get-tuple-element.136), channel_id=1, source_target_pairs={{0,4},{4,0},{8,12},{12,8},{1,5},{5,1},{9,13},{13,9},{2,6},{6,2},{1... | collective-permute-start | bytes 2654216 | tf_op jit(solution)/shard_map/ppermute | solution.py:20
  749.5 57.4 %collective-permute-start.156 = (bf16[4,192,384]{2,1,0:T(8,128)(2,1)}, bf16[4,192,384]{2,1,0:T(8,128)(2,1)}, u32[]{:S(2)}, u32[]{:S(2)}) collective-permute-start(bf16[4,192,384]{2,1,0:T(8,128)(2,1)} %slice.795), channel_id=1, source_target_pairs={{0,16},{16,0},{1,17},{17,1},{2,18},{18,2},{3,19},{19,3},{4,20},{20... | collective-permute-start | bytes 1769480 | tf_op jit(solution)/shard_map/ppermute | solution.py:20
  751.0 60.4 %collective-permute-start.151 = (bf16[4,192,384]{2,1,0:T(8,128)(2,1)}, bf16[4,192,384]{2,1,0:T(8,128)(2,1)}, u32[]{:S(2)}, u32[]{:S(2)}) collective-permute-start(bf16[4,192,384]{2,1,0:T(8,128)(2,1)} %slice.789), channel_id=1, source_target_pairs={{0,16},{16,0},{1,17},{17,1},{2,18},{18,2},{3,19},{19,3},{4,20},{20... | collective-permute-start | bytes 1769480 | tf_op jit(solution)/shard_map/ppermute | solution.py:20
  752.8 51.3 %collective-permute-start.126 = (bf16[48,384]{1,0:T(8,128)(2,1)}, bf16[48,384]{1,0:T(8,128)(2,1)}, u32[]{:S(2)}, u32[]{:S(2)}) collective-permute-start(bf16[48,384]{1,0:T(8,128)(2,1)} %get-tuple-element.118), channel_id=1, source_target_pairs={{0,4},{4,0},{8,12},{12,8},{1,5},{5,1},{9,13},{13,9},{2,6},{6,2},{1... | collective-permute-start | bytes 110600 | tf_op jit(solution)/shard_map/ppermute | solution.py:20
  752.8 51.2 %collective-permute-start.127 = (bf16[48,384]{1,0:T(8,128)(2,1)}, bf16[48,384]{1,0:T(8,128)(2,1)}, u32[]{:S(2)}, u32[]{:S(2)}) collective-permute-start(bf16[48,384]{1,0:T(8,128)(2,1)} %get-tuple-element.118), channel_id=1, source_target_pairs={{0,8},{4,12},{8,0},{12,4},{1,9},{5,13},{9,1},{13,5},{2,10},{6,14},... | collective-permute-start | bytes 110600 | tf_op jit(solution)/shard_map/ppermute | solution.py:20
  834.1 55.3 %collective-permute-start.140 = (bf16[4,192,768]{2,1,0:T(8,128)(2,1)S(1)}, bf16[4,192,768]{2,1,0:T(8,128)(2,1)S(1)}, u32[]{:S(2)}, u32[]{:S(2)}) collective-permute-start(bf16[4,192,768]{2,1,0:T(8,128)(2,1)S(1)} %bitcast.825), channel_id=1, source_target_pairs={{0,4},{4,0},{8,12},{12,8},{1,5},{5,1},{9,13},{13,9},{2,6},{6,2},{1... | collective-permute-start | bytes 3538952 | tf_op jit(solution)/shard_map/ppermute | solution.py:20
  (301 other events, 3188.4 us)
Sparse Core Ops, SparseCore 0:
  712.8 88.9 all-reduce.6

commit v2 on v1

v2 whole, which is shorter than its diff:
```python
import jax
import jax.numpy as jnp
import numpy as np
from jax import lax
from jax.experimental import pallas as pl
from jax.experimental.pallas import tpu as pltpu
from jax.sharding import PartitionSpec as P

HEAD_DIM = 64
WINDOW = 64
EPS = 1e-06
SQRT_HALF = 0.7071067811865476
INV_ROOT_TAU = 0.3989422804014327
SCALE = HEAD_DIM**-0.5
HIDE = -1e30
LOW = jnp.bfloat16
F32 = jnp.float32
VMEM_BYTES = 60 * 2**20


def hop(values, axis, step):
    count = lax.axis_size(axis)
    return lax.ppermute(values, axis, [(i, i ^ step) for i in range(count)])


def hop_pair(values, step):
    ranks = lax.axis_size("tensor")
    pairs = [
        (a * ranks + i, (1 - a) * ranks + (i ^ step)) for a in range(2) for i in range(ranks)
    ]
    return lax.ppermute(values, ("shard", "tensor"), pairs)


def pick(values, index, axis=0):
    return lax.dynamic_index_in_dim(values, index, axis, keepdims=False)


def ordered(parts, me, axis=0):
    shape = list(parts[0].shape)
    shape.insert(axis, len(parts))
    out = jnp.zeros(shape, parts[0].dtype)
    for j, part in enumerate(parts):
        out = lax.dynamic_update_index_in_dim(out, part, me ^ j, axis)
    return out


def round_up(value, step):
    return -(-value // step) * step


class Place:
    def __init__(self):
        self.shard = lax.axis_index("shard")
        self.context = lax.axis_index("context")
        self.tensor = lax.axis_index("tensor")
        self.shards = lax.axis_size("shard")
        self.ranks = lax.axis_size("tensor")
        self.quarters = lax.axis_size("context")
        self.paired = self.shards == 2


def gather_columns(place, part):
    if place.paired:
        return jnp.concatenate([part, hop(part, "shard", 1)], -1)
    return lax.all_gather(part, "shard", axis=part.ndim - 1, tiled=True)


def gather_blocks(place, mine, axis=0):
    blocks = [mine] + [hop(mine, "tensor", k) for k in range(1, place.ranks)]
    first = gather_columns(place, jnp.stack(blocks, axis))
    second = hop(first, "context", 2)
    return [first, hop(first, "context", 1), second, hop(second, "context", 1)]


def add(*terms):
    total = terms[0].astype(F32)
    for term in terms[1:]:
        total = total + term.astype(F32)
    return total.astype(LOW)


def reduce_blocks(place, pieces, axis=0):
    first = add(pieces[0], hop(pieces[1], "context", 1))
    second = add(pieces[2], hop(pieces[3], "context", 1))
    total = add(first, hop(second, "context", 2))
    if place.paired:
        half = total.shape[-1] // 2
        mine = add(total[..., :half], hop(total[..., half:], "shard", 1))
    else:
        mine = lax.psum_scatter(total, "shard", scatter_dimension=total.ndim - 1, tiled=True)
    block = lambda k: lax.index_in_dim(mine, k, axis, keepdims=False)
    first = add(block(0), *[hop(block(k), "tensor", k) for k in range(1, place.ranks)])
    second = hop(first, "context", 2)
    parts = [first, hop(first, "context", 1), second, hop(second, "context", 1)]
    return ordered(parts, place.context).astype(F32)


class Layout:
    def __init__(self, place, clips, live):
        self.place = place
        self.batches, self.frames, self.places = clips.shape[:3]
        ranks = place.ranks
        self.whole = 1 if place.paired else self.batches
        self.split = self.batches - self.whole
        self.alive = live > 0
        self.first = -(-self.whole * self.places // ranks)
        self.later = -(-self.split * self.places // (2 * ranks))
        self.room = max(32, round_up(self.first + self.later, 16))
        self.block = self.frames * self.room
        self.place_rows = ranks * self.block
        self.units = self.whole * self.frames + self.split
        self.frame_rows = round_up(self.units * self.places, 16)
        self.natural_blocks = self.batches * self.frames
        self.sent = round_up(self.frames * self.first + self.later, 16)
        self.sent_pair = round_up(self.later, 16)

    def label(self, batch, frame, spot):
        return (batch * self.frames * self.place.ranks + frame) * self.places + spot

    def place_labels(self, shard, tensor, k):
        frame = self.frames * (tensor ^ k) + jnp.arange(self.frames)[:, None]
        slot = jnp.arange(self.room)[None]
        spot = self.first * tensor + slot
        whole = slot < self.first
        labels = self.label(spot // self.places, frame, spot % self.places)
        labels = jnp.where(whole & (spot < self.whole * self.places), labels, -1)
        if self.split:
            flat = self.later * (self.place.ranks * shard + tensor) + slot - self.first
            inside = (slot >= self.first) & (slot < self.first + self.later)
            inside = inside & (flat < self.split * self.places)
            other = self.label(self.whole + flat // self.places, frame, flat % self.places)
            labels = jnp.where(inside, other, labels)
        return labels, jnp.broadcast_to(whole, labels.shape)

    def frame_labels(self, shard, tensor):
        row = jnp.arange(self.frame_rows)
        unit, spot = row // self.places, row % self.places
        whole = unit < self.whole * self.frames
        labels = self.label(
            unit // self.frames, self.frames * tensor + unit % self.frames, spot
        )
        later = self.label(
            self.whole + unit - self.whole * self.frames, self.frames * tensor + shard, spot
        )
        labels = jnp.where(whole, labels, later)
        return jnp.where(unit < self.units, labels, -1), whole

    def natural_labels(self, tensor):
        batch = jnp.arange(self.batches)[:, None, None]
        frame = self.frames * tensor + jnp.arange(self.frames)[None, :, None]
        spot = jnp.arange(WINDOW)[None, None]
        return jnp.where(spot < self.places, self.label(batch, frame, spot), -1)

    def held(self, labels):
        batch = jnp.maximum(labels, 0) // (self.frames * self.place.ranks * self.places)
        return self.living(labels) | (batch < self.whole)

    def living(self, labels):
        batch = jnp.maximum(labels, 0) // (self.frames * self.place.ranks * self.places)
        return jnp.any((batch[..., None] == jnp.arange(self.batches)) & self.alive, -1)


def one_hot(targets, sources):
    targets = jnp.concatenate([item.reshape(-1) for item in targets])
    sources = jnp.concatenate([item.reshape(-1) for item in sources])
    sources = jnp.where(sources < 0, -2, sources)
    return (targets[:, None] == sources[None]).astype(LOW)


def call(body, outs, ins, scalars, flops=0, scratch=()):
    moved = sum(item.size * item.dtype.itemsize for item in list(outs) + list(ins))
    spec = pl.BlockSpec(memory_space=pltpu.VMEM)
    return pl.pallas_call(
        body,
        out_shape=tuple(outs),
        in_specs=[pl.BlockSpec(memory_space=pltpu.SMEM)] + [spec] * len(ins),
        out_specs=(spec,) * len(outs),
        scratch_shapes=list(scratch),
        compiler_params=pltpu.CompilerParams(vmem_limit_bytes=VMEM_BYTES),
        cost_estimate=pl.CostEstimate(flops=flops, bytes_accessed=moved, transcendentals=0),
    )(scalars, *ins)


def shape(*dims, dtype=LOW):
    return jax.ShapeDtypeStruct(dims, dtype)


def nn(first, second):
    return lax.dot_general(first, second, (((1,), (0,)), ((), ())), preferred_element_type=F32)


def nt(first, second):
    return lax.dot_general(first, second, (((1,), (1,)), ((), ())), preferred_element_type=F32)


def tn(first, second):
    return lax.dot_general(first, second, (((0,), (0,)), ((), ())), preferred_element_type=F32)


def swapper(scalars, paired):
    def swap(values):
        if not paired:
            return values
        half = values.shape[-1] // 2
        other = jnp.concatenate([values[:, half:], values[:, :half]], -1)
        return jnp.where(scalars[0] == 0, values, other)

    return swap


def unit_of(values):
    centred = values - jnp.mean(values, -1, keepdims=True)
    inverse = lax.rsqrt(jnp.mean(centred * centred, -1, keepdims=True) + EPS)
    return (centred * inverse, inverse)


def norm_back(grad, unit, inverse, gain):
    scaled = grad * gain
    inner = (
        scaled
        - jnp.mean(scaled, -1, keepdims=True)
        - unit * jnp.mean(scaled * unit, -1, keepdims=True)
    )
    return (
        inverse * inner,
        jnp.sum(grad * unit, 0, keepdims=True),
        jnp.sum(grad, 0, keepdims=True),
    )


def softmax(scores):
    weights = jnp.exp(scores - jnp.max(scores, -1, keepdims=True))
    return weights / jnp.sum(weights, -1, keepdims=True)


def score_back(probs, prob_grad):
    inner = jnp.sum(probs * prob_grad, -1, keepdims=True)
    return (probs * (prob_grad - inner)).astype(LOW)


def half_lanes(width):
    lane = lax.broadcasted_iota(jnp.int32, (1, width), 1)
    return [(lane // HEAD_DIM == e).astype(F32) for e in range(2)]


def column_sum(values):
    return jnp.sum(values.astype(F32), 0, keepdims=True)


def rows_at(start, size):
    return pl.ds(pl.multiple_of(start, 16), size)


class Program:
    def __init__(self, place, layout, width, group, scalars):
        self.place, self.layout, self.width, self.group = place, layout, width, group
        self.scalars = scalars
        self.ranks, self.quarters = place.ranks, place.quarters
        self.piece = group // self.quarters
        self.heads = group // HEAD_DIM
        self.all_heads = group * self.ranks
        spot = np.arange(layout.place_rows) % layout.room
        self.same_place = jnp.asarray(
            np.where(spot[:, None] == spot[None], 0, HIDE).astype(np.float32)
        )

    def call(self, body, outs, ins, flops=0, scratch=()):
        return call(body, outs, ins, self.scalars, flops, scratch)


    def send_rows(self, clips, cotangents, matrix, targets):
        lay, width = self.layout, self.width
        count, split = lay.natural_blocks, lay.split
        first = lay.whole * lay.frames

        def body(scalars, clips_ref, grads_ref, matrix_ref, *refs):
            sent, refs = refs[:targets], refs[targets:]
            rows = refs[-1]
            rows[...] = jnp.zeros_like(rows)
            for item in range(count):
                rows[item * WINDOW : item * WINDOW + lay.places] = clips_ref[item]
            for item in range(targets):
                part = matrix_ref[item * lay.block : (item + 1) * lay.block]
                sent[item][...] = nn(part, rows[...]).astype(LOW)
            for index, source in enumerate((clips_ref, grads_ref) if split else ()):
                for item in range(split):
                    frame = first + lay.frames * item + 1 - scalars[0]
                    refs[index][item] = source[frame]

        outs = [shape(lay.block, width)] * targets
        if split:
            outs += [shape(split, lay.places, width)] * 2
        return self.call(
            body, outs, [clips, cotangents, matrix], scratch=[pltpu.VMEM((count * WINDOW, width), LOW)]
        )

    def frames_of(self, clips, others, matrix):
        lay, width = self.layout, self.width
        count, split = lay.natural_blocks, lay.split

        def body(scalars, clips_ref, *refs):
            matrix_ref, out_ref, rows = refs[-3:]
            rows[...] = jnp.zeros_like(rows)
            for item in range(count):
                rows[item * WINDOW : item * WINDOW + lay.places] = clips_ref[item]
            for item in range(split):
                start = (count + item) * WINDOW
                rows[start : start + lay.places] = refs[0][item]
            out_ref[...] = nn(matrix_ref[...], rows[...]).astype(LOW)

        return self.call(
            body,
            [shape(lay.frame_rows, width)],
            [clips] + ([others] if split else []) + [matrix],
            scratch=[pltpu.VMEM(((count + split) * WINDOW, width), LOW)],
        )[0]


    def temporal(self, blocks, pairs, keep, pieces, along, shift):
        lay, width = self.layout, self.width
        rows, ranks = lay.place_rows, self.ranks
        wide = 3 * self.all_heads
        split = lay.split > 0

        def body(scalars, *refs):
            refs = list(refs)
            take = lambda n: [refs.pop(0) for _ in range(n)]
            block_refs, pair_refs = take(ranks), take(ranks if split else 0)
            keep_ref, piece_refs, along_ref, shift_ref, same = (
                take(1)[0], take(self.quarters), take(1)[0], take(1)[0], take(1)[0],
            )
            sent, sent_pair = take(ranks), take(ranks if split else 0)
            normed_ref, rows_ref, qkv, mixed, win, wout = take(6)
            swap = swapper(scalars, self.place.paired)
            for j in range(self.quarters):
                spot = scalars[1] ^ j
                for k in range(ranks):
                    for c in range(3):
                        at = c * self.all_heads + k * self.group + spot * self.piece
                        win[rows_at(at, self.piece)] = piece_refs[j][
                            k, c * self.piece : (c + 1) * self.piece
                        ]
                    at = k * self.group + spot * self.piece
                    wout[rows_at(at, self.piece)] = piece_refs[j][
                        k, 3 * self.piece : 4 * self.piece
                    ]
            start = jnp.concatenate([ref[...] for ref in block_refs]).astype(F32)
            start = jnp.where(keep_ref[:, 0:1] > 0, start, 0)
            if split:
                other = jnp.concatenate([ref[...] for ref in pair_refs]).astype(F32)
                start = jnp.where(keep_ref[:, 1:2] > 0, other, start)
            rows_ref[...] = start.astype(LOW)
            unit, _ = unit_of(start)
            normed_ref[...] = swap(unit * along_ref[0:1] + along_ref[3:4]).astype(LOW)

            @pl.loop(0, wide // 256)
            def _(n):
                at = pl.ds(pl.multiple_of(n * 256, 256), 256)
                qkv[:, at] = (nt(normed_ref[...], win[at]) + shift_ref[:, at]).astype(LOW)

            @pl.loop(0, self.all_heads // 128)
            def _(n):
                lanes = lambda c: pl.ds(pl.multiple_of(c * self.all_heads + n * 128, 128), 128)
                query, key, value = (qkv[:, lanes(c)] for c in range(3))
                total = jnp.zeros((rows, 128), F32)
                for mask in half_lanes(128):
                    scores = nt(query * mask.astype(LOW), key) * SCALE + same[...]
                    total = total + nn(softmax(scores).astype(LOW), value) * mask
                mixed[:, lanes(0)] = total.astype(LOW)

            out = swap(nn(mixed[...], wout[...])) + along_ref[6:7]
            for k in range(ranks):
                part = out[k * lay.block : (k + 1) * lay.block]
                sent[k][...] = part.astype(LOW)
                if split:
                    pair = jnp.where(scalars[0] == 0, part[lay.room :], part[: lay.room])
                    sent_pair[k][...] = pair.astype(LOW)

        outs = [shape(lay.block, width)] * ranks
        if split:
            outs += [shape(lay.room, width)] * ranks
        outs += [
            shape(rows, width),
            shape(rows, width),
            shape(rows, wide),
            shape(rows, self.all_heads),
            shape(wide, width),
            shape(self.all_heads, width),
        ]
        ins = list(blocks) + list(pairs) + [keep] + list(pieces) + [along, shift, self.same_place]
        flops = 2 * rows * width * (wide + self.all_heads) + 4 * rows * rows * self.all_heads
        outs = self.call(body, outs, ins, flops)
        sent, outs = outs[:ranks], outs[ranks:]
        if split:
            sent_pair, outs = outs[:ranks], outs[ranks:]
        else:
            sent_pair = ()
        return sent, sent_pair, outs

    def temporal_back(self, sources, matrix, qkv, mixed, wout):
        lay, width = self.layout, self.width
        rows, wide = lay.place_rows, 3 * self.all_heads

        def body(scalars, *refs):
            source_refs = refs[: len(sources)]
            matrix_ref, qkv_ref, mixed_ref, wout_ref, same, grad_ref, out_ref, part = refs[
                len(sources) :
            ]
            swap = swapper(scalars, self.place.paired)
            source = jnp.concatenate([ref[...] for ref in source_refs])
            grad_ref[...] = swap(nn(matrix_ref[...], source)).astype(LOW)
            part[...] = nt(grad_ref[...], wout_ref[...]).astype(LOW)

            @pl.loop(0, self.all_heads // 128)
            def _(n):
                lanes = lambda c: pl.ds(pl.multiple_of(c * self.all_heads + n * 128, 128), 128)
                query, key, value = (qkv_ref[:, lanes(c)] for c in range(3))
                grad = part[:, lanes(0)]
                totals = [jnp.zeros((rows, 128), F32) for _ in range(3)]
                for mask in half_lanes(128):
                    low = mask.astype(LOW)
                    probs = softmax(nt(query * low, key) * SCALE + same[...])
                    scored = score_back(probs, nt(grad * low, value))
                    for c, item in enumerate(
                        (
                            nn(scored, key) * SCALE,
                            tn(scored, query) * SCALE,
                            tn(probs.astype(LOW), grad),
                        )
                    ):
                        totals[c] = totals[c] + item * mask
                for c in range(3):
                    out_ref[:, lanes(c)] = totals[c].astype(LOW)

        outs = [shape(rows, width), shape(rows, wide)]
        ins = list(sources) + [matrix, qkv, mixed, wout, self.same_place]
        flops = 2 * rows * width * self.all_heads + 10 * rows * rows * self.all_heads
        return self.call(
            body, outs, ins, flops, scratch=[pltpu.VMEM((rows, self.all_heads), LOW)]
        )

    def temporal_weights(self, qkv_grad, normed, mixed, out_grad):
        lay, width = self.layout, self.width
        rows, ranks = lay.place_rows, self.ranks

        def body(scalars, grad_ref, normed_ref, mixed_ref, out_ref, *pieces):
            pieces, sums = pieces[: self.quarters], pieces[self.quarters]
            sums[...] = column_sum(grad_ref[...])

            def put(total, k, c):
                for j in range(self.quarters):
                    at = rows_at((scalars[1] ^ j) * self.piece, self.piece)
                    pieces[j][k, c * self.piece : (c + 1) * self.piece] = total[at]

            def inner(total):
                for c in range(3):
                    for k in range(ranks):
                        at = c * self.all_heads + k * self.group
                        part = tn(grad_ref[:, at : at + self.group], normed_ref[...])
                        total[...] = part.astype(LOW)
                        put(total, k, c)
                for k in range(ranks):
                    at = k * self.group
                    part = tn(mixed_ref[:, at : at + self.group], out_ref[...])
                    total[...] = part.astype(LOW)
                    put(total, k, 3)

            pl.run_scoped(inner, pltpu.VMEM((self.group, width), LOW))

        outs = [shape(ranks, 4 * self.piece, width)] * self.quarters
        outs += [shape(1, 3 * self.all_heads, dtype=F32)]
        flops = 8 * rows * width * self.all_heads
        outs = self.call(body, outs, [qkv_grad, normed, mixed, out_grad], flops)
        return outs[:-1], outs[-1]

    def temporal_input(self, qkv_grad, win, start, along):
        lay, width = self.layout, self.width
        ranks = self.ranks

        def body(scalars, grad_ref, win_ref, start_ref, along_ref, *refs):
            sent, sums = refs[:ranks], refs[ranks]
            swap = swapper(scalars, self.place.paired)
            unit, inverse = unit_of(start_ref[...].astype(F32))
            grad = swap(nn(grad_ref[...], win_ref[...]))
            back, gain, shift = norm_back(grad, unit, inverse, along_ref[0:1])
            sums[0:1] = gain
            sums[1:2] = shift
            for k in range(ranks):
                sent[k][...] = back[k * lay.block : (k + 1) * lay.block].astype(LOW)

        outs = [shape(lay.block, width)] * ranks + [shape(2, width, dtype=F32)]
        flops = 6 * lay.place_rows * width * self.all_heads
        outs = self.call(body, outs, [qkv_grad, win, start, along], flops)
        return outs[:-1], outs[-1]


    def spatial_in(self, sources, matrix, start, pieces, along, shift):
        lay, width = self.layout, self.width
        rows, ranks, quarters = lay.frame_rows, self.ranks, self.quarters
        piece, group = self.piece, self.group

        def body(scalars, *refs):
            refs = list(refs)
            take = lambda n: [refs.pop(0) for _ in range(n)]
            source_refs = take(len(sources))
            matrix_ref, start_ref = take(2)
            piece_refs = take(quarters)
            along_ref, shift_ref = take(2)
            after_ref, temporal_ref, normed_ref = take(3)
            qkv_refs = take(quarters)
            win, wout, fc = take(3)
            swap = swapper(scalars, self.place.paired)
            for i in range(quarters):
                spot = scalars[1] ^ i
                for j in range(quarters):
                    k = scalars[1] ^ j
                    for c in range(3):
                        at = j * 3 * group + c * group + spot * piece
                        win[rows_at(at, piece)] = piece_refs[i][k, c * piece : (c + 1) * piece]
                    at = j * group + spot * piece
                    wout[rows_at(at, piece)] = piece_refs[i][k, 3 * piece : 4 * piece]
                for k in range(ranks):
                    at = (scalars[2] ^ k) * group + spot * piece
                    fc[rows_at(at, piece)] = piece_refs[i][k, 4 * piece : 5 * piece]
            source = jnp.concatenate([ref[...] for ref in source_refs])
            temporal = swap(nn(matrix_ref[...], source)).astype(LOW)
            temporal_ref[...] = temporal
            after = start_ref[...].astype(F32) + nt(temporal, fc[...]) + along_ref[7:8]
            after_ref[...] = after
            unit, _ = unit_of(after)
            normed = swap(unit * along_ref[1:2] + along_ref[4:5]).astype(LOW)
            normed_ref[...] = normed
            for j in range(quarters):
                at = slice(j * 3 * group, (j + 1) * 3 * group)
                qkv_refs[j][...] = (nt(normed, win[at]) + shift_ref[:, at]).astype(LOW)

        outs = [shape(rows, width, dtype=F32), shape(rows, width), shape(rows, width)]
        outs += [shape(rows, 3 * group)] * quarters
        outs += [
            shape(3 * self.all_heads, width),
            shape(self.all_heads, width),
            shape(width, width),
        ]
        ins = list(sources) + [matrix, start] + list(pieces) + [along, shift]
        flops = 2 * rows * width * (3 * self.all_heads + width)
        outs = self.call(body, outs, ins, flops)
        return outs[:3], outs[3 : 3 + quarters], outs[3 + quarters :]

    def windows(self, refs, n):
        at = rows_at(n * (WINDOW - 16), WINDOW)
        return jnp.concatenate([ref[at] for ref in refs])

    def window_mask(self, n, axis):
        size = self.quarters * WINDOW
        dims = (size, 1) if axis == 0 else (1, size)
        index = lax.broadcasted_iota(jnp.int32, dims, axis) & (WINDOW - 1)
        start = n * (self.layout.places - WINDOW + 16)
        return (index >= start) & (index < start + self.layout.places)

    def put_windows(self, refs, n, values, mask):
        for j, ref in enumerate(refs):
            at = rows_at(n * (WINDOW - 16), WINDOW)
            part = slice(j * WINDOW, (j + 1) * WINDOW)
            old = ref[at].astype(F32)
            ref[at] = jnp.where(mask[part], values[part], old).astype(LOW)

    def spatial(self, qkv):
        lay, quarters, group = self.layout, self.quarters, self.group

        def body(scalars, *refs):
            qkv_refs, out_refs = refs[:quarters], refs[quarters:]
            for ref in out_refs:
                ref[...] = jnp.zeros_like(ref)

            @pl.loop(0, lay.units)
            def _(n):
                rows = self.windows(qkv_refs, n)
                hide = jnp.where(self.window_mask(n, 1), 0.0, HIDE)
                parts = []
                for h in range(self.heads):
                    query, key, value = (
                        rows[:, c * group + h * HEAD_DIM : c * group + (h + 1) * HEAD_DIM]
                        for c in range(3)
                    )
                    probs = softmax(nt(query, key) * SCALE + hide)
                    parts.append(nn(probs.astype(LOW), value))
                mask = self.window_mask(n, 0)
                self.put_windows(out_refs, n, jnp.concatenate(parts, -1), mask)

        outs = [shape(lay.frame_rows, group)] * quarters
        size = quarters * WINDOW
        return self.call(body, outs, list(qkv), 4 * lay.units * size * size * group)

    def spatial_back(self, qkv, grads):
        lay, quarters, group = self.layout, self.quarters, self.group

        def body(scalars, *refs):
            qkv_refs, grad_refs = refs[:quarters], refs[quarters : 2 * quarters]
            out_refs = refs[2 * quarters :]
            for ref in out_refs:
                ref[...] = jnp.zeros_like(ref)

            @pl.loop(0, lay.units)
            def _(n):
                rows = self.windows(qkv_refs, n)
                mask = self.window_mask(n, 0)
                grads = self.windows(grad_refs, n) * mask.astype(F32).astype(LOW)
                hide = jnp.where(self.window_mask(n, 1), 0.0, HIDE)
                parts = [[], [], []]
                for h in range(self.heads):
                    query, key, value = (
                        rows[:, c * group + h * HEAD_DIM : c * group + (h + 1) * HEAD_DIM]
                        for c in range(3)
                    )
                    grad = grads[:, h * HEAD_DIM : (h + 1) * HEAD_DIM]
                    probs = softmax(nt(query, key) * SCALE + hide)
                    scored = score_back(probs, nt(grad, value))
                    parts[0].append(nn(scored, key) * SCALE)
                    parts[1].append(tn(scored, query) * SCALE)
                    parts[2].append(tn(probs.astype(LOW), grad))
                values = jnp.concatenate(parts[0] + parts[1] + parts[2], -1)
                self.put_windows(out_refs, n, values, mask)

        outs = [shape(lay.frame_rows, 3 * group)] * quarters
        size = quarters * WINDOW
        flops = 10 * lay.units * size * size * group
        return self.call(body, outs, list(qkv) + list(grads), flops)

    def spatial_out(self, mixed, wout, after, grad, along):
        lay, width, group = self.layout, self.width, self.group
        rows, quarters = lay.frame_rows, self.quarters

        def body(scalars, *refs):
            mixed_refs = refs[:quarters]
            wout_ref, after_ref, grad_ref, along_ref, out_ref, normed_ref, low_ref = refs[quarters:]
            swap = swapper(scalars, self.place.paired)
            total = jnp.zeros((rows, width), F32)
            for j in range(quarters):
                total = total + nn(mixed_refs[j][...], wout_ref[j * group : (j + 1) * group])
            after = after_ref[...] + swap(total) + along_ref[8:9]
            out_ref[...] = after
            unit, _ = unit_of(after)
            normed_ref[...] = swap(unit * along_ref[2:3] + along_ref[5:6]).astype(LOW)
            low_ref[...] = swap(grad_ref[...].astype(F32)).astype(LOW)

        outs = [shape(rows, width, dtype=F32), shape(rows, width), shape(rows, width)]
        ins = list(mixed) + [wout, after, grad, along]
        return self.call(body, outs, ins, 2 * rows * width * self.all_heads)

    def feed_forward(self, normed, grad, weights, shift, totals):
        lay, width = self.layout, self.width
        rows = lay.frame_rows
        hidden = weights.shape[1]
        tile = 256

        def body(scalars, normed_ref, grad_ref, weight_ref, shift_ref, *refs):
            out_ref, back_ref, weight_grad, sums = refs[-4:]
            if totals is None:
                out_ref[...] = jnp.zeros_like(out_ref)
                back_ref[...] = jnp.zeros_like(back_ref)
            else:
                out_ref[...] = refs[0][...]
                back_ref[...] = refs[1][...]

            @pl.loop(0, hidden // tile)
            def _(n):
                at = pl.ds(pl.multiple_of(n * tile, tile), tile)
                up, down = weight_ref[0, at], weight_ref[1, at]
                values = nt(normed_ref[...], up) + shift_ref[:, at]
                half = 0.5 * (1.0 + lax.erf(values * SQRT_HALF))
                active = (values * half).astype(LOW)
                slope = half + values * jnp.exp(-0.5 * values * values) * INV_ROOT_TAU
                out_ref[...] += nn(active, down)
                weight_grad[1, at] = tn(active, grad_ref[...]).astype(LOW)
                hidden_grad = (nt(grad_ref[...], down) * slope).astype(LOW)
                weight_grad[0, at] = tn(hidden_grad, normed_ref[...]).astype(LOW)
                back_ref[...] += nn(hidden_grad, up)
                sums[:, at] = column_sum(hidden_grad)

        outs = [
            shape(rows, width, dtype=F32),
            shape(rows, width, dtype=F32),
            shape(2, hidden, width),
            shape(1, hidden, dtype=F32),
        ]
        ins = [normed, grad, weights, shift] + ([] if totals is None else list(totals))
        return self.call(body, outs, ins, 12 * rows * width * hidden)

    def feed_forward_back(self, after, out, back, grad, mixed, wout, along):
        lay, width, group = self.layout, self.width, self.group
        rows, quarters = lay.frame_rows, self.quarters

        def body(scalars, after_ref, out_ref, back_ref, grad_ref, wout_ref, along_ref, *refs):
            mixed_refs, refs = refs[:quarters], refs[quarters:]
            layer_ref, total_ref, sums, wout_grad = refs[:4]
            mixed_grads = refs[4:]
            swap = swapper(scalars, self.place.paired)
            after = after_ref[...]
            layer_ref[...] = (after + swap(out_ref[...]) + along_ref[9:10]).astype(LOW)
            unit, inverse = unit_of(after)
            back, gain, shift = norm_back(swap(back_ref[...]), unit, inverse, along_ref[2:3])
            grad = grad_ref[...].astype(F32)
            total = grad + back
            total_ref[...] = total
            low = total.astype(LOW)
            sums[0:1] = gain
            sums[1:2] = shift
            sums[2:3] = column_sum(low)
            sums[3:4] = column_sum(grad)
            low = swap(low.astype(F32)).astype(LOW)
            for j in range(quarters):
                at = slice(j * group, (j + 1) * group)
                mixed_grads[j][...] = nt(low, wout_ref[at]).astype(LOW)
                wout_grad[at] = tn(mixed_refs[j][...], low).astype(LOW)

        outs = [
            shape(rows, width),
            shape(rows, width, dtype=F32),
            shape(4, width, dtype=F32),
            shape(self.all_heads, width),
        ] + [shape(rows, group)] * quarters
        ins = [after, out, back, grad, wout, along] + list(mixed)
        outs = self.call(body, outs, ins, 4 * rows * width * self.all_heads)
        return outs[:4], outs[4:]

    def spatial_input(self, qkv_grads, win, after, total, along, fc, matrix):
        lay, width, group = self.layout, self.width, self.group
        rows, quarters, ranks = lay.frame_rows, self.quarters, self.ranks
        split = lay.split > 0

        def body(scalars, *refs):
            grad_refs = refs[:quarters]
            win_ref, after_ref, total_ref, along_ref, fc_ref, matrix_ref = refs[
                quarters : quarters + 6
            ]
            out_ref, low_ref, sums = refs[quarters + 6 : quarters + 9]
            sent = refs[quarters + 9 :]
            swap = swapper(scalars, self.place.paired)
            grad = jnp.zeros((rows, width), F32)
            for j in range(quarters):
                at = slice(j * 3 * group, (j + 1) * 3 * group)
                grad = grad + nn(grad_refs[j][...], win_ref[at])
            unit, inverse = unit_of(after_ref[...])
            back, gain, shift = norm_back(swap(grad), unit, inverse, along_ref[1:2])
            total = total_ref[...] + back
            out_ref[...] = total
            low = total.astype(LOW)
            low_ref[...] = low
            temporal = swap(nn(low, fc_ref[...])).astype(LOW)
            sums[0:1] = gain
            sums[1:2] = shift
            sums[2:3] = column_sum(temporal)
            sums[3:4] = column_sum(low)
            at = 0
            for ref in sent:
                size = ref.shape[0]
                ref[...] = nn(matrix_ref[at : at + size], temporal).astype(LOW)
                at += size

        outs = [
            shape(rows, width, dtype=F32),
            shape(rows, width),
            shape(4, width, dtype=F32),
        ]
        outs += [shape(lay.sent, width)] * ranks
        outs += [shape(lay.sent_pair, width)] * (ranks if split else 0)
        ins = list(qkv_grads) + [win, after, total, along, fc, matrix]
        outs = self.call(body, outs, ins, 2 * rows * width * (3 * self.all_heads + width))
        return outs[:3], outs[3 : 3 + ranks], outs[3 + ranks :]

    def spatial_weights(self, qkv_grads, normed, wout_grad, low, temporal):
        lay, width, group, piece = self.layout, self.width, self.group, self.piece
        rows, quarters, ranks = lay.frame_rows, self.quarters, self.ranks

        def body(scalars, *refs):
            grad_refs = refs[:quarters]
            normed_ref, wout_ref, low_ref, temporal_ref = refs[quarters : quarters + 4]
            pieces = refs[quarters + 4 : 2 * quarters + 4]
            sums = refs[2 * quarters + 4]

            def inner(total, fc):
                for j in range(quarters):
                    k = scalars[1] ^ j
                    at = slice(j * 3 * group, (j + 1) * 3 * group)
                    sums[:, at] = column_sum(grad_refs[j][...])
                    total[...] = tn(grad_refs[j][...], normed_ref[...]).astype(LOW)
                    for i in range(quarters):
                        spot = (scalars[1] ^ i) * piece
                        for c in range(3):
                            pieces[i][k, c * piece : (c + 1) * piece] = total[
                                rows_at(c * group + spot, piece)
                            ]
                        pieces[i][k, 3 * piece : 4 * piece] = wout_ref[
                            rows_at(j * group + spot, piece)
                        ]
                fc[...] = tn(low_ref[...], temporal_ref[...]).astype(LOW)
                for i in range(quarters):
                    for k in range(ranks):
                        at = (scalars[2] ^ k) * group + (scalars[1] ^ i) * piece
                        pieces[i][k, 4 * piece : 5 * piece] = fc[rows_at(at, piece)]

            pl.run_scoped(
                inner,
                pltpu.VMEM((3 * group, width), LOW),
                pltpu.VMEM((width, width), LOW),
            )

        outs = [shape(ranks, 5 * piece, width)] * quarters
        outs += [shape(1, 3 * self.all_heads, dtype=F32)]
        ins = list(qkv_grads) + [normed, wout_grad, low, temporal]
        flops = 2 * rows * width * (3 * self.all_heads + width)
        outs = self.call(body, outs, ins, flops)
        return outs[:-1], outs[-1]

    def natural(self, parts):
        lay, width = self.layout, self.width
        count = lay.natural_blocks
        counts = [len(rows) for _, rows in parts]

        def body(scalars, *refs):
            refs = list(refs)
            out_ref = refs.pop()
            total = jnp.zeros((count * WINDOW, width), F32)
            for size in counts:
                matrix = refs.pop(0)
                source = jnp.concatenate([refs.pop(0)[...] for _ in range(size)])
                total = total + nn(matrix[...], source)
            total = total.astype(LOW)
            for item in range(count):
                out_ref[item] = total[item * WINDOW : item * WINDOW + lay.places]

        ins = []
        for matrix, rows in parts:
            ins += [matrix] + list(rows)
        return self.call(body, [shape(count, lay.places, width)], ins)[0]


def body(
    clip_input,
    clip_slot,
    norm_gain,
    norm_shift,
    attention_in,
    attention_bias,
    attention_out,
    branch_bias,
    temporal_fc,
    hidden_in,
    hidden_bias,
    hidden_out,
    output_grad,
):
    place = Place()
    shards, quarters, ranks = place.shards, place.quarters, place.ranks
    shard, context, tensor = place.shard, place.context, place.tensor
    clips, live = clip_input[:, 0], clip_slot[:, 0]
    lay = Layout(place, clips, live)
    mask = live[:, None, None, None].astype(LOW)
    cotangents = output_grad[:, 0] * mask
    columns = attention_in.shape[1]
    width = columns * shards
    group = attention_in.shape[3]
    hidden = hidden_in.shape[1]
    piece = group // quarters
    split = lay.split > 0
    scalars = jnp.stack([shard, context, tensor]).astype(jnp.int32)
    prog = Program(place, lay, width, group, scalars)

    vectors = jnp.concatenate(
        [norm_gain, norm_shift, branch_bias, attention_bias.reshape(-1, columns)]
        + [hidden_bias.reshape(-1, columns)]
    )
    if place.paired:
        both = jnp.stack([vectors, hop(vectors, "shard", 1)])
        both = jnp.where(shard == 0, both, both[::-1])
    else:
        both = lax.all_gather(vectors, "shard")
    along = jnp.swapaxes(both[:, :10], 0, 1).reshape(10, width).astype(F32)
    last = 10 + attention_bias.size // columns
    own = both[:, 10:]
    own = jnp.stack([own] + [hop(own, "tensor", k) for k in range(1, ranks)], 1).astype(F32)
    biases = own[:, :, : last - 10].reshape((shards, ranks) + attention_bias.shape)
    biases = jnp.transpose(biases, (2, 3, 1, 4, 0, 5)).reshape(2, 2, ranks, group)
    biases = jnp.stack([biases[:, 0], jnp.zeros_like(biases[:, 0]), biases[:, 1]], 1)
    shift_a = biases[0].reshape(1, -1)
    shift_b = jnp.swapaxes(biases[1], 0, 1)
    shift_b = jnp.stack([pick(shift_b, context ^ j) for j in range(quarters)]).reshape(1, -1)
    up_shift = own[:, :, last - 10 :].reshape((shards, ranks) + hidden_bias.shape)
    up_shift = jnp.transpose(up_shift, (1, 2, 0, 3)).reshape(ranks, quarters, -1)
    up_shift = [pick(up_shift, context ^ j, 1).reshape(1, -1) for j in range(quarters)]

    def quarter_in(weight):
        part = pick(weight.reshape(columns, 3, quarters, piece), context, 2)
        return jnp.transpose(part, (1, 2, 0)).reshape(3 * piece, columns)

    def quarter(rows):
        return pick(rows.reshape(quarters, -1, rows.shape[-1]), context)

    fc_part = lax.dynamic_slice_in_dim(
        temporal_fc, (tensor * quarters + context) * piece, piece, 1
    ).T
    block_a = jnp.concatenate([quarter_in(attention_in[0]), quarter(attention_out[0])])
    block_b = jnp.concatenate([quarter_in(attention_in[1]), quarter(attention_out[1]), fc_part])
    up_part = pick(hidden_in.reshape(columns, quarters, -1), context, 1).T
    block_c = jnp.stack([up_part, quarter(hidden_out)])
    pieces_a = gather_blocks(place, block_a)
    pieces_b = gather_blocks(place, block_b)
    pieces_c = gather_blocks(place, block_c, 1)
    pieces_c = [item.reshape(2, -1, width) for item in pieces_c]

    steps = [(0, k) for k in range(ranks)] + [(1, k) for k in range(ranks if split else 0)]

    def across(values, step):
        pair, k = step
        if pair:
            return hop_pair(values, k)
        return values if k == 0 else hop(values, "tensor", k)

    flip = lambda pair: 1 - shard if pair else shard
    natural = lay.natural_labels(tensor)
    alive = lay.held(natural)
    frame, frame_whole = lay.frame_labels(shard, tensor)
    sending = one_hot(
        [lay.place_labels(flip(pair), tensor ^ k, k)[0] for pair, k in steps], [natural]
    )
    here = [lay.place_labels(shard, tensor, k) for k in range(ranks)]
    here_labels = jnp.stack([labels for labels, _ in here])
    here_whole = jnp.stack([whole for _, whole in here])
    here_mine = (here_whole | lay.held(here_labels)) & (here_labels >= 0)
    keep = jnp.stack([here_mine, (here_labels >= 0) & ~here_mine], -1)
    keep = keep.reshape(-1, 2).astype(F32)
    start_sources = [jnp.where(alive, natural, -1)]
    if split:
        spot = jnp.arange(WINDOW)
        batch = jnp.arange(lay.whole, lay.batches)[:, None]
        others = lay.label(batch, lay.frames * tensor + shard, spot)
        others = jnp.where((spot < lay.places) & ~lay.held(others), others, -1)
        start_sources.append(others)
    starting = one_hot([frame], start_sources)

    def source_labels(step):
        pair, k = step
        labels, whole = lay.place_labels(flip(pair), tensor ^ k, k)
        return jnp.where(whole, -1, labels) if pair else labels

    returning = one_hot(
        [frame],
        [source_labels((0, k)) for k in range(ranks)]
        + [pick(source_labels((1, k)), shard) for k in range(ranks if split else 0)],
    )

    def packed(labels, whole_too, index):
        parts = [labels[:, : lay.first].reshape(-1)] if whole_too else []
        if split:
            parts.append(pick(labels, index)[lay.first : lay.first + lay.later])
        parts = jnp.concatenate(parts)
        size = lay.sent if whole_too else lay.sent_pair
        return jnp.pad(parts, (0, size - parts.shape[0]), constant_values=-1)

    leaving = one_hot(
        [
            packed(lay.place_labels(flip(pair), tensor ^ k, k)[0], not pair, shard)
            for pair, k in steps
        ],
        [frame],
    )
    arriving = one_hot(
        [labels for labels, _ in here],
        [packed(here[k][0], not pair, flip(pair)) for pair, k in steps],
    )
    home = jnp.where(lay.living(natural), natural, -1)
    homing = one_hot([home], [source_labels(step) for step in steps])
    ending = [one_hot([home], [frame])]
    if split:
        far, far_whole = lay.frame_labels(1 - shard, tensor)
        ending.append(one_hot([home], [jnp.where(far_whole, -1, far)]))

    flat = lambda rows: rows.reshape((-1,) + rows.shape[2:])
    clips, cotangents = flat(clips), flat(cotangents)
    sent = prog.send_rows(clips, cotangents, sending, len(steps))
    blocks = [across(rows, step) for rows, step in zip(sent, steps)]
    other_clips, other_grads = [hop(rows, "shard", 1) for rows in sent[len(steps) :]] or (None,) * 2
    start = prog.frames_of(clips, other_clips, starting)
    grad = prog.frames_of(cotangents, other_grads, starting)

    sent, sent_pair, kept = prog.temporal(
        blocks[:ranks], blocks[ranks:], keep, pieces_a, along, shift_a
    )
    normed_a, start_a, qkv_a, mixed_a, win_a, wout_a = kept
    sources = [across(rows, step) for rows, step in zip(list(sent) + list(sent_pair), steps)]

    def to_groups(parts):
        return [parts[0]] + [hop(parts[j], "context", j) for j in range(1, quarters)]

    kept, qkv, weights_b = prog.spatial_in(sources, returning, start, pieces_b, along, shift_b)
    after_a, temporal, normed_b = kept
    win_b, wout_b, fc = weights_b
    qkv = to_groups(qkv)
    mixed = to_groups(prog.spatial(qkv))
    after_b, normed_c, low = prog.spatial_out(mixed, wout_b, after_a, grad, along)

    totals, piece_grads, up_bias_grads = None, [None] * quarters, [None] * quarters
    for j in (1, 3, 0, 2):
        out, back, piece_grads[j], up_bias_grads[j] = prog.feed_forward(
            normed_c, low, pieces_c[j], up_shift[j], totals
        )
        totals = (out, back)
    kept, mixed_grads = prog.feed_forward_back(
        after_b, totals[0], totals[1], grad, mixed, wout_b, along
    )
    layer_rows, total, sums_c, wout_grad = kept
    total_c = reduce_blocks(
        place, [item.reshape(2, ranks, -1, width) for item in piece_grads], 1
    )
    layer_out = [(ending[0], [layer_rows])]
    if split:
        layer_out.append((ending[1], [hop(layer_rows, "shard", 1)]))
    layer_out = prog.natural(layer_out)

    qkv_grads = to_groups(prog.spatial_back(qkv, to_groups(mixed_grads)))
    kept, sent, sent_pair = prog.spatial_input(
        qkv_grads, win_b, after_a, total, along, fc, leaving
    )
    total, low_fc, sums_b = kept
    pieces, pair_b = prog.spatial_weights(qkv_grads, normed_b, wout_grad, low_fc, temporal)
    total_b = reduce_blocks(place, pieces)
    sources = [across(rows, step) for rows, step in zip(list(sent) + list(sent_pair), steps)]
    out_grad_a, qkv_grad_a = prog.temporal_back(sources, arriving, qkv_a, mixed_a, wout_a)
    pieces, pair_a = prog.temporal_weights(qkv_grad_a, normed_a, mixed_a, out_grad_a)
    total_a = reduce_blocks(place, pieces)
    sent, sums_a = prog.temporal_input(qkv_grad_a, win_a, start_a, along)
    back = [across(sent[k], (pair, k)) for pair, k in steps]
    low_total = total.astype(LOW)
    input_grad = [(ending[0], [low_total])]
    if split:
        input_grad.append((ending[1], [hop(low_total, "shard", 1)]))
    input_grad.append((homing, back))
    input_grad = prog.natural(input_grad)

    def in_grad(total):
        part = total[:, : 3 * piece].reshape(quarters, 3, piece, columns)
        return jnp.transpose(part, (3, 1, 0, 2)).reshape(columns, 3, group)

    def out_grad(total):
        return total[:, 3 * piece : 4 * piece].reshape(group, columns)

    in_total = jnp.stack([in_grad(total_a), in_grad(total_b)])
    out_total = jnp.stack([out_grad(total_a), out_grad(total_b)])
    fc_total = total_b[:, 4 * piece :].reshape(group, columns).astype(LOW)
    fc_total = [fc_total] + [hop(fc_total, "tensor", k) for k in range(1, ranks)]
    fc_total = ordered(fc_total, tensor).reshape(width, columns).T.astype(F32)

    sums = jnp.concatenate([sums_a, sums_b, sums_c])
    sums = sums[jnp.asarray([0, 2, 6, 1, 3, 7, 4, 5, 8, 9])].reshape(-1)
    pair_a = jnp.swapaxes(pair_a.reshape(3, ranks, group), 0, 1)
    pair_b = pair_b.reshape(quarters, 3, group)
    pair_b = ordered([pair_b[j] for j in range(quarters)], context)
    inner = jnp.stack([pair_a, pair_b], 1)[:, :, ::2]
    inner = ordered([inner[k] for k in range(ranks)], tensor).reshape(-1)
    outer = ordered([item.reshape(ranks, -1) for item in up_bias_grads], context, 1)
    outer = ordered([outer[k] for k in range(ranks)], tensor).reshape(-1)
    sums = jnp.concatenate([sums, inner, outer])
    ends = [10 * width, 10 * width + inner.size]
    sums = lax.psum(sums, ("shard", "context", "tensor"))
    along, inner, outer = jnp.split(sums, ends)
    along = lax.dynamic_slice_in_dim(along.reshape(10, width), shard * columns, columns, 1)
    inner = pick(inner.reshape((ranks,) + attention_bias.shape[:3] + (HEAD_DIM,)), tensor)
    part = HEAD_DIM // shards
    inner = lax.dynamic_slice_in_dim(inner, shard * part, part, 3)
    outer = pick(outer.reshape(ranks, -1, shards, hidden_bias.shape[1]), tensor)
    outer = pick(outer, shard, 1)
    rows_shape = clip_input.shape
    return (
        layer_out.reshape(rows_shape),
        input_grad.reshape(rows_shape),
        along[:3],
        along[3:6],
        in_total,
        inner,
        out_total,
        along[6:],
        fc_total,
        total_c[:, 0].reshape(hidden, columns).T,
        outer,
        total_c[:, 1].reshape(hidden, columns),
    )


def solution(mesh):
    rows = P(None, "shard", "tensor", "context", None)
    weights = (
        P(None, "shard"),
        P(None, "shard"),
        P(None, "shard", None, "tensor"),
        P(None, None, "tensor", "shard"),
        P(None, "tensor", "shard"),
        P(None, "shard"),
        P("shard", None),
        P("shard", "tensor"),
        P("tensor", "shard"),
        P("tensor", "shard"),
    )
    return jax.shard_map(
        body,
        mesh=mesh,
        in_specs=(rows, P(None, "shard")) + weights + (rows,),
        out_specs=(rows, rows) + weights,
        check_vma=False,
    )
```

time: 965 us -> 656 us (0.68)
  local copies, waits for them, and re-layouts: 241 us -> 58.6 us
  Pallas kernels: 0 us -> 134 us
  matrix products: 99.2 us -> 0 us
  waiting for transfers between devices: 282 us -> 198 us
  other arithmetic: 102 us -> 42.8 us
  between operations: 17.7 us -> 2.98 us
    pallas_call x0 -> x20, Pallas kernels: none -> 134 us  [call(): pl.pallas_call(body, out_shape=tuple(outs), in_specs=[pl.BlockSpec(memory...]
    dot_general x49 -> x0, matrix products: 91.8 us -> none  [dot(): return jnp.einsum(form, first, second, preferred_element_type=F32)]
    ppermute x164 -> x86, waiting for transfers between devices: 236 us -> 167 us  [hop(): return lax.ppermute(values, axis, [(i, i ^ step) for i in range(count)])]
    psum x1 -> x0, waiting for transfers between devices: 46 us -> none  [body(): lax.psum(scatter_columns(place, fc_grad.T).T, ('context', 'tensor'))]
    another operation x59 -> x16, local copies, waits for them, and re-layouts: 45.3 us -> 1.32 us  [the longest x1 0.69 us: body(): shift_a = biases[0].reshape(1, -1)]
    ppermute x164 -> x86, starting transfers between devices: 158 us -> 115 us  [hop(): return lax.ppermute(values, axis, [(i, i ^ step) for i in range(count)])]
    ppermute x0 -> x16, starting transfers between devices: none -> 38.5 us  [hop_pair(): return lax.ppermute(values, ('shard', 'tensor'), pairs)]
    slice x62 -> x32, local copies, waits for them, and re-layouts: 52.4 us -> 14.8 us  [the longest x15 9.18 us: packed(): parts.append(pick(labels, index)[lay.first:lay.first + lay.later])]
  transfers between devices with their start and end apart: 165 -> 102, of which waited for: 56 -> 41; matrix products, arithmetic and copies ran while one was open for 42% -> 14% of each run, Pallas kernels for 0% -> 13%
where the time goes in v2:
time: 656 us; the launch traced here: 650 us
  waiting for transfers between devices  198 us (30%)
  starting transfers between devices  153 us (23%)
  Pallas kernels  134 us (20%)
  blocking collectives  60.4 us (9%)
  local copies, waits for them, and re-layouts  58.6 us (9%)
  other arithmetic  42.8 us (7%)
    ppermute x86, waiting for transfers between devices, hop(): return lax.ppermute(values, axis, [(i, i ^ step) for i in range(count)])  167 us
    pallas_call x20, Pallas kernels, call(): pl.pallas_call(body, out_shape=tuple(outs), in_specs=[pl.BlockSpec(memory...  134 us
    ppermute x86, starting transfers between devices, hop(): return lax.ppermute(values, axis, [(i, i ^ step) for i in range(count)])  115 us
    psum x1, blocking collectives, body(): sums = lax.psum(sums, ('shard', 'context', 'tensor'))  60.4 us
    ppermute x16, starting transfers between devices, hop_pair(): return lax.ppermute(values, ('shard', 'tensor'), pairs)  38.5 us
    ppermute x16, waiting for transfers between devices, hop_pair(): return lax.ppermute(values, ('shard', 'tensor'), pairs)  30.8 us
    convert_element_type x9, other arithmetic, add(): return total.astype(LOW)  19.1 us
    unnamed x254, local copies, waits for them, and re-layouts  19.1 us
  transfers between devices with their start and end apart: 102, of which 41 were waited for; matrix products, arithmetic and copies ran while one was open for 14% of the time, Pallas kernels for 13%

profile of v2, /device:TPU:0, one launch (start us, length us, event | category | flops | bytes accessed | tf_op | source)
XLA Modules:
  0.0 649.9 jit_solution(18203773485339650594)
XLA Ops:
  41.5 9.6 %collective-permute-start.26 = (bf16[240,384]{1,0:T(8,128)(2,1)S(1)}, bf16[240,384]{1,0:T(8,128)(2,1)S(1)}, u32[]{:S(2)}, u32[]{:S(2)}) collective-permute-start(bf16[240,384]{1,0:T(8,128)(2,1)S(1)} %get-tuple-element.322), channel_id=1, source_target_pairs={{0,1},{1,0},{2,3},{3,2},{4,5},{5,4},{6,7},{7,6},{8,9},{9,8},{10,11... | collective-permute-start | bytes 552968 | tf_op jit(solution)/shard_map/ppermute | solution.py:23
  56.2 9.7 %collective-permute-done.27 = bf16[240,384]{1,0:T(8,128)(2,1)S(1)} collective-permute-done((bf16[240,384]{1,0:T(8,128)(2,1)S(1)}, bf16[240,384]{1,0:T(8,128)(2,1)S(1)}, u32[]{:S(2)}, u32[]{:S(2)}) %collective-permute-start.27) | collective-permute-done | bytes 184352 | tf_op jit(solution)/shard_map/ppermute | solution.py:23
  71.1 8.4 %collective-permute-done.10 = bf16[4,192,384]{2,1,0:T(8,128)(2,1)S(1)} collective-permute-done((bf16[4,192,384]{2,1,0:T(8,128)(2,1)S(1)}, bf16[4,192,384]{2,1,0:T(8,128)(2,1)S(1)}, u32[]{:S(2)}, u32[]{:S(2)}) %collective-permute-start.10) | collective-permute-done | bytes 589856 | tf_op jit(solution)/shard_map/ppermute | solution.py:23
  81.3 8.6 %collective-permute-start.15 = (bf16[2,2,384]{2,1,0:T(2,128)(2,1)S(1)}, bf16[2,2,384]{2,1,0:T(2,128)(2,1)S(1)}, u32[]{:S(2)}, u32[]{:S(2)}) collective-permute-start(bf16[2,2,384]{2,1,0:T(2,128)(2,1)S(1)} %get-tuple-element.334), channel_id=1, source_target_pairs={{0,1},{1,0},{2,3},{3,2},{4,5},{5,4},{6,7},{7,6},{8,9},{9,8},{10,11... | collective-permute-start | bytes 9224 | tf_op jit(solution)/shard_map/ppermute | solution.py:23
  93.3 11.1 %collective-permute-start.16 = (bf16[2,2,384]{2,1,0:T(2,128)(2,1)S(1)}, bf16[2,2,384]{2,1,0:T(2,128)(2,1)S(1)}, u32[]{:S(2)}, u32[]{:S(2)}) collective-permute-start(bf16[2,2,384]{2,1,0:T(2,128)(2,1)S(1)} %get-tuple-element.334), channel_id=1, source_target_pairs={{0,2},{1,3},{2,0},{3,1},{4,6},{5,7},{6,4},{7,5},{8,10},{9,11},{10,... | collective-permute-start | bytes 9224 | tf_op jit(solution)/shard_map/ppermute | solution.py:23
  162.5 10.9 %collective-permute-done.31.refs_12_ = bf16[4,240,768]{2,1,0:T(8,128)(2,1)} collective-permute-done((bf16[4,240,768]{2,1,0:T(8,128)(2,1)S(1)}, bf16[4,240,768]{2,1,0:T(8,128)(2,1)}, u32[]{:S(2)}, u32[]{:S(2)}) %collective-permute-start.31) | collective-permute-done | bytes 1474592 | tf_op jit(solution)/shard_map/ppermute | solution.py:23
  176.7 14.0 %shard_map.239 = (bf16[64,768]{1,0:T(8,128)(2,1)}, bf16[64,768]{1,0:T(8,128)(2,1)}, bf16[64,768]{1,0:T(8,128)(2,1)}, bf16[64,768]{1,0:T(8,128)(2,1)}, bf16[32,76...) custom-call(s32[3]{0:T(128)} %pad_add_fusion.2.scalars, ...), custom_call_target="tpu_custom_call" | custom-call | flops 1409286144 | bytes 13476864 | tf_op jit(solution)/shard_map/pallas_call | solution.py:173
  191.5 11.1 %collective-permute-start.22 = (bf16[32,768]{1,0:T(8,128)(2,1)}, bf16[32,768]{1,0:T(8,128)(2,1)S(1)}, u32[]{:S(2)}, u32[]{:S(2)}) collective-permute-start(bf16[32,768]{1,0:T(8,128)(2,1)} %get-tuple-element.122), channel_id=1, source_target_pairs={{0,17},{1,16},{2,19},{3,18},{16,1},{17,0},{18,3},{19,2},{4,21},{5,... | collective-permute-start | bytes 147464 | tf_op jit(solution)/shard_map/ppermute | solution.py:31
  227.2 7.8 %shard_map.241 = (f32[256,768]{1,0:T(8,128)}, bf16[256,768]{1,0:T(8,128)(2,1)}, bf16[256,768]{1,0:T(8,128)(2,1)}, bf16[256,576]{1,0:T(8,128)(2,1)}, bf16[256,576...) custom-call(s32[3]{0:T(128)} %pad_add_fusion.2.scalars, ...), custom_call_target="tpu_custom_call" | custom-call | flops 1207959552 | bytes 15768576 | tf_op jit(solution)/shard_map/pallas_call | solution.py:173
  237.8 8.0 %collective-permute-done.34.refs_2_ = bf16[256,576]{1,0:T(8,128)(2,1)S(1)} collective-permute-done((bf16[256,576]{1,0:T(8,128)(2,1)}, bf16[256,576]{1,0:T(8,128)(2,1)S(1)}, u32[]{:S(2)}, u32[]{:S(2)}) %collective-permute-start.34) | collective-permute-done | bytes 294944 | tf_op jit(solution)/shard_map/ppermute | solution.py:23
  252.7 7.8 %shard_map.242 = (bf16[256,192]{1,0:T(8,128)(2,1)}, bf16[256,192]{1,0:T(8,128)(2,1)}, bf16[256,192]{1,0:T(8,128)(2,1)}, bf16[256,192]{1,0:T(8,128)(2,1)}) custom-call(s32[3]{0:T(128)} %pad_add_fusion.2.scalars, bf16[256,576]{1,0:T(8,128)(2,1)} %get-tuple-element.126.refs_0_, bf16[256,576]{1,0:T(8,128)(2,1)} %copy-done.25, bf16[256,576]{1,0:T(8,128)(2,1)} %copy-done.26, ...), custom_call_target="tpu_custom_call" | custom-call | flops 251658240 | bytes 1572864 | tf_op jit(solution)/shard_map/pallas_call | solution.py:173
  273.0 7.6 %shard_map.245 = (f32[256,768]{1,0:T(8,128)}, f32[256,768]{1,0:T(8,128)}, bf16[2,768,768]{2,1,0:T(8,128)(2,1)}, f32[1,768]{1,0:T(1,128)}) custom-call(s32[3]{0:T(128)} %pad_add_fusion.2.scalars, bf16[256,768]{1,0:T(8,128)(2,1)} %get-tuple-element.138.normed_ref, bf16[256,768]{1,0:T(8,128)(2,1)} %get-tuple-element.139.grad_ref, ...), custom_call_target="tpu_custom_call" | custom-call | flops 1811939328 | bytes 7084032 | tf_op jit(solution)/shard_map/pallas_call | solution.py:173
  280.6 8.0 %shard_map.246 = (f32[256,768]{1,0:T(8,128)}, f32[256,768]{1,0:T(8,128)}, bf16[2,768,768]{2,1,0:T(8,128)(2,1)}, f32[1,768]{1,0:T(1,128)}) custom-call(s32[3]{0:T(128)} %pad_add_fusion.2.scalars, bf16[256,768]{1,0:T(8,128)(2,1)} %get-tuple-element.138.normed_ref, bf16[256,768]{1,0:T(8,128)(2,1)} %get-tuple-element.139.grad_ref, ...), custom_call_target="tpu_custom_call" | custom-call | flops 1811939328 | bytes 8656896 | tf_op jit(solution)/shard_map/pallas_call | solution.py:173
  288.5 8.0 %shard_map.247 = (f32[256,768]{1,0:T(8,128)}, f32[256,768]{1,0:T(8,128)}, bf16[2,768,768]{2,1,0:T(8,128)(2,1)}, f32[1,768]{1,0:T(1,128)}) custom-call(s32[3]{0:T(128)} %pad_add_fusion.2.scalars, bf16[256,768]{1,0:T(8,128)(2,1)} %get-tuple-element.138.normed_ref, bf16[256,768]{1,0:T(8,128)(2,1)} %get-tuple-element.139.grad_ref, ...), custom_call_target="tpu_custom_call" | custom-call | flops 1811939328 | bytes 8656896 | tf_op jit(solution)/shard_map/pallas_call | solution.py:173
  296.6 8.0 %shard_map.248 = (f32[256,768]{1,0:T(8,128)}, f32[256,768]{1,0:T(8,128)}, bf16[2,768,768]{2,1,0:T(8,128)(2,1)}, f32[1,768]{1,0:T(1,128)}) custom-call(s32[3]{0:T(128)} %pad_add_fusion.2.scalars, bf16[256,768]{1,0:T(8,128)(2,1)} %get-tuple-element.138.normed_ref, bf16[256,768]{1,0:T(8,128)(2,1)} %get-tuple-element.139.grad_ref, ...), custom_call_target="tpu_custom_call" | custom-call | flops 1811939328 | bytes 8656896 | tf_op jit(solution)/shard_map/pallas_call | solution.py:173
  318.5 12.5 %shard_map.251 = (bf16[256,576]{1,0:T(8,128)(2,1)}, bf16[256,576]{1,0:T(8,128)(2,1)}, bf16[256,576]{1,0:T(8,128)(2,1)}, bf16[256,576]{1,0:T(8,128)(2,1)}) custom-call(s32[3]{0:T(128)} %pad_add_fusion.2.scalars, bf16[256,576]{1,0:T(8,128)(2,1)} %get-tuple-element.126.refs_0_, bf16[256,576]{1,0:T(8,128)(2,1)} %copy-done.25, bf16[256,576]{1,0:T(8,128)(2,1)} %copy-done.26, ...), custom_call_target="tpu_custom_call" | custom-call | flops 629145600 | bytes 2752512 | tf_op jit(solution)/shard_map/pallas_call | solution.py:173
  333.3 9.2 %collective-permute-done.52.refs_2_ = bf16[256,576]{1,0:T(8,128)(2,1)S(1)} collective-permute-done((bf16[256,576]{1,0:T(8,128)(2,1)}, bf16[256,576]{1,0:T(8,128)(2,1)S(1)}, u32[]{:S(2)}, u32[]{:S(2)}) %collective-permute-start.52) | collective-permute-done | bytes 294944 | tf_op jit(solution)/shard_map/ppermute | solution.py:23
  375.3 12.1 %shard_map.253 = (bf16[256,768]{1,0:T(8,128)(2,1)}, bf16[256,2304]{1,0:T(8,128)(2,1)}) custom-call(s32[3]{0:T(128)} %pad_add_fusion.2.scalars, bf16[48,768]{1,0:T(8,128)(2,1)} %get-tuple-element.161.refs_0_, bf16[48,768]{1,0:T(8,128)(2,1)} %copy-done.54, bf16[48,768]{1,0:T(8,128)(2,1)} %copy-done.55, bf16[48,768]{1,0:T(8,128)(2,1)} %copy-done.56, ...), custom_call_target="tpu_custom_call" | custom-call | flops 805306368 | bytes 5242880 | tf_op jit(solution)/shard_map/pallas_call | solution.py:173
  419.7 60.4 %psum.7 = f32[13824]{0:T(1024)} all-reduce(f32[13824]{0:T(1024)S(1)} %pad_maximum_fusion.11), channel_id=1, replica_groups=mesh['shard'=2,'context'=4,'tensor'=4] {'shard','context','tensor'}, use_global_device_ids=true, to_apply=%region_3.4 | all-reduce | flops 13824 | bytes 110592 | tf_op jit(solution)/shard_map/psum | solution.py:1064
  539.7 9.2 %collective-permute-done.54.refs_3_ = bf16[256,768]{1,0:T(8,128)(2,1)S(1)} collective-permute-done((bf16[256,768]{1,0:T(8,128)(2,1)S(1)}, bf16[256,768]{1,0:T(8,128)(2,1)S(1)}, u32[]{:S(2)}, u32[]{:S(2)}) %collective-permute-start.54) | collective-permute-done | bytes 393248 | tf_op jit(solution)/shard_map/ppermute | solution.py:23
  560.7 8.1 %collective-permute-done.77 = bf16[192,384]{1,0:T(8,128)(2,1)S(1)} collective-permute-done((bf16[192,384]{1,0:T(8,128)(2,1)}, bf16[192,384]{1,0:T(8,128)(2,1)S(1)}, u32[]{:S(2)}, u32[]{:S(2)}) %collective-permute-start.77) | collective-permute-done | bytes 147488 | tf_op jit(solution)/shard_map/ppermute | solution.py:23
  592.1 17.5 %collective-permute-done.95 = bf16[2,4,192,384]{3,2,0,1:T(8,128)(2,1)S(1)} collective-permute-done((bf16[2,4,192,384]{3,2,0,1:T(8,128)(2,1)S(1)}, bf16[2,4,192,384]{3,2,0,1:T(8,128)(2,1)S(1)}, u32[]{:S(2)}, u32[]{:S(2)}) %collective-permute-start.95) | collective-permute-done | bytes 1179680 | tf_op jit(solution)/shard_map/ppermute | solution.py:23
  614.7 9.3 %collective-permute-done.96 = bf16[2,192,384]{2,1,0:T(8,128)(2,1)S(1)} collective-permute-done((bf16[2,192,384]{2,1,0:T(8,128)(2,1)S(1)}, bf16[2,192,384]{2,1,0:T(8,128)(2,1)S(1)}, u32[]{:S(2)}, u32[]{:S(2)}) %collective-permute-start.96) | collective-permute-done | bytes 294944 | tf_op jit(solution)/shard_map/ppermute | solution.py:23
  624.0 11.7 %collective-permute-done.97 = bf16[2,192,384]{2,1,0:T(8,128)(2,1)S(1)} collective-permute-done((bf16[2,192,384]{2,1,0:T(8,128)(2,1)S(1)}, bf16[2,192,384]{2,1,0:T(8,128)(2,1)S(1)}, u32[]{:S(2)}, u32[]{:S(2)}) %collective-permute-start.97) | collective-permute-done | bytes 294944 | tf_op jit(solution)/shard_map/ppermute | solution.py:23
  (767 shorter events, 358.5 us)
Async XLA Ops:
  2.8 48.3 %collective-permute-start.7 = (bf16[192,384]{1,0:T(8,128)(2,1)S(1)}, bf16[192,384]{1,0:T(8,128)(2,1)S(1)}, u32[]{:S(2)}, u32[]{:S(2)}) collective-permute-start(bf16[192,384]{1,0:T(8,128)(2,1)S(1)} %get-tuple-element.324), channel_id=1, source_target_pairs={{0,1},{1,0},{2,3},{3,2},{4,5},{5,4},{6,7},{7,6},{8,9},{9,8},{10,11... | collective-permute-start | bytes 442376 | tf_op jit(solution)/shard_map/ppermute | solution.py:23
  5.9 46.7 %collective-permute-start.8 = (bf16[192,384]{1,0:T(8,128)(2,1)S(1)}, bf16[192,384]{1,0:T(8,128)(2,1)S(1)}, u32[]{:S(2)}, u32[]{:S(2)}) collective-permute-start(bf16[192,384]{1,0:T(8,128)(2,1)S(1)} %get-tuple-element.324), channel_id=1, source_target_pairs={{0,2},{1,3},{2,0},{3,1},{4,6},{5,7},{6,4},{7,5},{8,10},{9,11},{10,... | collective-permute-start | bytes 442376 | tf_op jit(solution)/shard_map/ppermute | solution.py:23
  37.8 29.2 %collective-permute-start.43 = (bf16[2,4,192,384]{3,2,1,0:T(8,128)(2,1)}, bf16[2,4,192,384]{3,2,1,0:T(8,128)(2,1)}, u32[]{:S(2)}, u32[]{:S(2)}) collective-permute-start(bf16[2,4,192,384]{3,2,1,0:T(8,128)(2,1)} %pad_maximum_fusion.4), channel_id=1, source_target_pairs={{0,16},{16,0},{1,17},{17,1},{2,18},{18,2},{3,19},{19,3},{4,20},{20... | collective-permute-start | bytes 3538952 | tf_op jit(solution)/shard_map/ppermute | solution.py:23
  69.6 104.1 %collective-permute-start.44 = (bf16[2,4,192,768]{3,2,1,0:T(8,128)(2,1)}, bf16[2,4,192,768]{3,2,1,0:T(8,128)(2,1)}, u32[]{:S(2)}, u32[]{:S(2)}) collective-permute-start(bf16[2,4,192,768]{3,2,1,0:T(8,128)(2,1)} %pad_maximum_fusion), channel_id=1, source_target_pairs={{0,8},{4,12},{8,0},{12,4},{1,9},{5,13},{9,1},{13,5},{2,10},{6,14},... | collective-permute-start | bytes 7077896 | tf_op jit(solution)/shard_map/ppermute | solution.py:23
  79.7 69.7 %collective-permute-start.12 = (bf16[4,192,768]{2,1,0:T(8,128)(2,1)S(1)}, bf16[4,192,768]{2,1,0:T(8,128)(2,1)}, u32[]{:S(2)}, u32[]{:S(2)}) collective-permute-start(bf16[4,192,768]{2,1,0:T(8,128)(2,1)S(1)} %pad_maximum_fusion.3.refs_9_), channel_id=1, source_target_pairs={{0,8},{4,12},{8,0},{12,4},{1,9},{5,13},{9,1},{13,5},{2,10},{6,14},... | collective-permute-start | bytes 3538952 | tf_op jit(solution)/shard_map/ppermute | solution.py:23
  91.0 82.3 %collective-permute-start.31 = (bf16[4,240,768]{2,1,0:T(8,128)(2,1)S(1)}, bf16[4,240,768]{2,1,0:T(8,128)(2,1)}, u32[]{:S(2)}, u32[]{:S(2)}) collective-permute-start(bf16[4,240,768]{2,1,0:T(8,128)(2,1)S(1)} %pad_maximum_fusion.2.refs_10_), channel_id=1, source_target_pairs={{0,8},{4,12},{8,0},{12,4},{1,9},{5,13},{9,1},{13,5},{2,10},{6,14},... | collective-permute-start | bytes 4423688 | tf_op jit(solution)/shard_map/ppermute | solution.py:23
  111.3 50.5 %collective-permute-start.11 = (bf16[4,192,768]{2,1,0:T(8,128)(2,1)S(1)}, bf16[4,192,768]{2,1,0:T(8,128)(2,1)}, u32[]{:S(2)}, u32[]{:S(2)}) collective-permute-start(bf16[4,192,768]{2,1,0:T(8,128)(2,1)S(1)} %pad_maximum_fusion.3.refs_9_), channel_id=1, source_target_pairs={{0,4},{4,0},{8,12},{12,8},{1,5},{5,1},{9,13},{13,9},{2,6},{6,2},{1... | collective-permute-start | bytes 3538952 | tf_op jit(solution)/shard_map/ppermute | solution.py:23
  161.2 30.3 %collective-permute-start.30 = (bf16[4,240,768]{2,1,0:T(8,128)(2,1)S(1)}, bf16[4,240,768]{2,1,0:T(8,128)(2,1)}, u32[]{:S(2)}, u32[]{:S(2)}) collective-permute-start(bf16[4,240,768]{2,1,0:T(8,128)(2,1)S(1)} %pad_maximum_fusion.2.refs_10_), channel_id=1, source_target_pairs={{0,4},{4,0},{8,12},{12,8},{1,5},{5,1},{9,13},{13,9},{2,6},{6,2},{1... | collective-permute-start | bytes 4423688 | tf_op jit(solution)/shard_map/ppermute | solution.py:23
  161.9 111.1 %collective-permute-start.46 = (bf16[2,4,192,768]{3,2,1,0:T(8,128)(2,1)}, bf16[2,4,192,768]{3,2,1,0:T(8,128)(2,1)}, u32[]{:S(2)}, u32[]{:S(2)}) collective-permute-start(bf16[2,4,192,768]{3,2,1,0:T(8,128)(2,1)} %pad_maximum_fusion), channel_id=1, source_target_pairs={{0,4},{4,0},{8,12},{12,8},{1,5},{5,1},{9,13},{13,9},{2,6},{6,2},{1... | collective-permute-start | bytes 7077896 | tf_op jit(solution)/shard_map/ppermute | solution.py:23
  173.4 52.7 %collective-permute-start.32 = (bf16[4,240,768]{2,1,0:T(8,128)(2,1)}, bf16[4,240,768]{2,1,0:T(8,128)(2,1)S(1)}, u32[]{:S(2)}, u32[]{:S(2)}) collective-permute-start(bf16[4,240,768]{2,1,0:T(8,128)(2,1)} %collective-permute-done.31.refs_12_), channel_id=1, source_target_pairs={{0,4},{4,0},{8,12},{12,8},{1,5},{5,1},{9,13},{13,9},{2,6},{6,2},{1... | collective-permute-start | bytes 4423688 | tf_op jit(solution)/shard_map/ppermute | solution.py:23
  173.7 106.9 %collective-permute-start.45 = (bf16[2,4,192,768]{3,2,1,0:T(8,128)(2,1)}, bf16[2,4,192,768]{3,2,1,0:T(8,128)(2,1)}, u32[]{:S(2)}, u32[]{:S(2)}) collective-permute-start(bf16[2,4,192,768]{3,2,1,0:T(8,128)(2,1)} %collective-permute-done.44), channel_id=1, source_target_pairs={{0,4},{4,0},{8,12},{12,8},{1,5},{5,1},{9,13},{13,9},{2,6},{6,2},{1... | collective-permute-start | bytes 7077896 | tf_op jit(solution)/shard_map/ppermute | solution.py:23
  372.6 118.1 %collective-permute-start.93 = (bf16[2,4,192,768]{3,2,0,1:T(8,128)(2,1)}, bf16[2,4,192,768]{3,2,0,1:T(8,128)(2,1)}, u32[]{:S(2)}, u32[]{:S(2)}) collective-permute-start(bf16[2,4,192,768]{3,2,0,1:T(8,128)(2,1)} %copy.222), channel_id=1, source_target_pairs={{0,4},{4,0},{8,12},{12,8},{1,5},{5,1},{9,13},{13,9},{2,6},{6,2},{1... | collective-permute-start | bytes 7077896 | tf_op jit(solution)/shard_map/ppermute | solution.py:23
  372.6 30.0 %collective-permute-start.47 = (bf16[256,768]{1,0:T(8,128)(2,1)S(1)}, bf16[256,768]{1,0:T(8,128)(2,1)S(1)}, u32[]{:S(2)}, u32[]{:S(2)}) collective-permute-start(bf16[256,768]{1,0:T(8,128)(2,1)S(1)} %copy-done.19), channel_id=1, source_target_pairs={{0,16},{16,0},{1,17},{17,1},{2,18},{18,2},{3,19},{19,3},{4,20},{20... | collective-permute-start | bytes 1179656 | tf_op jit(solution)/shard_map/ppermute | solution.py:23
  400.1 80.0 %collective-permute-start.80 = (bf16[4,240,768]{2,1,0:T(8,128)(2,1)}, bf16[4,240,768]{2,1,0:T(8,128)(2,1)S(1)}, u32[]{:S(2)}, u32[]{:S(2)}) collective-permute-start(bf16[4,240,768]{2,1,0:T(8,128)(2,1)} %get-tuple-element.201), channel_id=1, source_target_pairs={{0,4},{4,0},{8,12},{12,8},{1,5},{5,1},{9,13},{13,9},{2,6},{6,2},{1... | collective-permute-start | bytes 4423688 | tf_op jit(solution)/shard_map/ppermute | solution.py:23
  400.5 115.0 %collective-permute-start.79 = (bf16[4,240,768]{2,1,0:T(8,128)(2,1)}, bf16[4,240,768]{2,1,0:T(8,128)(2,1)}, u32[]{:S(2)}, u32[]{:S(2)}) collective-permute-start(bf16[4,240,768]{2,1,0:T(8,128)(2,1)} %get-tuple-element.199), channel_id=1, source_target_pairs={{0,4},{4,0},{8,12},{12,8},{1,5},{5,1},{9,13},{13,9},{2,6},{6,2},{1... | collective-permute-start | bytes 4423688 | tf_op jit(solution)/shard_map/ppermute | solution.py:23
  408.5 75.4 %collective-permute-start.69 = (bf16[4,192,768]{2,1,0:T(8,128)(2,1)}, bf16[4,192,768]{2,1,0:T(8,128)(2,1)}, u32[]{:S(2)}, u32[]{:S(2)}) collective-permute-start(bf16[4,192,768]{2,1,0:T(8,128)(2,1)} %get-tuple-element.195), channel_id=1, source_target_pairs={{0,4},{4,0},{8,12},{12,8},{1,5},{5,1},{9,13},{13,9},{2,6},{6,2},{1... | collective-permute-start | bytes 3538952 | tf_op jit(solution)/shard_map/ppermute | solution.py:23
  418.1 65.8 %collective-permute-start.71 = (bf16[4,192,768]{2,1,0:T(8,128)(2,1)}, bf16[4,192,768]{2,1,0:T(8,128)(2,1)}, u32[]{:S(2)}, u32[]{:S(2)}) collective-permute-start(bf16[4,192,768]{2,1,0:T(8,128)(2,1)} %add_convert_fusion.6), channel_id=1, source_target_pairs={{0,8},{4,12},{8,0},{12,4},{1,9},{5,13},{9,1},{13,5},{2,10},{6,14},... | collective-permute-start | bytes 3538952 | tf_op jit(solution)/shard_map/ppermute | solution.py:23
  481.7 35.8 %collective-permute-start.81 = (bf16[4,240,768]{2,1,0:T(8,128)(2,1)}, bf16[4,240,768]{2,1,0:T(8,128)(2,1)}, u32[]{:S(2)}, u32[]{:S(2)}) collective-permute-start(bf16[4,240,768]{2,1,0:T(8,128)(2,1)} %add_convert_fusion.2), channel_id=1, source_target_pairs={{0,8},{4,12},{8,0},{12,4},{1,9},{5,13},{9,1},{13,5},{2,10},{6,14},... | collective-permute-start | bytes 4423688 | tf_op jit(solution)/shard_map/ppermute | solution.py:23
  505.8 72.2 %collective-permute-start.92 = (bf16[2,4,192,768]{3,2,0,1:T(8,128)(2,1)}, bf16[2,4,192,768]{3,2,0,1:T(8,128)(2,1)}, u32[]{:S(2)}, u32[]{:S(2)}) collective-permute-start(bf16[2,4,192,768]{3,2,0,1:T(8,128)(2,1)} %copy.220), channel_id=1, source_target_pairs={{0,4},{4,0},{8,12},{12,8},{1,5},{5,1},{9,13},{13,9},{2,6},{6,2},{1... | collective-permute-start | bytes 7077896 | tf_op jit(solution)/shard_map/ppermute | solution.py:23
  509.7 68.3 %collective-permute-start.94 = (bf16[2,4,192,768]{3,2,0,1:T(8,128)(2,1)}, bf16[2,4,192,768]{3,2,0,1:T(8,128)(2,1)}, u32[]{:S(2)}, u32[]{:S(2)}) collective-permute-start(bf16[2,4,192,768]{3,2,0,1:T(8,128)(2,1)} %fusion), channel_id=1, source_target_pairs={{0,8},{4,12},{8,0},{12,4},{1,9},{5,13},{9,1},{13,5},{2,10},{6,14},... | collective-permute-start | bytes 7077896 | tf_op jit(solution)/shard_map/ppermute | solution.py:23
  523.1 35.2 %collective-permute-start.82 = (bf16[4,240,384]{2,1,0:T(8,128)(2,1)}, bf16[4,240,384]{2,1,0:T(8,128)(2,1)}, u32[]{:S(2)}, u32[]{:S(2)}) collective-permute-start(bf16[4,240,384]{2,1,0:T(8,128)(2,1)} %slice.416), channel_id=1, source_target_pairs={{0,16},{16,0},{1,17},{17,1},{2,18},{18,2},{3,19},{19,3},{4,20},{20... | collective-permute-start | bytes 2211848 | tf_op jit(solution)/shard_map/ppermute | solution.py:23
  581.5 28.1 %collective-permute-start.95 = (bf16[2,4,192,384]{3,2,0,1:T(8,128)(2,1)S(1)}, bf16[2,4,192,384]{3,2,0,1:T(8,128)(2,1)S(1)}, u32[]{:S(2)}, u32[]{:S(2)}) collective-permute-start(bf16[2,4,192,384]{3,2,0,1:T(8,128)(2,1)S(1)} %slice.426), channel_id=1, source_target_pairs={{0,16},{16,0},{1,17},{17,1},{2,18},{18,2},{3,19},{19,3},{4,20},{20... | collective-permute-start | bytes 3538952 | tf_op jit(solution)/shard_map/ppermute | solution.py:23
  587.2 27.4 %collective-permute-start.90 = (bf16[192,384]{1,0:T(8,128)(2,1)S(1)}, bf16[192,384]{1,0:T(8,128)(2,1)S(1)}, u32[]{:S(2)}, u32[]{:S(2)}) collective-permute-start(bf16[192,384]{1,0:T(8,128)(2,1)S(1)} %bitcast.299), channel_id=1, source_target_pairs={{0,2},{1,3},{2,0},{3,1},{4,6},{5,7},{6,4},{7,5},{8,10},{9,11},{10,... | collective-permute-start | bytes 442376 | tf_op jit(solution)/shard_map/ppermute | solution.py:23
  587.4 49.4 %collective-permute-start.91 = (bf16[192,384]{1,0:T(8,128)(2,1)S(1)}, bf16[192,384]{1,0:T(8,128)(2,1)S(1)}, u32[]{:S(2)}, u32[]{:S(2)}) collective-permute-start(bf16[192,384]{1,0:T(8,128)(2,1)S(1)} %bitcast.300), channel_id=1, source_target_pairs={{0,3},{1,2},{2,1},{3,0},{4,7},{5,6},{6,5},{7,4},{8,11},{9,10},{10,... | collective-permute-start | bytes 442376 | tf_op jit(solution)/shard_map/ppermute | solution.py:23
  (200 other events, 2731.4 us)

commit v3 on v2

--- a/solution.py
+++ b/solution.py
@@ -65,11 +65,36 @@
     return lax.all_gather(part, "shard", axis=part.ndim - 1, tiled=True)
 
 
-def gather_blocks(place, mine, axis=0):
-    blocks = [mine] + [hop(mine, "tensor", k) for k in range(1, place.ranks)]
-    first = gather_columns(place, jnp.stack(blocks, axis))
-    second = hop(first, "context", 2)
-    return [first, hop(first, "context", 1), second, hop(second, "context", 1)]
+def tie(values, *others):
+    return lax.optimization_barrier((values,) + others)[0]
+
+
+class Gather:
+    def __init__(self, place, block, short=False):
+        self.place, self.short = place, short
+        mine = pick(block, place.context)
+        self.mine = jnp.stack([mine, pick(block, place.context ^ 2)]) if short else mine
+
+    def hops(self):
+        parts = [self.mine] + [hop(self.mine, "tensor", k) for k in range(1, self.place.ranks)]
+        self.blocks = jnp.stack(parts, 1 if self.short else 0)
+
+    def columns(self):
+        self.first = gather_columns(self.place, self.blocks)
+
+    def rows(self):
+        if not self.short:
+            self.second = hop(self.first, "context", 2)
+
+    def cores(self):
+        if self.short:
+            return [self.first, hop(self.first, "context", 1)]
+        return [
+            self.first,
+            hop(self.first, "context", 1),
+            self.second,
+            hop(self.second, "context", 1),
+        ]
 
 
 def add(*terms):
@@ -79,20 +104,51 @@
     return total.astype(LOW)
 
 
-def reduce_blocks(place, pieces, axis=0):
-    first = add(pieces[0], hop(pieces[1], "context", 1))
-    second = add(pieces[2], hop(pieces[3], "context", 1))
-    total = add(first, hop(second, "context", 2))
-    if place.paired:
-        half = total.shape[-1] // 2
-        mine = add(total[..., :half], hop(total[..., half:], "shard", 1))
-    else:
-        mine = lax.psum_scatter(total, "shard", scatter_dimension=total.ndim - 1, tiled=True)
-    block = lambda k: lax.index_in_dim(mine, k, axis, keepdims=False)
-    first = add(block(0), *[hop(block(k), "tensor", k) for k in range(1, place.ranks)])
-    second = hop(first, "context", 2)
-    parts = [first, hop(first, "context", 1), second, hop(second, "context", 1)]
-    return ordered(parts, place.context).astype(F32)
+class Reduce:
+    def __init__(self, place, pieces, short=False):
+        self.place, self.short = place, short
+        self.kept = [pieces[0], pieces[2]]
+        self.come = [hop(pieces[1], "context", 1), hop(pieces[3], "context", 1)]
+
+    def cores(self):
+        self.first, self.second = [add(*pair) for pair in zip(self.kept, self.come)]
+        return [self.first, self.second]
+
+    def rows(self):
+        if self.short:
+            self.total = jnp.stack([self.first, self.second])
+        else:
+            self.total = add(self.first, hop(self.second, "context", 2))
+        return [self.total]
+
+    def columns(self):
+        total = self.total
+        if self.place.paired:
+            half = total.shape[-1] // 2
+            self.mine = add(total[..., :half], hop(total[..., half:], "shard", 1))
+        else:
+            axis = total.ndim - 1
+            self.mine = lax.psum_scatter(total, "shard", scatter_dimension=axis, tiled=True)
+        return [self.mine]
+
+    def hops(self):
+        axis = 1 if self.short else 0
+        block = lambda k: lax.index_in_dim(self.mine, k, axis, keepdims=False)
+        parts = [hop(block(k), "tensor", k) for k in range(1, self.place.ranks)]
+        self.sum = add(block(0), *parts)
+        return [self.sum]
+
+    def finish(self):
+        total = self.sum
+        if self.short:
+            other = hop(total, "context", 2)
+            both = add(total, other[::-1])
+            far = hop(both, "context", 1)
+            parts = [both[0], far[0], both[1], far[1]]
+        else:
+            second = hop(total, "context", 2)
+            parts = [total, hop(total, "context", 1), second, hop(second, "context", 1)]
+        return ordered(parts, self.place.context).astype(F32)
 
 
 class Layout:
@@ -167,18 +223,24 @@
     return (targets[:, None] == sources[None]).astype(LOW)
 
 
-def call(body, outs, ins, scalars, flops=0, scratch=()):
+def call(body, outs, ins, scalars, flops=0, scratch=(), after=(), name=None):
+    given, count = body, len(ins)
+    if after:
+        body = lambda scalars, *refs: given(scalars, *refs[:count], *refs[count + len(after) :])
     moved = sum(item.size * item.dtype.itemsize for item in list(outs) + list(ins))
     spec = pl.BlockSpec(memory_space=pltpu.VMEM)
     return pl.pallas_call(
         body,
+        name=name,
         out_shape=tuple(outs),
-        in_specs=[pl.BlockSpec(memory_space=pltpu.SMEM)] + [spec] * len(ins),
+        in_specs=[pl.BlockSpec(memory_space=pltpu.SMEM)]
+        + [spec] * len(ins)
+        + [pl.BlockSpec(memory_space=pl.ANY)] * len(after),
         out_specs=(spec,) * len(outs),
         scratch_shapes=list(scratch),
         compiler_params=pltpu.CompilerParams(vmem_limit_bytes=VMEM_BYTES),
         cost_estimate=pl.CostEstimate(flops=flops, bytes_accessed=moved, transcendentals=0),
-    )(scalars, *ins)
+    )(scalars, *ins, *after)
 
 
 def shape(*dims, dtype=LOW):
@@ -264,8 +326,9 @@
             np.where(spot[:, None] == spot[None], 0, HIDE).astype(np.float32)
         )
 
-    def call(self, body, outs, ins, flops=0, scratch=()):
-        return call(body, outs, ins, self.scalars, flops, scratch)
+    def call(self, body, outs, ins, flops=0, scratch=(), after=()):
+        name = body.__qualname__.split(".")[1]
+        return call(body, outs, ins, self.scalars, flops, scratch, after, name)
 
 
     def send_rows(self, clips, cotangents, matrix, targets):
@@ -316,7 +379,7 @@
         )[0]
 
 
-    def temporal(self, blocks, pairs, keep, pieces, along, shift):
+    def temporal(self, blocks, pairs, keep, pieces, along, shift, wait=()):
         lay, width = self.layout, self.width
         rows, ranks = lay.place_rows, self.ranks
         wide = 3 * self.all_heads
@@ -389,7 +452,7 @@
         ]
         ins = list(blocks) + list(pairs) + [keep] + list(pieces) + [along, shift, self.same_place]
         flops = 2 * rows * width * (wide + self.all_heads) + 4 * rows * rows * self.all_heads
-        outs = self.call(body, outs, ins, flops)
+        outs = self.call(body, outs, ins, flops, after=wait)
         sent, outs = outs[:ranks], outs[ranks:]
         if split:
             sent_pair, outs = outs[:ranks], outs[ranks:]
@@ -397,7 +460,7 @@
             sent_pair = ()
         return sent, sent_pair, outs
 
-    def temporal_back(self, sources, matrix, qkv, mixed, wout):
+    def temporal_back(self, sources, matrix, qkv, mixed, wout, wait=()):
         lay, width = self.layout, self.width
         rows, wide = lay.place_rows, 3 * self.all_heads
 
@@ -436,16 +499,18 @@
         ins = list(sources) + [matrix, qkv, mixed, wout, self.same_place]
         flops = 2 * rows * width * self.all_heads + 10 * rows * rows * self.all_heads
         return self.call(
-            body, outs, ins, flops, scratch=[pltpu.VMEM((rows, self.all_heads), LOW)]
+            body, outs, ins, flops, [pltpu.VMEM((rows, self.all_heads), LOW)], wait
         )
 
-    def temporal_weights(self, qkv_grad, normed, mixed, out_grad):
+    def temporal_weights(self, qkv_grad, normed, mixed, out_grad, vectors):
         lay, width = self.layout, self.width
         rows, ranks = lay.place_rows, self.ranks
 
-        def body(scalars, grad_ref, normed_ref, mixed_ref, out_ref, *pieces):
-            pieces, sums = pieces[: self.quarters], pieces[self.quarters]
-            sums[...] = column_sum(grad_ref[...])
+        extra = vectors.shape[1]
+
+        def body(scalars, grad_ref, normed_ref, mixed_ref, out_ref, vectors_ref, *pieces):
+            for j in range(self.quarters):
+                pieces[j][:, 4 * self.piece :] = vectors_ref[...]
 
             def put(total, k, c):
                 for j in range(self.quarters):
@@ -467,18 +532,17 @@
 
             pl.run_scoped(inner, pltpu.VMEM((self.group, width), LOW))
 
-        outs = [shape(ranks, 4 * self.piece, width)] * self.quarters
-        outs += [shape(1, 3 * self.all_heads, dtype=F32)]
+        outs = [shape(ranks, 4 * self.piece + extra, width)] * self.quarters
         flops = 8 * rows * width * self.all_heads
-        outs = self.call(body, outs, [qkv_grad, normed, mixed, out_grad], flops)
-        return outs[:-1], outs[-1]
+        return self.call(body, outs, [qkv_grad, normed, mixed, out_grad, vectors], flops)
 
     def temporal_input(self, qkv_grad, win, start, along):
         lay, width = self.layout, self.width
         ranks = self.ranks
 
         def body(scalars, grad_ref, win_ref, start_ref, along_ref, *refs):
-            sent, sums = refs[:ranks], refs[ranks]
+            sent, sums, pair_sums = refs[:ranks], refs[ranks], refs[ranks + 1]
+            pair_sums[...] = column_sum(grad_ref[...])
             swap = swapper(scalars, self.place.paired)
             unit, inverse = unit_of(start_ref[...].astype(F32))
             grad = swap(nn(grad_ref[...], win_ref[...]))
@@ -489,12 +553,13 @@
                 sent[k][...] = back[k * lay.block : (k + 1) * lay.block].astype(LOW)
 
         outs = [shape(lay.block, width)] * ranks + [shape(2, width, dtype=F32)]
+        outs += [shape(1, 3 * self.all_heads, dtype=F32)]
         flops = 6 * lay.place_rows * width * self.all_heads
         outs = self.call(body, outs, [qkv_grad, win, start, along], flops)
-        return outs[:-1], outs[-1]
-
-
-    def spatial_in(self, sources, matrix, start, pieces, along, shift):
+        return outs[:-2], outs[-2], outs[-1]
+
+
+    def spatial_in(self, sources, matrix, start, pieces, along, shift, wait=()):
         lay, width = self.layout, self.width
         rows, ranks, quarters = lay.frame_rows, self.ranks, self.quarters
         piece, group = self.piece, self.group
@@ -543,7 +608,7 @@
         ]
         ins = list(sources) + [matrix, start] + list(pieces) + [along, shift]
         flops = 2 * rows * width * (3 * self.all_heads + width)
-        outs = self.call(body, outs, ins, flops)
+        outs = self.call(body, outs, ins, flops, after=wait)
         return outs[:3], outs[3 : 3 + quarters], outs[3 + quarters :]
 
     def windows(self, refs, n):
@@ -564,7 +629,7 @@
             old = ref[at].astype(F32)
             ref[at] = jnp.where(mask[part], values[part], old).astype(LOW)
 
-    def spatial(self, qkv):
+    def spatial(self, qkv, wait=()):
         lay, quarters, group = self.layout, self.quarters, self.group
 
         def body(scalars, *refs):
@@ -589,9 +654,9 @@
 
         outs = [shape(lay.frame_rows, group)] * quarters
         size = quarters * WINDOW
-        return self.call(body, outs, list(qkv), 4 * lay.units * size * size * group)
-
-    def spatial_back(self, qkv, grads):
+        return self.call(body, outs, list(qkv), 4 * lay.units * size * size * group, after=wait)
+
+    def spatial_back(self, qkv, grads, wait=()):
         lay, quarters, group = self.layout, self.quarters, self.group
 
         def body(scalars, *refs):
@@ -624,9 +689,9 @@
         outs = [shape(lay.frame_rows, 3 * group)] * quarters
         size = quarters * WINDOW
         flops = 10 * lay.units * size * size * group
-        return self.call(body, outs, list(qkv) + list(grads), flops)
-
-    def spatial_out(self, mixed, wout, after, grad, along):
+        return self.call(body, outs, list(qkv) + list(grads), flops, after=wait)
+
+    def spatial_out(self, mixed, wout, after, grad, along, wait=()):
         lay, width, group = self.layout, self.width, self.group
         rows, quarters = lay.frame_rows, self.quarters
 
@@ -645,46 +710,76 @@
 
         outs = [shape(rows, width, dtype=F32), shape(rows, width), shape(rows, width)]
         ins = list(mixed) + [wout, after, grad, along]
-        return self.call(body, outs, ins, 2 * rows * width * self.all_heads)
-
-    def feed_forward(self, normed, grad, weights, shift, totals):
+        return self.call(body, outs, ins, 2 * rows * width * self.all_heads, after=wait)
+
+    def feed_forward(self, normed, grad, ups, downs, shifts, totals):
         lay, width = self.layout, self.width
-        rows = lay.frame_rows
-        hidden = weights.shape[1]
+        rows, count = lay.frame_rows, len(ups)
+        hidden = ups[0].shape[0]
         tile = 256
-
-        def body(scalars, normed_ref, grad_ref, weight_ref, shift_ref, *refs):
-            out_ref, back_ref, weight_grad, sums = refs[-4:]
-            if totals is None:
-                out_ref[...] = jnp.zeros_like(out_ref)
-                back_ref[...] = jnp.zeros_like(back_ref)
-            else:
-                out_ref[...] = refs[0][...]
-                back_ref[...] = refs[1][...]
-
-            @pl.loop(0, hidden // tile)
-            def _(n):
-                at = pl.ds(pl.multiple_of(n * tile, tile), tile)
-                up, down = weight_ref[0, at], weight_ref[1, at]
-                values = nt(normed_ref[...], up) + shift_ref[:, at]
+        steps = hidden // tile
+        at = lambda n, item: jnp.clip(n - item * steps, 0, steps - 1)
+
+        def body(scalars, normed_ref, grad_ref, *refs):
+            refs = list(refs)
+            take = lambda n: [refs.pop(0) for _ in range(n)]
+            up_refs, down_refs, shift_refs = take(count), take(count), take(count)
+            before = take(2 if totals else 0)
+            out_ref, back_ref = take(2)
+            up_grads, down_grads, sums = take(count), take(count), take(count)
+            n = pl.program_id(0)
+
+            @pl.when(n == 0)
+            def _():
+                out_ref[...] = before[0][...] if totals else jnp.zeros_like(out_ref)
+                back_ref[...] = before[1][...] if totals else jnp.zeros_like(back_ref)
+
+            def work(item):
+                up, down = up_refs[item][...], down_refs[item][0]
+                values = nt(normed_ref[...], up) + shift_refs[item][...]
                 half = 0.5 * (1.0 + lax.erf(values * SQRT_HALF))
                 active = (values * half).astype(LOW)
                 slope = half + values * jnp.exp(-0.5 * values * values) * INV_ROOT_TAU
                 out_ref[...] += nn(active, down)
-                weight_grad[1, at] = tn(active, grad_ref[...]).astype(LOW)
+                down_grads[item][...] = tn(active, grad_ref[...]).astype(LOW)
                 hidden_grad = (nt(grad_ref[...], down) * slope).astype(LOW)
-                weight_grad[0, at] = tn(hidden_grad, normed_ref[...]).astype(LOW)
+                up_grads[item][...] = tn(hidden_grad, normed_ref[...]).astype(LOW)
                 back_ref[...] += nn(hidden_grad, up)
-                sums[:, at] = column_sum(hidden_grad)
-
-        outs = [
-            shape(rows, width, dtype=F32),
-            shape(rows, width, dtype=F32),
-            shape(2, hidden, width),
-            shape(1, hidden, dtype=F32),
+                sums[item][...] = column_sum(hidden_grad)
+
+            for item in range(count):
+                pl.when(n // steps == item)(lambda item=item: work(item))
+
+        whole = pl.BlockSpec((rows, width), lambda n: (0, 0))
+        up_specs = [pl.BlockSpec((tile, width), lambda n, i=i: (at(n, i), 0)) for i in range(count)]
+        down_specs = [
+            pl.BlockSpec((1, tile, width), lambda n, i=i, k=k: (k, at(n, i), 0))
+            for i, (_, k) in enumerate(downs)
         ]
-        ins = [normed, grad, weights, shift] + ([] if totals is None else list(totals))
-        return self.call(body, outs, ins, 12 * rows * width * hidden)
+        line_specs = [pl.BlockSpec((1, tile), lambda n, i=i: (0, at(n, i))) for i in range(count)]
+        outs = [shape(rows, width, dtype=F32)] * 2
+        outs += [shape(hidden, width)] * (2 * count) + [shape(1, hidden, dtype=F32)] * count
+        ins = [normed, grad] + list(ups) + [item for item, _ in downs] + list(shifts)
+        ins += list(totals or ())
+        got = pl.pallas_call(
+            body,
+            name="feed_forward",
+            grid=(count * steps,),
+            out_shape=tuple(outs),
+            in_specs=[pl.BlockSpec(memory_space=pltpu.SMEM), whole, whole]
+            + up_specs
+            + down_specs
+            + line_specs
+            + [whole] * (2 if totals else 0),
+            out_specs=tuple([whole, whole] + up_specs + up_specs + line_specs),
+            compiler_params=pltpu.CompilerParams(vmem_limit_bytes=VMEM_BYTES),
+            cost_estimate=pl.CostEstimate(
+                flops=12 * rows * width * hidden * count,
+                bytes_accessed=2 * sum(item.size * 2 for item in ins),
+                transcendentals=0,
+            ),
+        )(self.scalars, *ins)
+        return got[:2], got[2 : 2 + count], got[2 + count : 2 + 2 * count], got[2 + 2 * count :]
 
     def feed_forward_back(self, after, out, back, grad, mixed, wout, along):
         lay, width, group = self.layout, self.width, self.group
@@ -723,7 +818,7 @@
         outs = self.call(body, outs, ins, 4 * rows * width * self.all_heads)
         return outs[:4], outs[4:]
 
-    def spatial_input(self, qkv_grads, win, after, total, along, fc, matrix):
+    def spatial_input(self, qkv_grads, win, after, total, along, fc, matrix, wait=()):
         lay, width, group = self.layout, self.width, self.group
         rows, quarters, ranks = lay.frame_rows, self.quarters, self.ranks
         split = lay.split > 0
@@ -765,7 +860,7 @@
         outs += [shape(lay.sent, width)] * ranks
         outs += [shape(lay.sent_pair, width)] * (ranks if split else 0)
         ins = list(qkv_grads) + [win, after, total, along, fc, matrix]
-        outs = self.call(body, outs, ins, 2 * rows * width * (3 * self.all_heads + width))
+        outs = self.call(body, outs, ins, 2 * rows * width * (3 * self.all_heads + width), after=wait)
         return outs[:3], outs[3 : 3 + ranks], outs[3 + ranks :]
 
     def spatial_weights(self, qkv_grads, normed, wout_grad, low, temporal):
@@ -860,6 +955,7 @@
     columns = attention_in.shape[1]
     width = columns * shards
     group = attention_in.shape[3]
+    heads = group // HEAD_DIM
     hidden = hidden_in.shape[1]
     piece = group // quarters
     split = lay.split > 0
@@ -889,24 +985,34 @@
     up_shift = jnp.transpose(up_shift, (1, 2, 0, 3)).reshape(ranks, quarters, -1)
     up_shift = [pick(up_shift, context ^ j, 1).reshape(1, -1) for j in range(quarters)]
 
-    def quarter_in(weight):
-        part = pick(weight.reshape(columns, 3, quarters, piece), context, 2)
-        return jnp.transpose(part, (1, 2, 0)).reshape(3 * piece, columns)
-
-    def quarter(rows):
-        return pick(rows.reshape(quarters, -1, rows.shape[-1]), context)
-
-    fc_part = lax.dynamic_slice_in_dim(
-        temporal_fc, (tensor * quarters + context) * piece, piece, 1
-    ).T
-    block_a = jnp.concatenate([quarter_in(attention_in[0]), quarter(attention_out[0])])
-    block_b = jnp.concatenate([quarter_in(attention_in[1]), quarter(attention_out[1]), fc_part])
-    up_part = pick(hidden_in.reshape(columns, quarters, -1), context, 1).T
-    block_c = jnp.stack([up_part, quarter(hidden_out)])
-    pieces_a = gather_blocks(place, block_a)
-    pieces_b = gather_blocks(place, block_b)
-    pieces_c = gather_blocks(place, block_c, 1)
-    pieces_c = [item.reshape(2, -1, width) for item in pieces_c]
+    def in_block(weight):
+        block = weight.reshape(columns, 3, quarters, piece)
+        return jnp.transpose(block, (2, 1, 3, 0)).reshape(quarters, 3 * piece, columns)
+
+    def in_quarters(rows):
+        return rows.reshape(quarters, -1, rows.shape[-1])
+
+    fc_block = lax.dynamic_slice_in_dim(temporal_fc, tensor * group, group, 1).T
+    fc_block = in_quarters(fc_block)
+    block_a = jnp.concatenate([in_block(attention_in[0]), in_quarters(attention_out[0])], 1)
+    block_b = jnp.concatenate(
+        [in_block(attention_in[1]), in_quarters(attention_out[1]), fc_block], 1
+    )
+    block_up = jnp.transpose(hidden_in.reshape(columns, quarters, -1), (1, 2, 0))
+    gather_a, gather_b = Gather(place, block_a), Gather(place, block_b)
+    gather_down = Gather(place, in_quarters(hidden_out), True)
+    gather_up = Gather(place, block_up)
+    gather_a.hops()
+    gather_b.mine = tie(gather_b.mine, gather_a.blocks)
+    gather_b.hops()
+    gather_down.mine = tie(gather_down.mine, gather_b.blocks)
+    gather_down.hops()
+    gather_up.mine = tie(gather_up.mine, gather_down.blocks)
+    gather_up.hops()
+    for item in (gather_a, gather_b, gather_down, gather_up):
+        item.columns()
+        item.rows()
+    pieces_a, pieces_b = gather_a.cores(), gather_b.cores()
 
     steps = [(0, k) for k in range(ranks)] + [(1, k) for k in range(ranks if split else 0)]
 
@@ -984,7 +1090,7 @@
     grad = prog.frames_of(cotangents, other_grads, starting)
 
     sent, sent_pair, kept = prog.temporal(
-        blocks[:ranks], blocks[ranks:], keep, pieces_a, along, shift_a
+        blocks[:ranks], blocks[ranks:], keep, pieces_a, along, shift_a, [gather_b.first]
     )
     normed_a, start_a, qkv_a, mixed_a, win_a, wout_a = kept
     sources = [across(rows, step) for rows, step in zip(list(sent) + list(sent_pair), steps)]
@@ -992,44 +1098,90 @@
     def to_groups(parts):
         return [parts[0]] + [hop(parts[j], "context", j) for j in range(1, quarters)]
 
-    kept, qkv, weights_b = prog.spatial_in(sources, returning, start, pieces_b, along, shift_b)
+    kept, qkv, weights_b = prog.spatial_in(
+        sources, returning, start, pieces_b, along, shift_b, [gather_down.first, gather_up.blocks]
+    )
     after_a, temporal, normed_b = kept
     win_b, wout_b, fc = weights_b
     qkv = to_groups(qkv)
-    mixed = to_groups(prog.spatial(qkv))
+    mixed = to_groups(prog.spatial(qkv, [gather_up.first]))
+    downs, ups = gather_down.cores(), gather_up.cores()
+    downs = [item.reshape(2, -1, width) for item in downs]
+    ups = [item.reshape(-1, width) for item in ups]
     after_b, normed_c, low = prog.spatial_out(mixed, wout_b, after_a, grad, along)
 
-    totals, piece_grads, up_bias_grads = None, [None] * quarters, [None] * quarters
-    for j in (1, 3, 0, 2):
-        out, back, piece_grads[j], up_bias_grads[j] = prog.feed_forward(
-            normed_c, low, pieces_c[j], up_shift[j], totals
+    totals = None
+    up_grads, down_grads, up_bias_grads = ([None] * quarters for _ in range(3))
+    for pair in ((1, 3), (0, 2)):
+        totals, *got = prog.feed_forward(
+            normed_c,
+            low,
+            [ups[j] for j in pair],
+            [(downs[j % 2], j // 2) for j in pair],
+            [up_shift[j] for j in pair],
+            totals,
         )
-        totals = (out, back)
+        for index, j in enumerate(pair):
+            up_grads[j] = got[0][index].reshape(ranks, -1, width)
+            down_grads[j] = got[1][index].reshape(ranks, -1, width)
+            up_bias_grads[j] = got[2][index]
+    reduce_down, reduce_up = Reduce(place, down_grads, True), Reduce(place, up_grads)
     kept, mixed_grads = prog.feed_forward_back(
         after_b, totals[0], totals[1], grad, mixed, wout_b, along
     )
     layer_rows, total, sums_c, wout_grad = kept
-    total_c = reduce_blocks(
-        place, [item.reshape(2, ranks, -1, width) for item in piece_grads], 1
-    )
+    wait = reduce_down.cores() + reduce_up.cores()
+
+    mixed_grads = to_groups(mixed_grads)
+    qkv_grads = to_groups(prog.spatial_back(qkv, mixed_grads, wait))
+    reduce_down.rows()
+    wait = reduce_down.columns() + reduce_up.rows()
     layer_out = [(ending[0], [layer_rows])]
     if split:
         layer_out.append((ending[1], [hop(layer_rows, "shard", 1)]))
     layer_out = prog.natural(layer_out)
-
-    qkv_grads = to_groups(prog.spatial_back(qkv, to_groups(mixed_grads)))
     kept, sent, sent_pair = prog.spatial_input(
-        qkv_grads, win_b, after_a, total, along, fc, leaving
+        qkv_grads, win_b, after_a, total, along, fc, leaving, wait
     )
     total, low_fc, sums_b = kept
     pieces, pair_b = prog.spatial_weights(qkv_grads, normed_b, wout_grad, low_fc, temporal)
-    total_b = reduce_blocks(place, pieces)
+    reduce_b = Reduce(place, pieces, True)
+    wait = reduce_b.cores() + reduce_up.columns()
     sources = [across(rows, step) for rows, step in zip(list(sent) + list(sent_pair), steps)]
-    out_grad_a, qkv_grad_a = prog.temporal_back(sources, arriving, qkv_a, mixed_a, wout_a)
-    pieces, pair_a = prog.temporal_weights(qkv_grad_a, normed_a, mixed_a, out_grad_a)
-    total_a = reduce_blocks(place, pieces)
-    sent, sums_a = prog.temporal_input(qkv_grad_a, win_a, start_a, along)
+    out_grad_a, qkv_grad_a = prog.temporal_back(
+        sources, arriving, qkv_a, mixed_a, wout_a, wait
+    )
+    reduce_down.hops()
+    reduce_b.rows()
+    reduce_b.columns()
+    sent, sums_a, pair_a = prog.temporal_input(qkv_grad_a, win_a, start_a, along)
     back = [across(sent[k], (pair, k)) for pair, k in steps]
+
+    sums = jnp.concatenate([sums_a, sums_b, sums_c])
+    sums = jnp.stack([sums[k] for k in (0, 2, 6, 1, 3, 7, 4, 5, 8, 9)])
+    pair_a = jnp.swapaxes(pair_a.reshape(3, ranks, group), 0, 1)
+    pair_b = ordered([pair_b.reshape(quarters, 3, group)[j] for j in range(quarters)], context)
+    inner = jnp.stack([pair_a, pair_b], 1)[:, :, ::2]
+    inner = inner.reshape(ranks, 4 * heads, shards, HEAD_DIM // shards)
+    inner = jnp.swapaxes(inner, 1, 2).reshape(ranks, 1, width)
+    outer = ordered([item.reshape(ranks, -1) for item in up_bias_grads], context, 1)
+    outer = outer.reshape(ranks, -1, shards, hidden_bias.shape[1])
+    outer = jnp.swapaxes(outer, 1, 2).reshape(ranks, 1, width)
+    vectors = [jnp.broadcast_to(sums, (ranks,) + sums.shape), inner, outer]
+    vectors = jnp.concatenate(vectors, 1)
+    if place.paired:
+        flipped = jnp.concatenate([vectors[..., columns:], vectors[..., :columns]], -1)
+        vectors = jnp.where(shard == 0, vectors, flipped)
+    vectors = jnp.pad(vectors, ((0, 0), (0, 16 - vectors.shape[1]), (0, 0))).astype(LOW)
+    pieces = prog.temporal_weights(qkv_grad_a, normed_a, mixed_a, out_grad_a, vectors)
+    reduce_a = Reduce(place, pieces)
+    reduce_up.hops()
+    reduce_b.hops()
+    for stage in ("cores", "rows", "columns", "hops"):
+        getattr(reduce_a, stage)()
+    total_up, total_down, total_b, total_a = (
+        item.finish() for item in (reduce_up, reduce_down, reduce_b, reduce_a)
+    )
     low_total = total.astype(LOW)
     input_grad = [(ending[0], [low_total])]
     if split:
@@ -1050,25 +1202,8 @@
     fc_total = [fc_total] + [hop(fc_total, "tensor", k) for k in range(1, ranks)]
     fc_total = ordered(fc_total, tensor).reshape(width, columns).T.astype(F32)
 
-    sums = jnp.concatenate([sums_a, sums_b, sums_c])
-    sums = sums[jnp.asarray([0, 2, 6, 1, 3, 7, 4, 5, 8, 9])].reshape(-1)
-    pair_a = jnp.swapaxes(pair_a.reshape(3, ranks, group), 0, 1)
-    pair_b = pair_b.reshape(quarters, 3, group)
-    pair_b = ordered([pair_b[j] for j in range(quarters)], context)
-    inner = jnp.stack([pair_a, pair_b], 1)[:, :, ::2]
-    inner = ordered([inner[k] for k in range(ranks)], tensor).reshape(-1)
-    outer = ordered([item.reshape(ranks, -1) for item in up_bias_grads], context, 1)
-    outer = ordered([outer[k] for k in range(ranks)], tensor).reshape(-1)
-    sums = jnp.concatenate([sums, inner, outer])
-    ends = [10 * width, 10 * width + inner.size]
-    sums = lax.psum(sums, ("shard", "context", "tensor"))
-    along, inner, outer = jnp.split(sums, ends)
-    along = lax.dynamic_slice_in_dim(along.reshape(10, width), shard * columns, columns, 1)
-    inner = pick(inner.reshape((ranks,) + attention_bias.shape[:3] + (HEAD_DIM,)), tensor)
-    part = HEAD_DIM // shards
-    inner = lax.dynamic_slice_in_dim(inner, shard * part, part, 3)
-    outer = pick(outer.reshape(ranks, -1, shards, hidden_bias.shape[1]), tensor)
-    outer = pick(outer, shard, 1)
+    vectors = total_a[0, 4 * piece :]
+    along, inner, outer = vectors[:10], vectors[10], vectors[11]
     rows_shape = clip_input.shape
     return (
         layer_out.reshape(rows_shape),
@@ -1076,13 +1211,13 @@
         along[:3],
         along[3:6],
         in_total,
-        inner,
+        inner.reshape(attention_bias.shape),
         out_total,
         along[6:],
         fc_total,
-        total_c[:, 0].reshape(hidden, columns).T,
-        outer,
-        total_c[:, 1].reshape(hidden, columns),
+        total_up.reshape(hidden, columns).T,
+        outer.reshape(hidden_bias.shape),
+        total_down.reshape(hidden, columns),
     )
 
 

time: 656 us -> 580 us (0.88)
  blocking collectives: 60.4 us -> 0 us
  starting transfers between devices: 153 us -> 137 us
  waiting for transfers between devices: 198 us -> 186 us
  other arithmetic: 42.8 us -> 53.3 us
  Pallas kernels: 134 us -> 126 us
    psum x1 -> x0, blocking collectives: 60.4 us -> none  [body(): sums = lax.psum(sums, ('shard', 'context', 'tensor'))]
    ppermute x16, waiting for transfers between devices: 30.8 us -> 12.2 us  [hop_pair(): return lax.ppermute(values, ('shard', 'tensor'), pairs)]
    ppermute x16, starting transfers between devices: 38.5 us -> 25.6 us  [hop_pair(): return lax.ppermute(values, ('shard', 'tensor'), pairs)]
    pallas_call x20 -> x18, Pallas kernels: 134 us -> 126 us  [the longest x16 102 us: call(): pl.pallas_call(body, name=name, out_shape=tuple(outs), in_specs=[pl.Block...]
    ppermute x86 -> x97, waiting for transfers between devices: 167 us -> 174 us  [hop(): return lax.ppermute(values, axis, [(i, i ^ step) for i in range(count)])]
    ppermute x86 -> x97, starting transfers between devices: 115 us -> 112 us  [hop(): return lax.ppermute(values, axis, [(i, i ^ step) for i in range(count)])]
    unnamed x254 -> x392, local copies, waits for them, and re-layouts: 19.1 us -> 17 us
    convert_element_type x9 -> x16, other arithmetic: 19.1 us -> 18.1 us  [add(): return total.astype(LOW)]
  transfers between devices with their start and end apart: 102 -> 113, of which waited for: 41 -> 39; matrix products, arithmetic and copies ran while one was open for 14% -> 18% of each run, Pallas kernels for 13% -> 20%
where the time goes in v3:
time: 580 us; the launch traced here: 571 us
  waiting for transfers between devices  186 us (32%)
  starting transfers between devices  137 us (24%)
  Pallas kernels  126 us (22%)
  local copies, waits for them, and re-layouts  64.7 us (11%)
  other arithmetic  53.3 us (9%)
    ppermute x97, waiting for transfers between devices, hop(): return lax.ppermute(values, axis, [(i, i ^ step) for i in range(count)])  174 us
    ppermute x97, starting transfers between devices, hop(): return lax.ppermute(values, axis, [(i, i ^ step) for i in range(count)])  112 us
    pallas_call x16, Pallas kernels, call(): pl.pallas_call(body, name=name, out_shape=tuple(outs), in_specs=[pl.Block...  102 us
    ppermute x16, starting transfers between devices, hop_pair(): return lax.ppermute(values, ('shard', 'tensor'), pairs)  25.6 us
    pallas_call x2, Pallas kernels, feed_forward(): pl.pallas_call(body, name='feed_forward', grid=(count * steps,), out_shap...  24.3 us
    convert_element_type x16, other arithmetic, add(): return total.astype(LOW)  18.1 us
    unnamed x392, local copies, waits for them, and re-layouts  17 us
    slice x15, local copies, waits for them, and re-layouts, packed(): parts.append(pick(labels, index)[lay.first:lay.first + lay.later])  12.7 us
  transfers between devices with their start and end apart: 113, of which 39 were waited for; matrix products, arithmetic and copies ran while one was open for 18% of the time, Pallas kernels for 20%

profile of v3, /device:TPU:0, one launch (start us, length us, event | category | flops | bytes accessed | tf_op | source)
XLA Modules:
  0.0 571.4 jit_solution(5402255462930910657)
XLA Ops:
  56.6 9.4 %collective-permute-done.19 = bf16[240,384]{1,0:T(8,128)(2,1)S(1)} collective-permute-done((bf16[240,384]{1,0:T(8,128)(2,1)S(1)}, bf16[240,384]{1,0:T(8,128)(2,1)S(1)}, u32[]{:S(2)}, u32[]{:S(2)}) %collective-permute-start.19) | collective-permute-done | bytes 184352 | tf_op jit(solution)/shard_map/ppermute | solution.py:23
  73.3 6.7 %collective-permute-done.33 = bf16[2,192,384]{2,1,0:T(8,128)(2,1)S(1)} collective-permute-done((bf16[2,192,384]{2,1,0:T(8,128)(2,1)S(1)}, bf16[2,192,384]{2,1,0:T(8,128)(2,1)S(1)}, u32[]{:S(2)}, u32[]{:S(2)}) %collective-permute-start.33) | collective-permute-done | bytes 294944 | tf_op jit(solution)/shard_map/ppermute | solution.py:23
  80.8 14.4 %collective-permute-done.34 = bf16[2,192,384]{2,1,0:T(8,128)(2,1)S(1)} collective-permute-done((bf16[2,192,384]{2,1,0:T(8,128)(2,1)S(1)}, bf16[2,192,384]{2,1,0:T(8,128)(2,1)S(1)}, u32[]{:S(2)}, u32[]{:S(2)}) %collective-permute-start.34) | collective-permute-done | bytes 294944 | tf_op jit(solution)/shard_map/ppermute | solution.py:23
  144.1 15.0 %collective-permute-done.43 = bf16[4,192,384]{2,1,0:T(8,128)(2,1)} collective-permute-done((bf16[4,192,384]{2,1,0:T(8,128)(2,1)S(1)}, bf16[4,192,384]{2,1,0:T(8,128)(2,1)}, u32[]{:S(2)}, u32[]{:S(2)}) %collective-permute-start.43) | collective-permute-done | bytes 589856 | tf_op jit(solution)/shard_map/ppermute | solution.py:23
  170.7 14.5 %temporal.1 = (bf16[64,768]{1,0:T(8,128)(2,1)}, bf16[64,768]{1,0:T(8,128)(2,1)}, bf16[64,768]{1,0:T(8,128)(2,1)}, bf16[64,768]{1,0:T(8,128)(2,1)}, bf16[32,768]{...) custom-call(s32[3]{0:T(128)} %pad_add_fusion.2.scalars, ...), custom_call_target="tpu_custom_call" | custom-call | flops 1409286144 | bytes 13476864 | tf_op jit(solution)/shard_map/temporal/pallas_call | solution.py:232
  201.6 7.8 %collective-permute-done.23.refs_2_ = bf16[64,768]{1,0:T(8,128)(2,1)S(1)} collective-permute-done((bf16[64,768]{1,0:T(8,128)(2,1)}, bf16[64,768]{1,0:T(8,128)(2,1)S(1)}, u32[]{:S(2)}, u32[]{:S(2)}) %collective-permute-start.23) | collective-permute-done | bytes 98336 | tf_op jit(solution)/shard_map/ppermute | solution.py:23
  217.2 7.9 %spatial_in.1 = (f32[256,768]{1,0:T(8,128)}, bf16[256,768]{1,0:T(8,128)(2,1)}, bf16[256,768]{1,0:T(8,128)(2,1)}, bf16[256,576]{1,0:T(8,128)(2,1)}, bf16[256,576]...) custom-call(s32[3]{0:T(128)} %pad_add_fusion.2.scalars, ...), custom_call_target="tpu_custom_call" | custom-call | flops 1207959552 | bytes 15768576 | tf_op jit(solution)/shard_map/spatial_in/pallas_call | solution.py:232
  228.4 7.6 %collective-permute-done.41.refs_2_ = bf16[256,576]{1,0:T(8,128)(2,1)S(1)} collective-permute-done((bf16[256,576]{1,0:T(8,128)(2,1)}, bf16[256,576]{1,0:T(8,128)(2,1)S(1)}, u32[]{:S(2)}, u32[]{:S(2)}) %collective-permute-start.41) | collective-permute-done | bytes 294944 | tf_op jit(solution)/shard_map/ppermute | solution.py:23
  242.9 7.6 %spatial.1 = (bf16[256,192]{1,0:T(8,128)(2,1)}, bf16[256,192]{1,0:T(8,128)(2,1)}, bf16[256,192]{1,0:T(8,128)(2,1)}, bf16[256,192]{1,0:T(8,128)(2,1)}) custom-call(s32[3]{0:T(128)} %pad_add_fusion.2.scalars, bf16[256,576]{1,0:T(8,128)(2,1)} %get-tuple-element.132.refs_0_, bf16[256,576]{1,0:T(8,128)(2,1)} %copy-done.24, bf16[256,576]{1,0:T(8,128)(2,1)} %copy-done.25, ...), custom_call_target="tpu_custom_call" | custom-call | flops 251658240 | bytes 1572864 | tf_op jit(solution)/shard_map/spatial/pallas_call | solution.py:232
  263.1 11.8 %feed_forward.2 = (f32[256,768]{1,0:T(8,128)}, f32[256,768]{1,0:T(8,128)}, bf16[768,768]{1,0:T(8,128)(2,1)}, bf16[768,768]{1,0:T(8,128)(2,1)}, bf16[768,768]{1,0...) custom-call(s32[3]{0:T(128)} %pad_add_fusion.2.scalars, ...), custom_call_target="tpu_custom_call" | custom-call | flops 3623878656 | bytes 15734784 | tf_op jit(solution)/shard_map/feed_forward/pallas_call | solution.py:764
  280.1 12.5 %feed_forward.3 = (f32[256,768]{1,0:T(8,128)}, f32[256,768]{1,0:T(8,128)}, bf16[768,768]{1,0:T(8,128)(2,1)}, bf16[768,768]{1,0:T(8,128)(2,1)}, bf16[768,768]{1,0...) custom-call(s32[3]{0:T(128)} %pad_add_fusion.2.scalars, ...), custom_call_target="tpu_custom_call" | custom-call | flops 3623878656 | bytes 17307648 | tf_op jit(solution)/shard_map/feed_forward/pallas_call | solution.py:764
  307.9 14.9 %collective-permute-done.63 = bf16[2,4,192,384]{3,2,1,0:T(8,128)(2,1)} collective-permute-done((bf16[2,4,192,384]{3,2,1,0:T(8,128)(2,1)S(1)}, bf16[2,4,192,384]{3,2,1,0:T(8,128)(2,1)}, u32[]{:S(2)}, u32[]{:S(2)}) %collective-permute-start.63) | collective-permute-done | bytes 1179680 | tf_op jit(solution)/shard_map/ppermute | solution.py:23
  339.0 12.3 %spatial_back.1 = (bf16[256,576]{1,0:T(8,128)(2,1)}, bf16[256,576]{1,0:T(8,128)(2,1)}, bf16[256,576]{1,0:T(8,128)(2,1)}, bf16[256,576]{1,0:T(8,128)(2,1)}) custom-call(s32[3]{0:T(128)} %pad_add_fusion.2.scalars, bf16[256,576]{1,0:T(8,128)(2,1)} %get-tuple-element.132.refs_0_, bf16[256,576]{1,0:T(8,128)(2,1)} %copy-done.24, bf16[256,576]{1,0:T(8,128)(2,1)} %copy-done.25, ...), custom_call_target="tpu_custom_call" | custom-call | flops 629145600 | bytes 2752512 | tf_op jit(solution)/shard_map/spatial_back/pallas_call | solution.py:232
  368.4 7.3 %spatial_input.1 = (f32[256,768]{1,0:T(8,128)}, bf16[256,768]{1,0:T(8,128)(2,1)}, f32[4,768]{1,0:T(4,128)}, bf16[48,768]{1,0:T(8,128)(2,1)}, bf16[48,768]{1,0:T(...) custom-call(s32[3]{0:T(128)} %pad_add_fusion.2.scalars, ...), custom_call_target="tpu_custom_call" | custom-call | flops 1207959552 | bytes 9349120 | tf_op jit(solution)/shard_map/spatial_input/pallas_call | solution.py:232
  375.6 6.6 %spatial_weights.1 = (bf16[4,240,768]{2,1,0:T(8,128)(2,1)}, bf16[4,240,768]{2,1,0:T(8,128)(2,1)}, bf16[4,240,768]{2,1,0:T(8,128)(2,1)}, bf16[4,240,768]{2,1,0:T(8,128)(2,1)}, f32[1,2304]{1,0:T(1,128)}) custom-call(s32[3]{0:T(128)} %pad_add_fusion.2.scalars, bf16[256,576]{1,0:T(8,128)(2,1)} %get-tuple-element.163.refs_0_, ...), custom_call_target="tpu_custom_call" | custom-call | flops 1207959552 | bytes 9446400 | tf_op jit(solution)/shard_map/spatial_weights/pallas_call | solution.py:232
  390.6 5.6 collective-permute-done.102
  427.3 11.7 %temporal_back.1 = (bf16[256,768]{1,0:T(8,128)(2,1)}, bf16[256,2304]{1,0:T(8,128)(2,1)}) custom-call(s32[3]{0:T(128)} %pad_add_fusion.2.scalars, bf16[48,768]{1,0:T(8,128)(2,1)} %get-tuple-element.171.refs_0_, bf16[48,768]{1,0:T(8,128)(2,1)} %copy-done.86, bf16[48,768]{1,0:T(8,128)(2,1)} %copy-done.87, bf16[48,768]{1,0:T(8,128)(2,1)} %copy-done.88, ...), custom_call_target="tpu_custom_call" | custom-call | flops 805306368 | bytes 5242880 | tf_op jit(solution)/shard_map/temporal_back/pallas_call | solution.py:232
  447.0 5.9 %temporal_weights.1 = (bf16[4,208,768]{2,1,0:T(8,128)(2,1)}, bf16[4,208,768]{2,1,0:T(8,128)(2,1)}, bf16[4,208,768]{2,1,0:T(8,128)(2,1)}, bf16[4,208,768]{2,1,0:T(8,128)(2,1)}) custom-call(s32[3]{0:T(128)} %pad_add_fusion.2.scalars, bf16[256,2304]{1,0:T(8,128)(2,1)} %get-tuple-element.190.grad_ref, bf16[256,768]{1,0:T(8,128)(2,1)} %get-tuple-element.197.normed_ref, ...), custom_call_target="tpu_custom_call" | custom-call | flops 1207959552 | bytes 7569408 | tf_op jit(solution)/shard_map/temporal_weights/pallas_call | solution.py:232
  465.0 7.7 %collective-permute-done.94 = bf16[2,240,384]{2,1,0:T(8,128)(2,1)S(1)} collective-permute-done((bf16[2,240,384]{2,1,0:T(8,128)(2,1)S(1)}, bf16[2,240,384]{2,1,0:T(8,128)(2,1)S(1)}, u32[]{:S(2)}, u32[]{:S(2)}) %collective-permute-start.94) | collective-permute-done | bytes 368672 | tf_op jit(solution)/shard_map/ppermute | solution.py:23
  474.2 12.8 %collective-permute-done.95 = bf16[2,240,384]{2,1,0:T(8,128)(2,1)S(1)} collective-permute-done((bf16[2,240,384]{2,1,0:T(8,128)(2,1)S(1)}, bf16[2,240,384]{2,1,0:T(8,128)(2,1)S(1)}, u32[]{:S(2)}, u32[]{:S(2)}) %collective-permute-start.95) | collective-permute-done | bytes 368672 | tf_op jit(solution)/shard_map/ppermute | solution.py:23
  488.8 6.1 %collective-permute-start.76 = (bf16[64,768]{1,0:T(8,128)(2,1)}, bf16[64,768]{1,0:T(8,128)(2,1)S(1)}, u32[]{:S(2)}, u32[]{:S(2)}) collective-permute-start(bf16[64,768]{1,0:T(8,128)(2,1)} %get-tuple-element.194), channel_id=1, source_target_pairs={{0,1},{1,0},{2,3},{3,2},{4,5},{5,4},{6,7},{7,6},{8,9},{9,8},{10,11... | collective-permute-start | bytes 294920 | tf_op jit(solution)/shard_map/ppermute | solution.py:23
  494.8 7.1 %collective-permute-done.97 = bf16[2,240,384]{2,1,0:T(8,128)(2,1)S(1)} collective-permute-done((bf16[2,240,384]{2,1,0:T(8,128)(2,1)S(1)}, bf16[2,240,384]{2,1,0:T(8,128)(2,1)S(1)}, u32[]{:S(2)}, u32[]{:S(2)}) %collective-permute-start.97) | collective-permute-done | bytes 368672 | tf_op jit(solution)/shard_map/ppermute | solution.py:23
  533.0 8.9 %collective-permute-done.100 = bf16[192,384]{1,0:T(8,128)(2,1)S(1)} collective-permute-done((bf16[192,384]{1,0:T(8,128)(2,1)S(1)}, bf16[192,384]{1,0:T(8,128)(2,1)S(1)}, u32[]{:S(2)}, u32[]{:S(2)}) %collective-permute-start.100) | collective-permute-done | bytes 147488 | tf_op jit(solution)/shard_map/ppermute | solution.py:23
  550.4 7.3 %collective-permute-done.88 = bf16[208,384]{1,0:T(8,128)(2,1)S(1)} collective-permute-done((bf16[208,384]{1,0:T(8,128)(2,1)S(1)}, bf16[208,384]{1,0:T(8,128)(2,1)S(1)}, u32[]{:S(2)}, u32[]{:S(2)}) %collective-permute-start.88) | collective-permute-done | bytes 159776 | tf_op jit(solution)/shard_map/ppermute | solution.py:23
  (934 shorter events, 338.3 us)
Async XLA Ops:
  2.8 45.6 %collective-permute-start.7 = (bf16[192,384]{1,0:T(8,128)(2,1)S(1)}, bf16[192,384]{1,0:T(8,128)(2,1)S(1)}, u32[]{:S(2)}, u32[]{:S(2)}) collective-permute-start(bf16[192,384]{1,0:T(8,128)(2,1)S(1)} %bitcast.305), channel_id=1, source_target_pairs={{0,1},{1,0},{2,3},{3,2},{4,5},{5,4},{6,7},{7,6},{8,9},{9,8},{10,11... | collective-permute-start | bytes 442376 | tf_op jit(solution)/shard_map/ppermute | solution.py:23
  5.9 42.5 %collective-permute-start.8 = (bf16[192,384]{1,0:T(8,128)(2,1)S(1)}, bf16[192,384]{1,0:T(8,128)(2,1)S(1)}, u32[]{:S(2)}, u32[]{:S(2)}) collective-permute-start(bf16[192,384]{1,0:T(8,128)(2,1)S(1)} %bitcast.306), channel_id=1, source_target_pairs={{0,2},{1,3},{2,0},{3,1},{4,6},{5,7},{6,4},{7,5},{8,10},{9,11},{10,... | collective-permute-start | bytes 442376 | tf_op jit(solution)/shard_map/ppermute | solution.py:23
  8.5 40.0 %collective-permute-start.9 = (bf16[192,384]{1,0:T(8,128)(2,1)S(1)}, bf16[192,384]{1,0:T(8,128)(2,1)S(1)}, u32[]{:S(2)}, u32[]{:S(2)}) collective-permute-start(bf16[192,384]{1,0:T(8,128)(2,1)S(1)} %bitcast.307), channel_id=1, source_target_pairs={{0,3},{1,2},{2,1},{3,0},{4,7},{5,6},{6,5},{7,4},{8,11},{9,10},{10,... | collective-permute-start | bytes 442376 | tf_op jit(solution)/shard_map/ppermute | solution.py:23
  8.9 57.9 %collective-permute-start.14 = (bf16[12,384]{1,0:T(8,128)(2,1)S(1)}, bf16[12,384]{1,0:T(8,128)(2,1)S(1)}, u32[]{:S(2)}, u32[]{:S(2)}) collective-permute-start(bf16[12,384]{1,0:T(8,128)(2,1)S(1)} %concatenate.116), channel_id=1, source_target_pairs={{0,16},{16,0},{1,17},{17,1},{2,18},{18,2},{3,19},{19,3},{4,20},{20... | collective-permute-start | bytes 27656 | tf_op jit(solution)/shard_map/ppermute | solution.py:23
  66.1 48.7 %collective-permute-start.21 = (bf16[4,240,384]{2,1,0:T(8,128)(2,1)S(1)}, bf16[4,240,384]{2,1,0:T(8,128)(2,1)S(1)}, u32[]{:S(2)}, u32[]{:S(2)}) collective-permute-start(bf16[4,240,384]{2,1,0:T(8,128)(2,1)S(1)} %pad_maximum_fusion.8), channel_id=1, source_target_pairs={{0,16},{16,0},{1,17},{17,1},{2,18},{18,2},{3,19},{19,3},{4,20},{20... | collective-permute-start | bytes 2211848 | tf_op jit(solution)/shard_map/ppermute | solution.py:23
  66.7 38.9 %collective-permute-start.10 = (bf16[4,192,384]{2,1,0:T(8,128)(2,1)S(1)}, bf16[4,192,384]{2,1,0:T(8,128)(2,1)S(1)}, u32[]{:S(2)}, u32[]{:S(2)}) collective-permute-start(bf16[4,192,384]{2,1,0:T(8,128)(2,1)S(1)} %pad_maximum_fusion.9), channel_id=1, source_target_pairs={{0,16},{16,0},{1,17},{17,1},{2,18},{18,2},{3,19},{19,3},{4,20},{20... | collective-permute-start | bytes 1769480 | tf_op jit(solution)/shard_map/ppermute | solution.py:23
  80.0 31.7 %collective-permute-start = (bf16[64,768]{1,0:T(8,128)(2,1)S(1)}, bf16[64,768]{1,0:T(8,128)(2,1)S(1)}, u32[]{:S(2)}, u32[]{:S(2)}) collective-permute-start(bf16[64,768]{1,0:T(8,128)(2,1)S(1)} %copy-done.166), channel_id=1, source_target_pairs={{0,1},{1,0},{2,3},{3,2},{4,5},{5,4},{6,7},{7,6},{8,9},{9,8},{10,11... | collective-permute-start | bytes 294920 | tf_op jit(solution)/shard_map/ppermute | solution.py:23
  114.8 44.3 %collective-permute-start.12 = (bf16[4,192,768]{2,1,0:T(8,128)(2,1)S(1)}, bf16[4,192,768]{2,1,0:T(8,128)(2,1)}, u32[]{:S(2)}, u32[]{:S(2)}) collective-permute-start(bf16[4,192,768]{2,1,0:T(8,128)(2,1)S(1)} %pad_maximum_fusion.5.refs_9_), channel_id=1, source_target_pairs={{0,8},{4,12},{8,0},{12,4},{1,9},{5,13},{9,1},{13,5},{2,10},{6,14},... | collective-permute-start | bytes 3538952 | tf_op jit(solution)/shard_map/ppermute | solution.py:23
  120.0 42.8 %collective-permute-start.36 = (bf16[2,4,192,384]{3,2,1,0:T(8,128)(2,1)}, bf16[2,4,192,384]{3,2,1,0:T(8,128)(2,1)}, u32[]{:S(2)}, u32[]{:S(2)}) collective-permute-start(bf16[2,4,192,384]{3,2,1,0:T(8,128)(2,1)} %pad_maximum_fusion.6), channel_id=1, source_target_pairs={{0,16},{16,0},{1,17},{17,1},{2,18},{18,2},{3,19},{19,3},{4,20},{20... | collective-permute-start | bytes 3538952 | tf_op jit(solution)/shard_map/ppermute | solution.py:23
  121.7 47.5 %collective-permute-start.31 = (bf16[4,240,768]{2,1,0:T(8,128)(2,1)S(1)}, bf16[4,240,768]{2,1,0:T(8,128)(2,1)}, u32[]{:S(2)}, u32[]{:S(2)}) collective-permute-start(bf16[4,240,768]{2,1,0:T(8,128)(2,1)S(1)} %pad_maximum_fusion.3.refs_16_.refs_10_), channel_id=1, source_target_pairs={{0,8},{4,12},{8,0},{12,4},{1,9},{5,13},{9,1},{13,5},{2,10},{6,14},... | collective-permute-start | bytes 4423688 | tf_op jit(solution)/shard_map/ppermute | solution.py:23
  135.8 30.5 %collective-permute-start.11 = (bf16[4,192,768]{2,1,0:T(8,128)(2,1)S(1)}, bf16[4,192,768]{2,1,0:T(8,128)(2,1)}, u32[]{:S(2)}, u32[]{:S(2)}) collective-permute-start(bf16[4,192,768]{2,1,0:T(8,128)(2,1)S(1)} %pad_maximum_fusion.5.refs_9_), channel_id=1, source_target_pairs={{0,4},{4,0},{8,12},{12,8},{1,5},{5,1},{9,13},{13,9},{2,6},{6,2},{1... | collective-permute-start | bytes 3538952 | tf_op jit(solution)/shard_map/ppermute | solution.py:23
  166.2 96.7 %collective-permute-start.51 = (bf16[2,4,192,768]{3,2,1,0:T(8,128)(2,1)}, bf16[2,4,192,768]{3,2,1,0:T(8,128)(2,1)}, u32[]{:S(2)}, u32[]{:S(2)}) collective-permute-start(bf16[2,4,192,768]{3,2,1,0:T(8,128)(2,1)} %pad_maximum_fusion.refs_16_), channel_id=1, source_target_pairs={{0,4},{4,0},{8,12},{12,8},{1,5},{5,1},{9,13},{13,9},{2,6},{6,2},{1... | collective-permute-start | bytes 7077896 | tf_op jit(solution)/shard_map/ppermute | solution.py:23
  169.2 46.9 %collective-permute-start.32 = (bf16[4,240,768]{2,1,0:T(8,128)(2,1)}, bf16[4,240,768]{2,1,0:T(8,128)(2,1)S(1)}, u32[]{:S(2)}, u32[]{:S(2)}) collective-permute-start(bf16[4,240,768]{2,1,0:T(8,128)(2,1)} %collective-permute-done.31.refs_12_), channel_id=1, source_target_pairs={{0,4},{4,0},{8,12},{12,8},{1,5},{5,1},{9,13},{13,9},{2,6},{6,2},{1... | collective-permute-start | bytes 4423688 | tf_op jit(solution)/shard_map/ppermute | solution.py:23
  199.8 63.2 %collective-permute-start.49 = (bf16[4,192,768]{2,1,0:T(8,128)(2,1)}, bf16[4,192,768]{2,1,0:T(8,128)(2,1)}, u32[]{:S(2)}, u32[]{:S(2)}) collective-permute-start(bf16[4,192,768]{2,1,0:T(8,128)(2,1)} %pad_maximum_fusion.7.refs_4_), channel_id=1, source_target_pairs={{0,4},{4,0},{8,12},{12,8},{1,5},{5,1},{9,13},{13,9},{2,6},{6,2},{1... | collective-permute-start | bytes 3538952 | tf_op jit(solution)/shard_map/ppermute | solution.py:23
  201.0 61.9 %collective-permute-start.50 = (bf16[4,192,768]{2,1,0:T(8,128)(2,1)}, bf16[4,192,768]{2,1,0:T(8,128)(2,1)}, u32[]{:S(2)}, u32[]{:S(2)}) collective-permute-start(bf16[4,192,768]{2,1,0:T(8,128)(2,1)} %collective-permute-done.48), channel_id=1, source_target_pairs={{0,4},{4,0},{8,12},{12,8},{1,5},{5,1},{9,13},{13,9},{2,6},{6,2},{1... | collective-permute-start | bytes 3538952 | tf_op jit(solution)/shard_map/ppermute | solution.py:23
  296.1 34.7 %collective-permute-start.58 = (bf16[4,192,768]{2,1,0:T(8,128)(2,1)}, bf16[4,192,768]{2,1,0:T(8,128)(2,1)}, u32[]{:S(2)}, u32[]{:S(2)}) collective-permute-start(bf16[4,192,768]{2,1,0:T(8,128)(2,1)} %bitcast.70), channel_id=1, source_target_pairs={{0,4},{4,0},{8,12},{12,8},{1,5},{5,1},{9,13},{13,9},{2,6},{6,2},{1... | collective-permute-start | bytes 3538952 | tf_op jit(solution)/shard_map/ppermute | solution.py:23
  298.9 34.1 %collective-permute-start.64 = (bf16[4,192,768]{2,1,0:T(8,128)(2,1)}, bf16[4,192,768]{2,1,0:T(8,128)(2,1)}, u32[]{:S(2)}, u32[]{:S(2)}) collective-permute-start(bf16[4,192,768]{2,1,0:T(8,128)(2,1)} %fusion.refs_11_), channel_id=1, source_target_pairs={{0,8},{4,12},{8,0},{12,4},{1,9},{5,13},{9,1},{13,5},{2,10},{6,14},... | collective-permute-start | bytes 3538952 | tf_op jit(solution)/shard_map/ppermute | solution.py:23
  330.7 30.5 %collective-permute-start.109 = (bf16[2,192,384]{2,1,0:T(8,128)(2,1)}, bf16[2,192,384]{2,1,0:T(8,128)(2,1)}, u32[]{:S(2)}, u32[]{:S(2)}) collective-permute-start(bf16[2,192,384]{2,1,0:T(8,128)(2,1)} %get-tuple-element.319), channel_id=1, source_target_pairs={{0,2},{1,3},{2,0},{3,1},{4,6},{5,7},{6,4},{7,5},{8,10},{9,11},{10,... | collective-permute-start | bytes 884744 | tf_op jit(solution)/shard_map/ppermute | solution.py:23
  421.1 41.5 %collective-permute-start.105 = (bf16[192,384]{1,0:T(8,128)(2,1)}, bf16[192,384]{1,0:T(8,128)(2,1)}, u32[]{:S(2)}, u32[]{:S(2)}) collective-permute-start(bf16[192,384]{1,0:T(8,128)(2,1)} %get-tuple-element.295), channel_id=1, source_target_pairs={{0,4},{4,0},{8,12},{12,8},{1,5},{5,1},{9,13},{13,9},{2,6},{6,2},{1... | collective-permute-start | bytes 442376 | tf_op jit(solution)/shard_map/ppermute | solution.py:23
  424.3 39.3 %collective-permute-start.106 = (bf16[192,384]{1,0:T(8,128)(2,1)}, bf16[192,384]{1,0:T(8,128)(2,1)}, u32[]{:S(2)}, u32[]{:S(2)}) collective-permute-start(bf16[192,384]{1,0:T(8,128)(2,1)} %get-tuple-element.295), channel_id=1, source_target_pairs={{0,8},{4,12},{8,0},{12,4},{1,9},{5,13},{9,1},{13,5},{2,10},{6,14},... | collective-permute-start | bytes 442376 | tf_op jit(solution)/shard_map/ppermute | solution.py:23
  425.8 31.5 %collective-permute-start.93 = (bf16[2,4,240,384]{3,2,1,0:T(8,128)(2,1)}, bf16[2,4,240,384]{3,2,1,0:T(8,128)(2,1)S(1)}, u32[]{:S(2)}, u32[]{:S(2)}) collective-permute-start(bf16[2,4,240,384]{3,2,1,0:T(8,128)(2,1)} %pad_maximum_fusion.2), channel_id=1, source_target_pairs={{0,16},{16,0},{1,17},{17,1},{2,18},{18,2},{3,19},{19,3},{4,20},{20... | collective-permute-start | bytes 4423688 | tf_op jit(solution)/shard_map/ppermute | solution.py:23
  463.6 38.7 %collective-permute-start.83 = (bf16[4,208,768]{2,1,0:T(8,128)(2,1)S(1)}, bf16[4,208,768]{2,1,0:T(8,128)(2,1)S(1)}, u32[]{:S(2)}, u32[]{:S(2)}) collective-permute-start(bf16[4,208,768]{2,1,0:T(8,128)(2,1)S(1)} %copy-done.158), channel_id=1, source_target_pairs={{0,4},{4,0},{8,12},{12,8},{1,5},{5,1},{9,13},{13,9},{2,6},{6,2},{1... | collective-permute-start | bytes 3833864 | tf_op jit(solution)/shard_map/ppermute | solution.py:23
  463.6 39.3 %collective-permute-start.85 = (bf16[4,208,768]{2,1,0:T(8,128)(2,1)S(1)}, bf16[4,208,768]{2,1,0:T(8,128)(2,1)S(1)}, u32[]{:S(2)}, u32[]{:S(2)}) collective-permute-start(bf16[4,208,768]{2,1,0:T(8,128)(2,1)S(1)} %add_convert_fusion.4), channel_id=1, source_target_pairs={{0,8},{4,12},{8,0},{12,4},{1,9},{5,13},{9,1},{13,5},{2,10},{6,14},... | collective-permute-start | bytes 3833864 | tf_op jit(solution)/shard_map/ppermute | solution.py:23
  472.7 34.8 %collective-permute-start.65 = (bf16[256,768]{1,0:T(8,128)(2,1)S(1)}, bf16[256,768]{1,0:T(8,128)(2,1)S(1)}, u32[]{:S(2)}, u32[]{:S(2)}) collective-permute-start(bf16[256,768]{1,0:T(8,128)(2,1)S(1)} %copy-done.19), channel_id=1, source_target_pairs={{0,16},{16,0},{1,17},{17,1},{2,18},{18,2},{3,19},{19,3},{4,20},{20... | collective-permute-start | bytes 1179656 | tf_op jit(solution)/shard_map/ppermute | solution.py:23
  (279 other events, 3712.4 us)

commit v4 on v1

v4 whole, which is shorter than its diff:
```python
import jax
import jax.numpy as jnp
import numpy as np
from jax import lax
from jax.experimental import pallas as pl
from jax.experimental.pallas import tpu as pltpu
from jax.sharding import PartitionSpec as P

HEAD_DIM = 64
WINDOW = 64
CHUNK = 32
EPS = 1e-06
SQRT_HALF = 0.7071067811865476
INV_ROOT_TAU = 0.3989422804014327
SCALE = HEAD_DIM**-0.5
HIDE = -1e30
LOW = jnp.bfloat16
F32 = jnp.float32
VMEM_BYTES = 60 * 2**20
PEAK = 1.15e9
COSTS = {
    "natural_last": 60,
    "send_rows": 6,
    "temporal_start": 10,
    "temporal": 30,
    "temporal_out": 6,
    "spatial_in": 8,
    "spatial": 20,
    "spatial_out": 8,
    "feed_forward": 26,
    "feed_forward_back": 10,
    "spatial_back": 28,
    "spatial_input": 20,
    "temporal_grad": 20,
    "temporal_back": 70,
    "temporal_input": 70,
    "group_weights": 0.2,
    "natural": 0.2,
    "out_weights": 0.2,
    "frames_of": 0.2,
}


def hop(values, axis, step):
    count = lax.axis_size(axis)
    return lax.ppermute(values, axis, [(i, i ^ step) for i in range(count)])


def hop_group(values):
    quarters, ranks = lax.axis_size("context"), lax.axis_size("tensor")
    pairs = [
        (c * ranks + i, c * ranks + (i ^ group_of(c))) for c in range(quarters) for i in range(ranks)
    ]
    return lax.ppermute(values, ("context", "tensor"), pairs)


def group_of(context):
    return 2 * (context % 2) + context // 2


def pick(values, index, axis=0):
    return lax.dynamic_index_in_dim(values, index, axis, keepdims=False)


def ordered(parts, me, axis=0):
    shape = list(parts[0].shape)
    shape.insert(axis, len(parts))
    out = jnp.zeros(shape, parts[0].dtype)
    for j, part in enumerate(parts):
        out = lax.dynamic_update_index_in_dim(out, part, me ^ j, axis)
    return out


def round_up(value, step):
    return -(-value // step) * step


class Place:
    def __init__(self):
        self.shard = lax.axis_index("shard")
        self.context = lax.axis_index("context")
        self.tensor = lax.axis_index("tensor")
        self.shards = lax.axis_size("shard")
        self.ranks = lax.axis_size("tensor")
        self.quarters = lax.axis_size("context")
        self.paired = self.shards == 2


def tie(values, *others):
    return lax.optimization_barrier((values,) + others)[0] if others else values


def add(*terms):
    total = terms[0].astype(F32)
    for term in terms[1:]:
        total = total + term.astype(F32)
    return total.astype(LOW)


class Gather:
    def __init__(self, place, mine):
        self.place = place
        self.parts = [mine] + [hop(mine, "tensor", k) for k in range(1, place.ranks)]

    def columns(self, *later):
        blocks = jnp.stack([tie(part, *later) for part in self.parts])
        if self.place.paired:
            self.parts = [blocks, hop(blocks, "shard", 1)]
        else:
            self.parts = [lax.all_gather(blocks, "shard", axis=2, tiled=True)]
        self.far = [hop(blocks, "context", 2)] if self.place.paired else []

    def rows(self, *later):
        self.far.append(hop(tie(self.parts[-1], *later), "context", 2))

    def cores(self, *later):
        join = lambda parts: jnp.concatenate([tie(part, *later) for part in parts], -1)
        self.first, second = join(self.parts), join(self.far)
        return [self.first, hop(self.first, "context", 1), second, hop(second, "context", 1)]


class ReduceHidden:
    def __init__(self, place, pieces):
        self.place = place
        self.kept = [pieces[0], pieces[2]]
        self.come = [hop(pieces[1], "context", 1), hop(pieces[3], "context", 1)]
        self.middle = pieces[0].shape[1] // 2
        self.half = pieces[0].shape[2] // (2 if place.paired else 1)

    def part(self, index, rows, columns):
        return add(self.kept[index][:, rows, columns], self.come[index][:, rows, columns])

    def cores(self, *later):
        self.come = [tie(item, *later) for item in self.come]
        top, low = slice(self.middle), slice(self.middle, None)
        left, right = slice(self.half), slice(self.half, None)
        out = []
        if self.place.paired:
            sent = jnp.stack([self.part(index, top, right) for index in range(2)])
            out.append(sent)
            self.come_top = hop(sent, "shard", 1)
        sent = self.part(1, low, slice(None))
        self.come_low = hop(sent, "context", 2)
        self.kept_top = lambda: jnp.stack([self.part(index, top, left) for index in range(2)])
        self.kept_low = lambda at: self.part(0, low, at)
        return out + [sent]

    def scatter(self, total):
        axis = total.ndim - 1
        return lax.psum_scatter(total, "shard", scatter_dimension=axis, tiled=True)

    def legs(self, *later):
        come = tie(self.come_low, *later)
        left, right = slice(self.half), slice(self.half, None)
        if self.place.paired:
            top = add(self.kept_top(), tie(self.come_top, *later))
            low = add(self.kept_low(left), come[..., left])
            sent = add(self.kept_low(right), come[..., right])
            self.come_low = hop(sent, "shard", 1)
        else:
            top = self.scatter(self.kept_top())
            low, sent, self.come_low = self.scatter(add(self.kept_low(left), come)), top, None
        self.top, self.low = top[0], low
        self.come_top = hop(top[1], "context", 2)
        return [top, low, sent]

    def both(self, *later):
        top = add(self.top, tie(self.come_top, *later))
        low = self.low if self.come_low is None else add(self.low, tie(self.come_low, *later))
        mine = jnp.concatenate([top, low], 1)
        self.kept = mine[0]
        self.come = [hop(mine[k], "tensor", k) for k in range(1, self.place.ranks)]
        return [mine]

    def hops(self, *later):
        self.sum = add(self.kept, *[tie(come, *later) for come in self.come])
        return [self.sum]

    def finish(self):
        return gather_context(self.place, self.sum)


def gather_context(place, mine):
    second = hop(mine, "context", 2)
    both = jnp.stack([mine, second])
    far = hop(both, "context", 1)
    return ordered([both[0], far[0], both[1], far[1]], place.context).astype(F32)


class ReduceShared:
    def __init__(self, place, pieces, each):
        self.place, self.each = place, each
        self.kept = [pieces[0], pieces[2]]
        self.come = [hop(pieces[1], "context", 1), hop(pieces[3], "context", 1)]

    def cores(self, *later):
        first, second = [add(a, tie(b, *later)) for a, b in zip(self.kept, self.come)]
        self.kept, self.come = first, hop(second, "context", 2)
        return [first, second]

    def rows(self, *later):
        come = tie(self.come, *later)
        if self.place.paired:
            half = come.shape[-1] // 2
            sent = add(self.kept[:, half:], come[:, half:])
            self.kept, self.come = add(self.kept[:, :half], come[:, :half]), hop(sent, "shard", 1)
            return [sent]
        self.kept = lax.psum_scatter(
            add(self.kept, come), "shard", scatter_dimension=1, tiled=True
        )
        self.come = None
        return [self.kept]

    def columns(self, *later):
        mine = self.kept if self.come is None else add(self.kept, tie(self.come, *later))
        ranks, each = self.place.ranks, self.each
        common = mine[ranks * each :]
        block = lambda k: jnp.concatenate([mine[k * each : (k + 1) * each], common])
        self.kept = block(0)
        self.come = [hop(block(k), "tensor", k) for k in range(1, ranks)]
        return [mine]

    def hops(self, *later):
        self.sum = add(self.kept, *[tie(come, *later) for come in self.come])
        return [self.sum]

    def finish(self):
        return gather_context(self.place, self.sum)


def sum_columns(place, kept, sent, *later):
    if place.paired:
        return add(kept, tie(hop(sent, "shard", 1), *later))
    return lax.psum_scatter(kept, "shard", scatter_dimension=1, tiled=True)


class SumContext:
    def __init__(self, place, total):
        self.core, self.shape = place.context % 2, total.shape
        halves = total.reshape(2, -1, total.shape[-1])
        self.kept, self.come = pick(halves, self.core), hop(pick(halves, 1 - self.core), "context", 1)

    def cores(self, *later):
        self.kept = add(self.kept, tie(self.come, *later))
        self.come = hop(self.kept, "context", 2)
        return [self.kept]

    def finish(self):
        half = add(self.kept, self.come)
        whole = ordered([half, hop(half, "context", 1)], self.core)
        return whole.reshape(self.shape).astype(F32)


class Layout:
    def __init__(self, place, clips):
        self.place = place
        self.batches, self.frames, self.places = clips.shape[:3]
        self.whole = 1 if place.paired else self.batches
        self.split = self.batches - self.whole
        self.first = self.whole * self.places
        self.later = -(-self.split * self.places // 2)
        self.slots = round_up(self.first + self.later, CHUNK)
        self.temporal_rows = self.frames * self.slots
        self.units = self.whole * self.frames + self.split
        self.frame_rows = round_up(self.units * self.places, 16)
        self.natural_blocks = self.batches * self.frames
        self.own = self.whole * self.frames * self.places // 16 * 16

    def label(self, batch, frame, spot):
        return (batch * self.frames * self.place.ranks + frame) * self.places + spot

    def split_labels(self, part, frames):
        flat = self.later * part + np.arange(self.later)[None]
        labels = self.label(
            self.whole + flat // self.places, np.asarray(frames)[:, None], flat % self.places
        )
        return np.where(flat < self.split * self.places, labels, -1)

    def frames_at(self, tensor):
        return self.frames * tensor + np.arange(self.frames)

    def temporal_labels(self, shard, tensor):
        frames = self.frames_at(tensor)
        slot = np.arange(self.first)[None]
        parts = [self.label(slot // self.places, frames[:, None], slot % self.places)]
        if self.split:
            parts.append(self.split_labels(shard, frames))
        labels = np.concatenate(parts, 1)
        spare = self.slots - labels.shape[1]
        return np.pad(labels, ((0, 0), (0, spare)), constant_values=-1)

    def frame_labels(self, shard, tensor, far=False):
        row = np.arange(self.frame_rows)
        unit, spot = row // self.places, row % self.places
        batch, frame = unit // self.frames, self.frames * tensor + unit % self.frames
        later = unit - self.whole * self.frames
        batch = np.where(later >= 0, self.whole + later, batch)
        frame = np.where(later >= 0, self.frames * tensor + shard, frame)
        inside = (unit < self.units) & ((later >= 0) | (not far))
        return np.where(inside, self.label(batch, frame, spot), -1)

    def natural_labels(self, tensor):
        batch = np.arange(self.batches)[:, None, None]
        frame = self.frames_at(tensor)[None, :, None]
        spot = np.arange(WINDOW)[None, None]
        return np.where(spot < self.places, self.label(batch, frame, spot), -1)

    def other_labels(self, shard, tensor):
        batch = np.arange(self.whole, self.batches)[:, None]
        spot = np.arange(WINDOW)[None]
        labels = self.label(batch, self.frames * tensor + shard, spot)
        return np.where(spot < self.places, labels, -1)

    def moves(self, shard, tensor):
        natural, frame = self.natural_labels(tensor), self.frame_labels(shard, tensor)
        temporal = self.temporal_labels(shard, tensor)
        moves = {
            "beginning": ([temporal], [natural]),
            "starting": ([frame], [natural]),
            "returning": ([frame], [temporal]),
            "arriving": ([temporal], [frame]),
            "homing": ([natural], [temporal]),
            "ending": ([natural], [frame]),
        }
        if self.split:
            frames, other = self.frames_at(tensor), 1 - shard

            def packed(part, frames):
                labels = self.split_labels(part, frames).reshape(-1)
                spare = round_up(labels.size, 16) - labels.size
                return np.pad(labels, (0, spare), constant_values=-1)

            mine, theirs = packed(shard, frames), packed(other, frames)
            moves["beginning"][1].append(mine)
            moves["starting"][1].append(self.other_labels(shard, tensor))
            moves["returning"][1].append(packed(other, [frames[shard]]))
            moves["arriving"][1].append(packed(shard, [frames[other]]))
            moves["homing"][1].append(theirs)
            moves["begin_far"] = ([theirs], [natural])
            moves["return_far"] = ([packed(shard, [frames[other]])], [temporal])
            moves["arrive_far"] = ([packed(other, [frames[shard]])], [frame])
            moves["home_far"] = ([mine], [temporal])
            moves["end_far"] = ([natural], [self.frame_labels(other, tensor, True)[self.own :]])
        flat = lambda parts: np.concatenate([np.asarray(part).reshape(-1) for part in parts])
        return {key: (flat(targets), flat(sources)) for key, (targets, sources) in moves.items()}

    def matrices(self):
        ranks = self.place.ranks
        shards = 2 if self.split else 1
        table = [self.moves(i // ranks, i % ranks) for i in range(shards * ranks)]
        line = lambda moves: np.concatenate([part for pair in moves.values() for part in pair])
        lines = jnp.asarray(np.stack([line(moves) for moves in table]).astype(np.int32))
        index = self.place.tensor + (ranks * self.place.shard if self.split else 0)
        labels, at, out = pick(lines, index), 0, {}
        for key, (targets, sources) in table[0].items():
            ends = at + targets.size, at + targets.size + sources.size
            target, source = labels[at : ends[0]], labels[ends[0] : ends[1]]
            same = (target[:, None] == source[None]) & (target[:, None] >= 0)
            out[key], at = same.astype(LOW), ends[1]
        return out


def call(body, outs, ins, scalars, cost=1, scratch=(), after=(), name=None, specs=None):
    given, count = body, len(ins)
    if after:
        body = lambda scalars, *refs: given(scalars, *refs[:count], *refs[count + len(after) :])
    moved = sum(item.size * item.dtype.itemsize for item in list(outs) + list(ins))
    spec = pl.BlockSpec(memory_space=pltpu.VMEM)
    return pl.pallas_call(
        body,
        name=name,
        out_shape=tuple(outs),
        in_specs=[pl.BlockSpec(memory_space=pltpu.SMEM)]
        + list(specs or [spec] * len(ins))
        + [pl.BlockSpec(memory_space=pl.ANY)] * len(after),
        out_specs=(spec,) * len(outs),
        scratch_shapes=list(scratch),
        grid=(1,) if specs else (),
        compiler_params=pltpu.CompilerParams(vmem_limit_bytes=VMEM_BYTES),
        cost_estimate=pl.CostEstimate(
            flops=int(PEAK * cost), bytes_accessed=moved, transcendentals=0
        ),
    )(scalars, *ins, *after)


def shape(*dims, dtype=LOW):
    return jax.ShapeDtypeStruct(dims, dtype)


def nn(first, second):
    return lax.dot_general(first, second, (((1,), (0,)), ((), ())), preferred_element_type=F32)


def nt(first, second):
    return lax.dot_general(first, second, (((1,), (1,)), ((), ())), preferred_element_type=F32)


def tn(first, second):
    return lax.dot_general(first, second, (((0,), (0,)), ((), ())), preferred_element_type=F32)


def swapper(scalars, paired):
    def swap(values):
        if not paired:
            return values
        half = values.shape[-1] // 2
        other = jnp.concatenate([values[:, half:], values[:, :half]], -1)
        return jnp.where(scalars[0] == 0, values, other)

    return swap


def unit_of(values):
    centred = values - jnp.mean(values, -1, keepdims=True)
    inverse = lax.rsqrt(jnp.mean(centred * centred, -1, keepdims=True) + EPS)
    return (centred * inverse, inverse)


def norm_back(grad, unit, inverse, gain):
    scaled = grad * gain
    inner = (
        scaled
        - jnp.mean(scaled, -1, keepdims=True)
        - unit * jnp.mean(scaled * unit, -1, keepdims=True)
    )
    return (
        inverse * inner,
        jnp.sum(grad * unit, 0, keepdims=True),
        jnp.sum(grad, 0, keepdims=True),
    )


def softmax(scores):
    weights = jnp.exp(scores - jnp.max(scores, -1, keepdims=True))
    return weights / jnp.sum(weights, -1, keepdims=True)


def score_back(probs, prob_grad):
    inner = jnp.sum(probs * prob_grad, -1, keepdims=True)
    return (probs * (prob_grad - inner)).astype(LOW)


def half_lanes(width):
    lane = lax.broadcasted_iota(jnp.int32, (1, width), 1)
    return [(lane // HEAD_DIM == e).astype(F32) for e in range(2)]


def column_sum(values):
    return jnp.sum(values.astype(F32), 0, keepdims=True)


def rows_at(start, size):
    return pl.ds(pl.multiple_of(start, 16), size)


class Program:
    def __init__(self, place, layout, width, group, scalars):
        self.place, self.layout, self.width, self.group = place, layout, width, group
        self.scalars = scalars
        self.ranks, self.quarters = place.ranks, place.quarters
        self.piece = group // self.quarters
        self.heads = group // HEAD_DIM
        self.all_heads = group * self.ranks
        spot = np.arange(self.ranks * layout.frames * CHUNK) % CHUNK
        self.same_place = jnp.asarray(
            np.where(spot[:, None] == spot[None], 0, HIDE).astype(np.float32)
        )

    def call(self, body, outs, ins, flops=0, scratch=(), after=(), specs=None, cost=None):
        name = body.__qualname__.split(".")[1]
        cost = COSTS[cost or name]
        return call(body, outs, ins, self.scalars, cost, scratch, after, name, specs)

    def lanes(self, c, h):
        at = c * self.group + h * HEAD_DIM
        return slice(at, at + HEAD_DIM)


    def live(self, scalars, batch):
        return scalars[3 + batch] > 0

    def place_natural(self, scalars, rows, source):
        lay = self.layout
        rows[...] = jnp.zeros_like(rows)
        for item in range(lay.natural_blocks):

            @pl.when(self.live(scalars, item // lay.frames))
            def _(item=item):
                rows[item * WINDOW : item * WINDOW + lay.places] = source[item]

    def send_rows(self, clips, cotangents, matrix, wait=()):
        lay, width = self.layout, self.width
        count, split = lay.natural_blocks, lay.split
        first = lay.whole * lay.frames

        def body(scalars, clips_ref, grads_ref, matrix_ref, sent, frames, rows):
            self.place_natural(scalars, rows, clips_ref)
            sent[...] = nn(matrix_ref[...], rows[...]).astype(LOW)
            for index, source in enumerate((clips_ref, grads_ref)):
                for item in range(split):
                    frame = first + lay.frames * item + 1 - scalars[0]
                    frames[index, item] = source[frame]

        outs = [shape(matrix.shape[0], width), shape(2, split, lay.places, width)]
        scratch = [pltpu.VMEM((count * WINDOW, width), LOW)]
        return self.call(body, outs, [clips, cotangents, matrix], scratch=scratch, after=wait)

    def temporal_start(self, clips, come, matrix):
        lay, width = self.layout, self.width
        count, rows_in = lay.natural_blocks, lay.natural_blocks * WINDOW
        more = 0 if come is None else come.shape[0]

        def body(scalars, clips_ref, *refs):
            matrix_ref, start_ref, normed_ref, rows = refs[-4:]
            self.place_natural(scalars, rows, clips_ref)
            if more:
                rows[rows_in:] = refs[0][...]
            start = nn(matrix_ref[...], rows[...])
            start_ref[...] = start.astype(LOW)
            unit, _ = unit_of(start)
            swap = swapper(scalars, self.place.paired)
            normed_ref[...] = swap(unit).astype(LOW)

        outs = [shape(lay.temporal_rows, width)] * 2
        ins = [clips] + ([come] if more else []) + [matrix]
        scratch = [pltpu.VMEM((rows_in + more, width), LOW)]
        return self.call(body, outs, ins, scratch=scratch)

    def frames_of(self, clips, others, index, matrix, wait=()):
        lay, width = self.layout, self.width
        count, split = lay.natural_blocks, lay.split

        def body(scalars, clips_ref, *refs):
            matrix_ref, out_ref, rows = refs[-3:]
            self.place_natural(scalars, rows, clips_ref)
            for item in range(split):

                @pl.when(jnp.logical_not(self.live(scalars, lay.whole + item)))
                def _(item=item):
                    start = (count + item) * WINDOW
                    rows[start : start + lay.places] = refs[0][index, item]

            out_ref[...] = nn(matrix_ref[...], rows[...]).astype(LOW)

        return self.call(
            body,
            [shape(lay.frame_rows, width)],
            [clips] + ([others] if split else []) + [matrix],
            scratch=[pltpu.VMEM(((count + split) * WINDOW, width), LOW)],
            after=wait,
        )[0]


    def chunk(self, refs, n):
        lay = self.layout
        return jnp.concatenate(
            [
                ref[rows_at(frame * lay.slots + n * CHUNK, CHUNK)]
                for ref in refs
                for frame in range(lay.frames)
            ]
        )

    def put_chunk(self, refs, n, values):
        lay = self.layout
        for k, ref in enumerate(refs):
            for frame in range(lay.frames):
                at = (k * lay.frames + frame) * CHUNK
                ref[rows_at(frame * lay.slots + n * CHUNK, CHUNK)] = values[at : at + CHUNK]

    def temporal(self, units, weights, along, shift, wait=()):
        lay, width, group, ranks = self.layout, self.width, self.group, self.ranks
        rows = lay.temporal_rows

        def body(scalars, *refs):
            unit_refs, weight_refs = refs[:ranks], refs[ranks : ranks + len(weights)]
            refs = refs[ranks + len(weights) :]
            along_ref, shift_ref, same, refs = refs[0], refs[1], refs[2], refs[3:]
            qkv_refs, mixed_refs, normed_refs, out_refs = (
                refs[at : at + ranks] for at in range(0, 4 * ranks, ranks)
            )
            swap = swapper(scalars, self.place.paired)
            gain, move = swap(along_ref[0:1]), swap(along_ref[3:4])
            weight = jnp.concatenate([ref[: 3 * group] for ref in weight_refs], -1)
            for k in range(ranks):
                normed_refs[k][...] = (unit_refs[k][...].astype(F32) * gain + move).astype(LOW)
                qkv_refs[k][...] = (nt(normed_refs[k][...], weight) + shift_ref[...]).astype(LOW)

            @pl.loop(0, lay.slots // CHUNK)
            def _(n):
                values = self.chunk(qkv_refs, n)
                parts = []
                for h in range(self.heads):
                    query, key, value = (values[:, self.lanes(c, h)] for c in range(3))
                    probs = softmax(nt(query, key) * SCALE + same[...])
                    parts.append(nn(probs.astype(LOW), value))
                self.put_chunk(mixed_refs, n, jnp.concatenate(parts, -1).astype(LOW))

            weight = jnp.concatenate([ref[3 * group : 4 * group] for ref in weight_refs], -1)
            for k in range(ranks):
                out_refs[k][...] = nn(mixed_refs[k][...], weight).astype(LOW)

        outs = [shape(rows, 3 * group)] * ranks + [shape(rows, group)] * ranks
        outs += [shape(rows, width)] * (2 * ranks)
        ins = list(units) + list(weights) + [along, shift, self.same_place]
        flops = 8 * ranks * rows * width * group
        flops += 4 * ranks * rows * self.same_place.shape[0] * group
        outs = self.call(body, outs, ins, flops, after=wait)
        return [outs[at : at + ranks] for at in range(0, 4 * ranks, ranks)]

    def temporal_out(self, parts, along, matrix, wait=()):
        lay, width = self.layout, self.width
        far = [] if matrix is None else [matrix]

        def body(scalars, *refs):
            part_refs, along_ref, refs = refs[: self.ranks], refs[self.ranks], refs[self.ranks + 1 :]
            swap = swapper(scalars, self.place.paired)
            total = swap(sum(ref[...].astype(F32) for ref in part_refs)) + along_ref[6:7]
            out_ref = refs[len(far)]
            out_ref[...] = total.astype(LOW)
            if far:
                refs[2][...] = nn(refs[0][...], out_ref[...]).astype(LOW)

        outs = [shape(lay.temporal_rows, width)] + [shape(item.shape[0], width) for item in far]
        return self.call(body, outs, list(parts) + [along] + far, after=wait)

    def temporal_grad(self, parts, matrix, wait=()):
        lay, width = self.layout, self.width

        def body(scalars, *refs):
            matrix_ref, out_ref = refs[len(parts) :]
            swap = swapper(scalars, self.place.paired)
            source = jnp.concatenate([ref[...] for ref in refs[: len(parts)]])
            out_ref[...] = swap(nn(matrix_ref[...], source)).astype(LOW)

        outs = [shape(lay.temporal_rows, width)]
        return self.call(body, outs, list(parts) + [matrix], after=wait)[0]

    def temporal_back(self, qkv, grads, units, weights, wait=()):
        lay, width, group, ranks = self.layout, self.width, self.group, self.ranks
        rows = lay.temporal_rows

        def body(scalars, *refs):
            qkv_refs, grad_refs, unit_refs = (
                refs[at : at + ranks] for at in range(0, 3 * ranks, ranks)
            )
            refs = refs[3 * ranks :]
            weight_refs, same, refs = refs[: len(weights)], refs[len(weights)], refs[len(weights) + 1 :]
            out_refs, back_refs, sums = refs[:ranks], refs[ranks : 2 * ranks], refs[2 * ranks]
            mixed = refs[2 * ranks + 1 :]
            weight = jnp.concatenate([ref[3 * group : 4 * group] for ref in weight_refs], -1)
            for k in range(ranks):
                mixed[k][...] = nt(grad_refs[k][...], weight).astype(LOW)

            @pl.loop(0, lay.slots // CHUNK)
            def _(n):
                values, grads = self.chunk(qkv_refs, n), self.chunk(mixed, n)
                parts = [[], [], []]
                for h in range(self.heads):
                    query, key, value = (values[:, self.lanes(c, h)] for c in range(3))
                    grad = grads[:, self.lanes(0, h)]
                    probs = softmax(nt(query, key) * SCALE + same[...])
                    scored = score_back(probs, nt(grad, value))
                    parts[0].append(nn(scored, key) * SCALE)
                    parts[1].append(tn(scored, query) * SCALE)
                    parts[2].append(tn(probs.astype(LOW), grad))
                total = jnp.concatenate(parts[0] + parts[1] + parts[2], -1)
                self.put_chunk(out_refs, n, total.astype(LOW))

            weight = jnp.concatenate([ref[: 3 * group] for ref in weight_refs], -1)
            sums[...] = jnp.zeros_like(sums)
            for k in range(ranks):
                back = nn(out_refs[k][...], weight)
                back_refs[k][...] = back.astype(LOW)
                sums[0:1] += column_sum(back * unit_refs[k][...].astype(F32))
                sums[1:2] += column_sum(back)

        outs = [shape(rows, 3 * group)] * ranks + [shape(rows, width)] * ranks
        outs += [shape(8, width, dtype=F32)]
        ins = list(qkv) + list(grads) + list(units) + list(weights) + [self.same_place]
        flops = 8 * ranks * rows * width * group
        flops += 10 * ranks * rows * self.same_place.shape[0] * group
        scratch = [pltpu.VMEM((rows, group), LOW)] * ranks
        outs = self.call(body, outs, ins, flops, scratch, wait)
        return outs[:ranks], outs[ranks : 2 * ranks], outs[-1]

    def group_weights(self, qkv_grads, normed, mixed=(), out_grads=(), more=(), wait=()):
        width, group, count = self.width, self.group, len(qkv_grads)
        parts = 2 if self.place.paired else 1
        size = 3 * group + (group if mixed else 0)

        def body(scalars, *refs):
            refs = list(refs)
            take = lambda n: [refs.pop(0) for _ in range(n)]
            grad_refs, normed_refs = take(count), take(count)
            mixed_refs, out_grad_refs = take(len(mixed)), take(len(mixed))
            more_refs, (spread,), out_refs = take(len(more)), take(1), refs
            columns = width // parts

            def put(start, total):
                for part in range(parts):
                    values = total[:, part * columns : (part + 1) * columns]
                    out_refs[part][start : start + total.shape[0]] = values.astype(LOW)

            total = jnp.zeros((3 * group, width), F32)
            sums = jnp.zeros((1, 3 * group), F32)
            for j in range(count):
                total = total + tn(grad_refs[j][...], normed_refs[j][...])
                sums = sums + column_sum(grad_refs[j][...])
            put(0, total)
            if mixed:
                total = jnp.zeros((group, width), F32)
                for j in range(count):
                    total = total + tn(mixed_refs[j][...], out_grad_refs[j][...])
                put(3 * group, total)
            line = jnp.concatenate([sums[:, :group], sums[:, 2 * group :]], -1)
            top = lax.broadcasted_iota(jnp.int32, (16, 2 * group), 0) == 0
            line = jnp.where(top, line, 0.0).astype(LOW)
            for part in range(parts):
                out_refs[part][size : size + 16] = line if parts == 2 else nn(line, spread[...]).astype(LOW)
                for ref in more_refs:
                    rows = ref[:, part * columns : (part + 1) * columns]
                    rows = jnp.concatenate([rows, jnp.zeros_like(rows)])
                    out_refs[part][size + 16 :] = rows.astype(LOW)
                if not more:
                    out_refs[part][size + 16 :] = jnp.zeros((16, columns), LOW)

        outs = [shape(size + 32, width // parts)] * parts
        rows = qkv_grads[0].shape[0]
        ins = list(qkv_grads) + list(normed) + list(mixed) + list(out_grads) + list(more)
        ins += [self.spread()]
        return self.call(body, outs, ins, 2 * count * rows * width * size, after=wait)

    def spread(self):
        shards = self.place.shards
        columns, part = self.width // shards, HEAD_DIM // shards
        out = np.zeros((2 * self.group, self.width), np.float32)
        for item in range(2 * self.group):
            head, feature = divmod(item, HEAD_DIM)
            out[item, feature // part * columns + head * part + feature % part] = 1
        return jnp.asarray(out, LOW)

    def temporal_input(self, backs, start, along, matrix, wait=()):
        lay, width = self.layout, self.width
        far = [] if matrix is None else [matrix]

        def body(scalars, *refs):
            back_refs, refs = refs[: self.ranks], refs[self.ranks :]
            start_ref, along_ref, refs = refs[0], refs[1], refs[2:]
            out_ref = refs[len(far)]
            swap = swapper(scalars, self.place.paired)
            unit, inverse = unit_of(start_ref[...].astype(F32))
            grad = swap(sum(ref[...].astype(F32) for ref in back_refs))
            back, _, _ = norm_back(grad, unit, inverse, along_ref[0:1])
            out_ref[...] = back.astype(LOW)
            if far:
                refs[2][...] = nn(refs[0][...], out_ref[...]).astype(LOW)

        outs = [shape(lay.temporal_rows, width)] + [shape(item.shape[0], width) for item in far]
        return self.call(body, outs, list(backs) + [start, along] + far, after=wait)


    def spatial_in(self, sources, matrix, start, fc, along, wait=()):
        lay, width = self.layout, self.width
        rows = lay.frame_rows

        def body(scalars, *refs):
            source_refs, refs = refs[: len(sources)], refs[len(sources) :]
            matrix_ref, start_ref, fc_refs, refs = refs[0], refs[1], refs[2 : 2 + len(fc)], refs[2 + len(fc) :]
            along_ref, after_ref, temporal_ref, normed_ref = refs
            swap = swapper(scalars, self.place.paired)
            source = jnp.concatenate([ref[...] for ref in source_refs])
            temporal = nn(matrix_ref[...], source)
            temporal_ref[...] = temporal.astype(LOW)
            weight = jnp.concatenate([ref[...] for ref in fc_refs])
            after = start_ref[...].astype(F32) + nn(swap(temporal).astype(LOW), weight)
            after = after + along_ref[7:8]
            after_ref[...] = after
            unit, _ = unit_of(after)
            normed_ref[...] = swap(unit * along_ref[1:2] + along_ref[4:5]).astype(LOW)

        outs = [shape(rows, width, dtype=F32), shape(rows, width), shape(rows, width)]
        ins = list(sources) + [matrix, start] + list(fc) + [along]
        return self.call(body, outs, ins, 2 * rows * width * width, after=wait)

    def windows(self, refs, n):
        at = rows_at(n * (WINDOW - 16), WINDOW)
        return jnp.concatenate([ref[at] for ref in refs])

    def window_mask(self, n, axis):
        size = self.quarters * WINDOW
        dims = (size, 1) if axis == 0 else (1, size)
        index = lax.broadcasted_iota(jnp.int32, dims, axis) & (WINDOW - 1)
        start = n * (self.layout.places - WINDOW + 16)
        return (index >= start) & (index < start + self.layout.places)

    def put_windows(self, refs, n, values, mask):
        for j, ref in enumerate(refs):
            at = rows_at(n * (WINDOW - 16), WINDOW)
            part = slice(j * WINDOW, (j + 1) * WINDOW)
            old = ref[at].astype(F32)
            ref[at] = jnp.where(mask[part], values[part], old).astype(LOW)

    def spatial(self, normed, win, shift, wait=()):
        lay, width, quarters, group = self.layout, self.width, self.quarters, self.group

        def body(scalars, *refs):
            normed_refs, refs = refs[:quarters], refs[quarters:]
            win_refs, shift_ref, refs = refs[: len(win)], refs[len(win)], refs[len(win) + 1 :]
            qkv_refs, out_refs = refs[:quarters], refs[quarters:]
            weight = jnp.concatenate([ref[: 3 * group] for ref in win_refs], -1)
            for j in range(quarters):
                qkv_refs[j][...] = (nt(normed_refs[j][...], weight) + shift_ref[...]).astype(LOW)
                out_refs[j][...] = jnp.zeros_like(out_refs[j])

            @pl.loop(0, lay.units)
            def _(n):
                rows = self.windows(qkv_refs, n)
                hide = jnp.where(self.window_mask(n, 1), 0.0, HIDE)
                parts = []
                for h in range(self.heads):
                    query, key, value = (rows[:, self.lanes(c, h)] for c in range(3))
                    probs = softmax(nt(query, key) * SCALE + hide)
                    parts.append(nn(probs.astype(LOW), value))
                mask = self.window_mask(n, 0)
                self.put_windows(out_refs, n, jnp.concatenate(parts, -1), mask)

        outs = [shape(lay.frame_rows, 3 * group)] * quarters
        outs += [shape(lay.frame_rows, group)] * quarters
        size = quarters * WINDOW
        flops = 6 * quarters * lay.frame_rows * width * group + 4 * lay.units * size * size * group
        outs = self.call(body, outs, list(normed) + list(win) + [shift], flops, after=wait)
        return outs[:quarters], outs[quarters:]

    def spatial_back(self, qkv, grads, win, wait=()):
        lay, width, quarters, group = self.layout, self.width, self.quarters, self.group

        def body(scalars, *refs):
            qkv_refs, grad_refs = refs[:quarters], refs[quarters : 2 * quarters]
            win_refs = refs[2 * quarters : 2 * quarters + len(win)]
            refs = refs[2 * quarters + len(win) :]
            out_refs, back_refs = refs[:quarters], refs[quarters:]
            for ref in out_refs:
                ref[...] = jnp.zeros_like(ref)

            @pl.loop(0, lay.units)
            def _(n):
                rows = self.windows(qkv_refs, n)
                mask = self.window_mask(n, 0)
                grads = self.windows(grad_refs, n) * mask.astype(F32).astype(LOW)
                hide = jnp.where(self.window_mask(n, 1), 0.0, HIDE)
                parts = [[], [], []]
                for h in range(self.heads):
                    query, key, value = (rows[:, self.lanes(c, h)] for c in range(3))
                    grad = grads[:, self.lanes(0, h)]
                    probs = softmax(nt(query, key) * SCALE + hide)
                    scored = score_back(probs, nt(grad, value))
                    parts[0].append(nn(scored, key) * SCALE)
                    parts[1].append(tn(scored, query) * SCALE)
                    parts[2].append(tn(probs.astype(LOW), grad))
                values = jnp.concatenate(parts[0] + parts[1] + parts[2], -1)
                self.put_windows(out_refs, n, values, mask)

            weight = jnp.concatenate([ref[: 3 * group] for ref in win_refs], -1)
            for j in range(quarters):
                back_refs[j][...] = nn(out_refs[j][...], weight).astype(LOW)

        outs = [shape(lay.frame_rows, 3 * group)] * quarters
        outs += [shape(lay.frame_rows, width)] * quarters
        size = quarters * WINDOW
        flops = 10 * lay.units * size * size * group
        flops += 6 * quarters * lay.frame_rows * width * group
        outs = self.call(body, outs, list(qkv) + list(grads) + list(win), flops, after=wait)
        return outs[:quarters], outs[quarters:]

    def put_groups(self, scalars, out, pieces, first):
        for i in range(self.quarters):
            spot = (scalars[1] ^ i) * self.piece
            for j in range(self.quarters):
                k = group_of(scalars[1]) ^ group_of(j)
                out[rows_at(j * self.group + spot, self.piece)] = pieces[i][
                    k, first : first + self.piece
                ]

    def spatial_out(self, mixed, pieces, first, after, grad, along, wait=()):
        lay, width, group = self.layout, self.width, self.group
        rows, quarters = lay.frame_rows, self.quarters
        size = WINDOW

        def body(scalars, *refs):
            mixed_refs, piece_refs, refs = refs[:quarters], refs[quarters : 2 * quarters], refs[2 * quarters :]
            after_ref, grad_ref, along_ref, out_ref, normed_ref, low_ref, wout = refs
            swap = swapper(scalars, self.place.paired)
            self.put_groups(scalars, wout, piece_refs, 0)
            total = jnp.zeros((rows, width), F32)
            for j in range(quarters):
                total = total + nn(mixed_refs[j][...], wout[j * group : (j + 1) * group])
            after = after_ref[...] + swap(total) + along_ref[8:9]
            out_ref[...] = after
            unit, _ = unit_of(after)
            normed_ref[...] = swap(unit * along_ref[2:3] + along_ref[5:6]).astype(LOW)
            low_ref[...] = swap(grad_ref[...].astype(F32)).astype(LOW)

        outs = [
            shape(rows, width, dtype=F32),
            shape(rows, width),
            shape(rows, width),
            shape(self.all_heads, width),
        ]
        ins = list(mixed) + list(pieces) + [after, grad, along]
        whole = pl.BlockSpec(memory_space=pltpu.VMEM)
        part = pl.BlockSpec((self.ranks, size, width), lambda *_: (0, first // size, 0))
        specs = [whole] * quarters + [part] * quarters + [whole] * 3
        flops = 2 * rows * width * self.all_heads
        return self.call(body, outs, ins, flops, after=wait, specs=specs)

    def feed_forward(self, normed, grad, pieces, shifts, totals):
        lay, width = self.layout, self.width
        rows, count, ranks = lay.frame_rows, len(pieces), self.ranks
        hidden = shifts[0].shape[1]
        unit = hidden // ranks
        tile = 256

        def body(scalars, normed_ref, grad_ref, *refs):
            refs = list(refs)
            take = lambda n: [refs.pop(0) for _ in range(n)]
            piece_refs, shift_refs = take(count), take(count)
            before = take(2 if totals else 0)
            out_ref, back_ref = take(2)
            grad_refs, sum_refs = take(count), take(count)
            ups, downs, up_grad, down_grad = take(4)
            out_ref[...] = before[0][...] if totals else jnp.zeros_like(out_ref)
            back_ref[...] = before[1][...] if totals else jnp.zeros_like(back_ref)
            for item in range(count):
                for k in range(ranks):
                    at = slice(k * unit, (k + 1) * unit)
                    ups[at] = piece_refs[item][k, :unit]
                    downs[at] = piece_refs[item][k, unit : 2 * unit]

                @pl.loop(0, hidden // tile)
                def _(m, item=item):
                    at = pl.ds(pl.multiple_of(m * tile, tile), tile)
                    up, down = ups[at], downs[at]
                    values = nt(normed_ref[...], up) + shift_refs[item][:, at]
                    half = 0.5 * (1.0 + lax.erf(values * SQRT_HALF))
                    active = (values * half).astype(LOW)
                    slope = half + values * jnp.exp(-0.5 * values * values) * INV_ROOT_TAU
                    out_ref[...] += nn(active, down)
                    down_grad[at] = tn(active, grad_ref[...]).astype(LOW)
                    hidden_grad = (nt(grad_ref[...], down) * slope).astype(LOW)
                    up_grad[at] = tn(hidden_grad, normed_ref[...]).astype(LOW)
                    back_ref[...] += nn(hidden_grad, up)
                    sum_refs[item][:, at] = column_sum(hidden_grad)

                for k in range(ranks):
                    at = slice(k * unit, (k + 1) * unit)
                    grad_refs[item][k, :unit] = up_grad[at]
                    grad_refs[item][k, unit:] = down_grad[at]

        outs = [shape(rows, width, dtype=F32)] * 2
        outs += [shape(ranks, 2 * unit, width)] * count + [shape(1, hidden, dtype=F32)] * count
        ins = [normed, grad] + list(pieces) + list(shifts) + list(totals or ())
        flops = 12 * rows * width * hidden * count
        scratch = [pltpu.VMEM((hidden, width), LOW)] * 4
        outs = self.call(body, outs, ins, flops, scratch)
        return outs[:2], outs[2 : 2 + count], outs[2 + count :]

    def feed_forward_back(self, after, out, back, grad, mixed, wout, along):
        lay, width, group = self.layout, self.width, self.group
        rows, quarters = lay.frame_rows, self.quarters

        def body(scalars, after_ref, out_ref, back_ref, grad_ref, wout_ref, along_ref, *refs):
            mixed_refs, refs = refs[:quarters], refs[quarters:]
            layer_ref, total_ref, sums, wout_grad = refs[:4]
            mixed_grads = refs[4:]
            swap = swapper(scalars, self.place.paired)
            after = after_ref[...]
            layer_ref[...] = (after + swap(out_ref[...]) + along_ref[9:10]).astype(LOW)
            unit, inverse = unit_of(after)
            back, gain, shift = norm_back(swap(back_ref[...]), unit, inverse, along_ref[2:3])
            grad = grad_ref[...].astype(F32)
            total = grad + back
            total_ref[...] = total
            low = total.astype(LOW)
            sums[0:1] = gain
            sums[1:2] = shift
            sums[2:3] = column_sum(low)
            sums[3:4] = column_sum(grad)
            turned = swap(low.astype(F32)).astype(LOW)
            for j in range(quarters):
                at = slice(j * group, (j + 1) * group)
                mixed_grads[j][...] = nt(turned, wout_ref[at]).astype(LOW)
                wout_grad[at] = tn(mixed_refs[j][...], turned).astype(LOW)

        outs = [
            shape(rows, width),
            shape(rows, width, dtype=F32),
            shape(4, width, dtype=F32),
            shape(self.all_heads, width),
        ] + [shape(rows, group)] * quarters
        ins = [after, out, back, grad, wout, along] + list(mixed)
        outs = self.call(body, outs, ins, 4 * rows * width * self.all_heads)
        return outs[:4], outs[4:]

    def spatial_input(self, backs, after, total, along, fc, matrix, wait=()):
        lay, width = self.layout, self.width
        rows, quarters = lay.frame_rows, self.quarters
        far = [] if matrix is None else [matrix]

        def body(scalars, *refs):
            back_refs, refs = refs[:quarters], refs[quarters:]
            after_ref, total_ref, along_ref, refs = refs[0], refs[1], refs[2], refs[3:]
            fc_refs, refs = refs[: len(fc)], refs[len(fc) :]
            low_ref, out_ref, sums = refs[len(far) : len(far) + 3]
            swap = swapper(scalars, self.place.paired)
            grad = swap(sum(ref[...].astype(F32) for ref in back_refs))
            unit, inverse = unit_of(after_ref[...])
            back, gain, shift = norm_back(grad, unit, inverse, along_ref[1:2])
            low = (total_ref[...] + back).astype(LOW)
            low_ref[...] = low
            weight = jnp.concatenate([ref[...] for ref in fc_refs])
            temporal = swap(nt(low, weight)).astype(LOW)
            out_ref[...] = temporal
            sums[0:1] = gain
            sums[1:2] = shift
            sums[2:3] = column_sum(temporal)
            sums[3:4] = column_sum(low)
            if far:
                refs[4][...] = nn(refs[0][...], temporal).astype(LOW)

        outs = [shape(rows, width), shape(rows, width), shape(4, width, dtype=F32)]
        outs += [shape(item.shape[0], width) for item in far]
        ins = list(backs) + [after, total, along] + list(fc) + far
        return self.call(body, outs, ins, 2 * rows * width * width, after=wait)

    def out_weights(self, wout_grad, low, temporal, vectors, wait=()):
        width, group, piece = self.width, self.group, self.piece
        quarters, ranks = self.quarters, self.ranks
        extra, quarter = vectors.shape[1], width // quarters
        each = piece + extra

        def body(scalars, wout_ref, low_ref, temporal_ref, vectors_ref, *refs):
            pieces, fc = refs[:quarters], refs[quarters]
            swap = swapper(scalars, self.place.paired)
            turned = swap(temporal_ref[...].astype(F32)).astype(LOW)
            fc[...] = tn(low_ref[...], turned).astype(LOW)
            for i in range(quarters):
                spot = (scalars[1] ^ i) * piece
                for j in range(quarters):
                    k = group_of(scalars[1]) ^ group_of(j)
                    pieces[i][rows_at(k * each, piece)] = wout_ref[rows_at(j * group + spot, piece)]
                for k in range(ranks):
                    pieces[i][k * each + piece : (k + 1) * each] = vectors_ref[k]
                pieces[i][ranks * each :] = fc[rows_at((scalars[1] ^ i) * quarter, quarter)]

        outs = [shape(ranks * each + quarter, width)] * quarters
        ins = [wout_grad, low, temporal, vectors]
        flops = 2 * low.shape[0] * width * width
        return self.call(body, outs, ins, flops, [pltpu.VMEM((width, width), LOW)], wait)

    def natural(self, parts, wait=(), last=False):
        lay, width = self.layout, self.width
        count = lay.natural_blocks
        counts = [len(rows) for _, rows in parts]

        def body(scalars, *refs):
            refs = list(refs)
            out_ref = refs.pop()
            total = jnp.zeros((count * WINDOW, width), F32)
            for size in counts:
                matrix = refs.pop(0)
                source = jnp.concatenate([refs.pop(0)[...] for _ in range(size)])
                total = total + nn(matrix[...], source)
            total = total.astype(LOW)
            for item in range(count):
                part = total[item * WINDOW : item * WINDOW + lay.places]
                out_ref[item] = part

                @pl.when(jnp.logical_not(self.live(scalars, item // lay.frames)))
                def _(item=item):
                    out_ref[item] = jnp.zeros((lay.places, width), LOW)


        ins = []
        for matrix, rows in parts:
            ins += [matrix] + list(rows)
        cost = "natural_last" if last else None
        return self.call(body, [shape(count, lay.places, width)], ins, after=wait, cost=cost)[0]


def body(
    clip_input,
    clip_slot,
    norm_gain,
    norm_shift,
    attention_in,
    attention_bias,
    attention_out,
    branch_bias,
    temporal_fc,
    hidden_in,
    hidden_bias,
    hidden_out,
    output_grad,
):
    place = Place()
    shards, quarters, ranks = place.shards, place.quarters, place.ranks
    shard, context, tensor = place.shard, place.context, place.tensor
    clips, cotangents = clip_input[:, 0], output_grad[:, 0]
    lay = Layout(place, clips)
    columns = attention_in.shape[1]
    width = columns * shards
    group = attention_in.shape[3]
    heads = group // HEAD_DIM
    hidden = hidden_in.shape[1]
    piece = group // quarters
    scalars = jnp.concatenate([jnp.stack([shard, context, tensor]), clip_slot[:, 0]])
    prog = Program(place, lay, width, group, scalars.astype(jnp.int32))
    moves = lay.matrices()
    split = lay.split > 0

    def beside(rows):
        return [rows, hop(rows, "shard", 1)] if split else [rows]

    def swapped(rows, axis):
        return [rows[0]] + [hop(rows[k], axis, k) for k in range(1, len(rows))]

    def to_all(rows, axis):
        if axis == "context":
            far = hop(rows, axis, 2)
            return [rows, hop(rows, axis, 1), far, hop(far, axis, 1)]
        return [rows] + [hop(rows, axis, k) for k in range(1, ranks)]

    def shard_parts(block, axis=1):
        if place.paired:
            return [block, hop(block, "shard", 1)]
        return [lax.all_gather(block, "shard", axis=axis, tiled=True)]

    def bias_rows(index):
        rows = attention_bias[index].reshape(-1)
        return jnp.pad(rows, (0, columns - rows.size))[None]

    def in_rows(index):
        return jnp.transpose(attention_in[index], (1, 2, 0)).reshape(3 * group, columns)

    def bias_of(parts, row):
        kinds = 2 * heads * (HEAD_DIM // shards)
        if place.paired:
            lines = [part[row, :kinds] for part in parts]
            lines = jnp.where(shard == 0, jnp.stack(lines), jnp.stack(lines[::-1]))
        else:
            lines = parts[0][row].reshape(shards, columns)[:, :kinds]
        lines = lines.reshape(shards, 2, heads, HEAD_DIM // shards)
        lines = jnp.transpose(lines, (1, 2, 0, 3)).reshape(2, group).astype(F32)
        return jnp.concatenate([lines[0], jnp.zeros(group, F32), lines[1]])[None]

    flat = lambda rows: rows.reshape((-1,) + rows.shape[2:])
    clips, cotangents = flat(clips), flat(cotangents)
    quarter = lambda rows: pick(rows.reshape(quarters, -1, columns), context)
    up_part = pick(hidden_in.reshape(columns, quarters, -1), context, 1).T
    unit = up_part.shape[0]
    block = [up_part, quarter(hidden_out), quarter(attention_out[1])]
    block.append(jnp.pad(hidden_bias.reshape(1, -1), ((0, 15), (0, 0))))
    gather_c = Gather(place, jnp.concatenate(block))

    along = jnp.concatenate([norm_gain, norm_shift, branch_bias, bias_rows(0)])
    along = shard_parts(jnp.pad(along, ((0, 16 - along.shape[0]), (0, 0))))
    shift_a = bias_of(along, 10)
    if place.paired:
        along = jnp.where(shard == 0, *[jnp.concatenate(pair, -1) for pair in (along, along[::-1])])
    else:
        along = along[0]
    along = along[:10].astype(F32)

    come, others = None, None
    if split:
        sent, others = prog.send_rows(clips, cotangents, moves["begin_far"])
        come = hop(sent, "shard", 1)
    weights_a = jnp.concatenate([in_rows(0), attention_out[0]])
    weights_a = shard_parts(tie(weights_a, come) if split else weights_a)
    start_t, unit_a = prog.temporal_start(clips, come, moves["beginning"])
    units_a = to_all(unit_a, "tensor")
    gather_c.columns(unit_a)
    gather_c.rows()

    qkv_a, mixed_a, normed_a, parts = prog.temporal(
        units_a, weights_a, along, shift_a, gather_c.far[:1]
    )
    fc = shard_parts(tie(temporal_fc, parts[0]), 0)
    if split:
        others = hop(tie(others, parts[0]), "shard", 1)
    temporal_t = prog.temporal_out(
        swapped(parts, "tensor"), along, moves.get("return_far"), gather_c.far[-1:]
    )
    in_b = jnp.concatenate([in_rows(1), jnp.pad(bias_rows(1), ((0, 15), (0, 0)))])
    in_b = hop_group(tie(in_b, temporal_t[0]))
    weights_b = shard_parts(in_b)
    shift_b = bias_of(weights_b, 3 * group)
    sources = [temporal_t[0]] + [hop(rows, "shard", 1) for rows in temporal_t[1:]]

    start = prog.frames_of(clips, others, 0, moves["starting"])
    after_a, temporal, normed_b = prog.spatial_in(
        sources, moves["returning"], start, fc, along
    )
    normed_b = to_all(normed_b, "context")
    qkv_b, mixed = prog.spatial(normed_b, weights_b, shift_b)
    mixed = swapped(mixed, "context")
    grad = prog.frames_of(cotangents, others, 1, moves["starting"], [after_a])
    pieces_c = gather_c.cores(after_a)
    line = gather_c.first[:, 2 * unit + piece].astype(F32)
    up_shift = line.reshape((ranks, shards) + hidden_bias.shape)
    if place.paired:
        up_shift = jnp.where(shard == 0, up_shift, up_shift[:, ::-1])
    up_shift = jnp.swapaxes(up_shift, 1, 2).reshape(ranks, quarters, unit)
    up_shift = [pick(up_shift, context ^ j, 1).reshape(1, -1) for j in range(quarters)]
    after_b, normed_c, low, wout_b = prog.spatial_out(
        mixed, pieces_c, 2 * unit, after_a, grad, along
    )

    totals = None
    piece_grads, up_bias_grads = [None] * quarters, [None] * quarters
    for pair in ((1, 3), (0, 2)):
        totals, grads, sums = prog.feed_forward(
            normed_c, low, [pieces_c[j] for j in pair], [up_shift[j] for j in pair], totals
        )
        for index, j in enumerate(pair):
            piece_grads[j] = grads[index]
            up_bias_grads[j] = sums[index]
    reduce_c = ReduceHidden(place, piece_grads)
    kept, mixed_grads = prog.feed_forward_back(
        after_b, totals[0], totals[1], grad, mixed, wout_b, along
    )
    layer_rows, total, sums_c, wout_grad = kept
    wait = reduce_c.cores(layer_rows)

    mixed_grads = swapped(mixed_grads, "context")
    qkv_grads, backs = prog.spatial_back(qkv_b, mixed_grads, weights_b, wait)
    done = backs[0]
    backs = swapped(backs, "context")
    group_grads = prog.group_weights(qkv_grads, normed_b)
    low_total, temporal_grad, sums_b, *sent = prog.spatial_input(
        backs, after_a, total, along, fc, moves.get("arrive_far"), [group_grads[0]] + reduce_c.legs(done)
    )

    sources = [temporal_grad] + [hop(rows, "shard", 1) for rows in sent]
    out_grad = prog.temporal_grad(sources, moves["arriving"], reduce_c.both(low_total))
    out_grads = to_all(out_grad, "tensor")
    layer_out, home = [(moves["ending"], [layer_rows])], [(moves["ending"], [low_total])]
    if split:
        far = hop(tie(jnp.concatenate([layer_rows[lay.own :], low_total[lay.own :]]), out_grad), "shard", 1)
        layer_out.append((moves["end_far"], [far[: far.shape[0] // 2]]))
        home.append((moves["end_far"], [far[far.shape[0] // 2 :]]))
    layer_out = prog.natural(layer_out, [out_grad])
    part_in_b = sum_columns(place, group_grads[0], group_grads[-1], out_grads[1])
    sums = [sums_b[0], sums_c[0], sums_b[1], sums_c[1], sums_b[2], sums_b[3], sums_c[2], sums_c[3]]
    outer = ordered([item.reshape(ranks, -1) for item in up_bias_grads], context, 1)
    outer = outer.reshape(ranks, -1, shards, hidden_bias.shape[1])
    outer = jnp.swapaxes(outer, 1, 2).reshape(ranks, 1, width)
    sums = jnp.stack(sums)
    vectors = jnp.concatenate([jnp.broadcast_to(sums, (ranks,) + sums.shape), outer], 1)
    if place.paired:
        flipped = jnp.concatenate([vectors[..., columns:], vectors[..., :columns]], -1)
        vectors = jnp.where(shard == 0, vectors, flipped)
    vectors = jnp.pad(vectors, ((0, 0), (0, 16 - vectors.shape[1]), (0, 0))).astype(LOW)
    pieces = prog.out_weights(wout_grad, low_total, temporal, vectors, [out_grad])
    reduce_out = ReduceShared(place, pieces, piece + vectors.shape[1])
    wait = reduce_out.cores(out_grads[1]) + [part_in_b, layer_out]
    total_in_b = hop_group(part_in_b)
    qkv_grads, backs, sums_a = prog.temporal_back(qkv_a, out_grads, units_a, weights_a, wait)
    done = backs[0]
    backs = swapped(backs, "tensor")
    for step in (1, 2):
        sums_a = sums_a + hop(sums_a, "tensor", step)
    group_grads = prog.group_weights(qkv_grads, normed_a, mixed_a, out_grads, [sums_a])
    total_in_a = sum_columns(place, group_grads[0], group_grads[-1])
    sum_in = SumContext(place, jnp.concatenate([total_in_a, tie(total_in_b, done)]))
    wait = reduce_out.rows(backs[1]) + reduce_c.hops(done) + reduce_out.columns(backs[1])
    total_c = reduce_c.finish()
    wait += sum_in.cores(backs[1]) + [total_c]
    back, *sent = prog.temporal_input(
        backs, start_t, along, moves.get("home_far"), wait
    )
    home.append((moves["homing"], [back] + [hop(rows, "shard", 1) for rows in sent]))
    input_grad = prog.natural(home, last=True)

    total_in = sum_in.finish()
    total_in_a, total_in_b = total_in[: total_in_a.shape[0]], total_in[total_in_a.shape[0] :]
    reduce_out.hops()
    total_out = reduce_out.finish()

    def in_grad(total):
        part = total[: 3 * group].reshape(3, group, columns)
        return jnp.transpose(part, (2, 0, 1))

    def bias_grad(line):
        part = HEAD_DIM // shards
        if place.paired:
            return pick(line.reshape(2, heads, shards, part), shard, 2)
        return line[: 2 * heads * part].reshape(2, heads, part)

    in_total = jnp.stack([in_grad(total_in_a), in_grad(total_in_b)])
    inner = jnp.stack([bias_grad(total_in_a[4 * group]), bias_grad(total_in_b[3 * group])])
    out_b = total_out[:, :piece].reshape(group, columns)
    out_total = jnp.stack([total_in_a[3 * group : 4 * group], out_b])
    fc_total = total_out[:, -(width // quarters) :].reshape(width, columns).T
    vectors = total_out[0, piece:]
    sums_a = total_in_a[4 * group + 16 : 4 * group + 18]
    gains = jnp.concatenate([sums_a[:1], vectors[0:2]])
    shifts = jnp.concatenate([sums_a[1:], vectors[2:4]])
    rows_shape = clip_input.shape
    return (
        layer_out.reshape(rows_shape),
        input_grad.reshape(rows_shape),
        gains,
        shifts,
        in_total,
        inner,
        out_total,
        vectors[4:8],
        fc_total,
        total_c[:, :unit].reshape(hidden, columns).T,
        vectors[8].reshape(hidden_bias.shape),
        total_c[:, unit:].reshape(hidden, columns),
    )


def solution(mesh):
    rows = P(None, "shard", "tensor", "context", None)
    weights = (
        P(None, "shard"),
        P(None, "shard"),
        P(None, "shard", None, "tensor"),
        P(None, None, "tensor", "shard"),
        P(None, "tensor", "shard"),
        P(None, "shard"),
        P("shard", None),
        P("shard", "tensor"),
        P("tensor", "shard"),
        P("tensor", "shard"),
    )
    return jax.shard_map(
        body,
        mesh=mesh,
        in_specs=(rows, P(None, "shard")) + weights + (rows,),
        out_specs=(rows, rows) + weights,
        check_vma=False,
    )
```

time: 965 us -> 488 us (0.51)
  local copies, waits for them, and re-layouts: 241 us -> 57.6 us
  waiting for transfers between devices: 282 us -> 130 us
  Pallas kernels: 0 us -> 129 us
  matrix products: 99.2 us -> 0 us
  blocking collectives: 57 us -> 0 us
  other arithmetic: 102 us -> 48.5 us
  starting transfers between devices: 158 us -> 111 us
  between operations: 17.7 us -> 1.97 us
    pallas_call x0 -> x22, Pallas kernels: none -> 129 us  [call(): pl.pallas_call(body, name=name, out_shape=tuple(outs), in_specs=[pl.Block...]
    ppermute x164 -> x69, waiting for transfers between devices: 236 us -> 130 us  [hop(): return lax.ppermute(values, axis, [(i, i ^ step) for i in range(count)])]
    dot_general x49 -> x0, matrix products: 91.8 us -> none  [dot(): return jnp.einsum(form, first, second, preferred_element_type=F32)]
    ppermute x164 -> x69, starting transfers between devices: 158 us -> 95.4 us  [hop(): return lax.ppermute(values, axis, [(i, i ^ step) for i in range(count)])]
    psum x1 -> x0, waiting for transfers between devices: 46 us -> none  [body(): lax.psum(scatter_columns(place, fc_grad.T).T, ('context', 'tensor'))]
    another operation x59 -> x12, local copies, waits for them, and re-layouts: 45.3 us -> 1.42 us  [the longest x1 0.67 us: body(): vectors[8].reshape(hidden_bias.shape)]
    psum x1 -> x0, blocking collectives: 38.9 us -> none  [body(): lax.psum(jnp.concatenate([along, inner, outer]), ('shard', 'context', 'te...]
    slice x65 -> x39, local copies, waits for them, and re-layouts: 55.3 us -> 18.9 us  [the longest x7 7.61 us: matrices(): target, source = (labels[at:ends[0]], labels[ends[0]:ends[1]])]
  transfers between devices with their start and end apart: 165 -> 71, of which waited for: 56 -> 23; matrix products, arithmetic and copies ran while one was open for 42% -> 18% of each run, Pallas kernels for 0% -> 23%
where the time goes in v4:
time: 488 us; the launch traced here: 479 us
  waiting for transfers between devices  130 us (27%)
  Pallas kernels  129 us (26%)
  starting transfers between devices  111 us (23%)
  local copies, waits for them, and re-layouts  57.6 us (12%)
  other arithmetic  48.5 us (10%)
    ppermute x69, waiting for transfers between devices, hop(): return lax.ppermute(values, axis, [(i, i ^ step) for i in range(count)])  130 us
    pallas_call x22, Pallas kernels, call(): pl.pallas_call(body, name=name, out_shape=tuple(outs), in_specs=[pl.Block...  129 us
    ppermute x69, starting transfers between devices, hop(): return lax.ppermute(values, axis, [(i, i ^ step) for i in range(count)])  95.4 us
    unnamed x148, local copies, waits for them, and re-layouts  21.4 us
    convert_element_type x12, other arithmetic, add(): return total.astype(LOW)  17 us
    ppermute x2, starting transfers between devices, hop_group(): return lax.ppermute(values, ('context', 'tensor'), pairs)  16 us
  transfers between devices with their start and end apart: 71, of which 23 were waited for; matrix products, arithmetic and copies ran while one was open for 18% of the time, Pallas kernels for 23%

profile of v4, /device:TPU:0, one launch (start us, length us, event | category | flops | bytes accessed | tf_op | source)
XLA Modules:
  0.0 478.7 jit_solution(15951479035294215636)
XLA Ops:
  37.3 6.6 %collective-permute-start.1 = (bf16[256,768]{1,0:T(8,128)(2,1)S(1)}, bf16[256,768]{1,0:T(8,128)(2,1)}, u32[]{:S(2)}, u32[]{:S(2)}) collective-permute-start(bf16[256,768]{1,0:T(8,128)(2,1)S(1)} %copy-done.55), channel_id=1, source_target_pairs={{0,1},{1,0},{2,3},{3,2},{4,5},{5,4},{6,7},{7,6},{8,9},{9,8},{10,11... | collective-permute-start | bytes 1179656 | tf_op jit(solution)/shard_map/ppermute | solution.py:46
  46.9 10.8 %collective-permute-done.1.refs_1_.refs_9_ = bf16[256,768]{1,0:T(8,128)(2,1)} collective-permute-done((bf16[256,768]{1,0:T(8,128)(2,1)S(1)}, bf16[256,768]{1,0:T(8,128)(2,1)}, u32[]{:S(2)}, u32[]{:S(2)}) %collective-permute-start.1) | collective-permute-done | bytes 393248 | tf_op jit(solution)/shard_map/ppermute | solution.py:46
  60.8 7.4 %collective-permute-done.13 = bf16[4,448,384]{2,1,0:T(8,128)(2,1)} collective-permute-done((bf16[4,448,384]{2,1,0:T(8,128)(2,1)S(1)}, bf16[4,448,384]{2,1,0:T(8,128)(2,1)}, u32[]{:S(2)}, u32[]{:S(2)}) %collective-permute-start.13) | collective-permute-done | bytes 1376288 | tf_op jit(solution)/shard_map/ppermute | solution.py:46
  68.7 5.9 %collective-permute-done.2.refs_2_.refs_10_ = bf16[256,768]{1,0:T(8,128)(2,1)S(1)} collective-permute-done((bf16[256,768]{1,0:T(8,128)(2,1)S(1)}, bf16[256,768]{1,0:T(8,128)(2,1)S(1)}, u32[]{:S(2)}, u32[]{:S(2)}) %collective-permute-start.2) | collective-permute-done | bytes 393248 | tf_op jit(solution)/shard_map/ppermute | solution.py:46
  77.6 9.7 %temporal.1 = (bf16[256,576]{1,0:T(8,128)(2,1)}, bf16[256,576]{1,0:T(8,128)(2,1)}, bf16[256,576]{1,0:T(8,128)(2,1)}, bf16[256,576]{1,0:T(8,128)(2,1)}, bf16[256,...) custom-call(s32[7]{0:T(128)} %pad_add_fusion.scalars, ...), custom_call_target="tpu_custom_call" | custom-call | flops 34500001792 | bytes 7766272 | tf_op jit(solution)/shard_map/temporal/pallas_call | solution.py:369
  87.4 7.1 %collective-permute-start.10 = (bf16[256,768]{1,0:T(8,128)(2,1)}, bf16[256,768]{1,0:T(8,128)(2,1)S(1)}, u32[]{:S(2)}, u32[]{:S(2)}) collective-permute-start(bf16[256,768]{1,0:T(8,128)(2,1)} %get-tuple-element.137), channel_id=1, source_target_pairs={{0,1},{1,0},{2,3},{3,2},{4,5},{5,4},{6,7},{7,6},{8,9},{9,8},{10,11... | collective-permute-start | bytes 1179656 | tf_op jit(solution)/shard_map/ppermute | solution.py:46
  99.5 8.5 %collective-permute-done.10.refs_1_ = bf16[256,768]{1,0:T(8,128)(2,1)S(1)} collective-permute-done((bf16[256,768]{1,0:T(8,128)(2,1)}, bf16[256,768]{1,0:T(8,128)(2,1)S(1)}, u32[]{:S(2)}, u32[]{:S(2)}) %collective-permute-start.10) | collective-permute-done | bytes 393248 | tf_op jit(solution)/shard_map/ppermute | solution.py:46
  109.4 15.1 %collective-permute-done.11.refs_2_ = bf16[256,768]{1,0:T(8,128)(2,1)S(1)} collective-permute-done((bf16[256,768]{1,0:T(8,128)(2,1)}, bf16[256,768]{1,0:T(8,128)(2,1)S(1)}, u32[]{:S(2)}, u32[]{:S(2)}) %collective-permute-start.11) | collective-permute-done | bytes 393248 | tf_op jit(solution)/shard_map/ppermute | solution.py:46
  132.8 10.8 %collective-permute-start.21 = (bf16[592,384]{1,0:T(8,128)(2,1)S(1)}, bf16[592,384]{1,0:T(8,128)(2,1)S(1)}, u32[]{:S(2)}, u32[]{:S(2)}) collective-permute-start(bf16[592,384]{1,0:T(8,128)(2,1)S(1)} %fusion.11), channel_id=1, source_target_pairs={{0,0},{1,1},{2,2},{3,3},{4,6},{5,7},{6,4},{7,5},{8,9},{9,8},{10,11... | collective-permute-start | bytes 1363976 | tf_op jit(solution)/shard_map/ppermute | solution.py:54
  148.7 10.3 %collective-permute-start.19 = (bf16[256,768]{1,0:T(8,128)(2,1)}, bf16[256,768]{1,0:T(8,128)(2,1)S(1)}, u32[]{:S(2)}, u32[]{:S(2)}) collective-permute-start(bf16[256,768]{1,0:T(8,128)(2,1)} %get-tuple-element.145.refs_0_.refs_4_), channel_id=1, source_target_pairs={{0,8},{4,12},{8,0},{12,4},{1,9},{5,13},{9,1},{13,5},{2,10},{6,14},... | collective-permute-start | bytes 1179656 | tf_op jit(solution)/shard_map/ppermute | solution.py:46
  170.5 6.8 %collective-permute-done.22.refs_5_.refs_9_ = bf16[592,384]{1,0:T(8,128)(2,1)S(1)} collective-permute-done((bf16[592,384]{1,0:T(8,128)(2,1)S(1)}, bf16[592,384]{1,0:T(8,128)(2,1)S(1)}, u32[]{:S(2)}, u32[]{:S(2)}) %collective-permute-start.22) | collective-permute-done | bytes 454688 | tf_op jit(solution)/shard_map/ppermute | solution.py:46
  179.8 9.4 %spatial.1 = (bf16[256,576]{1,0:T(8,128)(2,1)}, bf16[256,576]{1,0:T(8,128)(2,1)}, bf16[256,576]{1,0:T(8,128)(2,1)}, bf16[256,576]{1,0:T(8,128)(2,1)}, bf16[256,1...) custom-call(s32[7]{0:T(128)} %pad_add_fusion.scalars, ...), custom_call_target="tpu_custom_call" | custom-call | flops 23000000512 | bytes 4057344 | tf_op jit(solution)/shard_map/spatial/pallas_call | solution.py:369
  202.6 13.5 %feed_forward.2 = (f32[256,768]{1,0:T(8,128)}, f32[256,768]{1,0:T(8,128)}, bf16[4,384,768]{2,1,0:T(8,128)(2,1)}, bf16[4,384,768]{2,1,0:T(8,128)(2,1)}, f32[1,768]{1,0:T(1,128)}, /*index=5*/f32[1,768]{1,0:T(1,128)}) custom-call(s32[7]{0:T(128)} %pad_add_fusion.scalars, bf16[256,768]{1,0:T(8,128)(2,1)} %get-tuple-element.157.normed_ref, ...), custom_call_target="tpu_custom_call" | custom-call | flops 29899999232 | bytes 12595200 | tf_op jit(solution)/shard_map/feed_forward/pallas_call | solution.py:369
  216.7 13.9 %feed_forward.3 = (f32[256,768]{1,0:T(8,128)}, f32[256,768]{1,0:T(8,128)}, bf16[4,384,768]{2,1,0:T(8,128)(2,1)}, bf16[4,384,768]{2,1,0:T(8,128)(2,1)}, f32[1,768]{1,0:T(1,128)}, /*index=5*/f32[1,768]{1,0:T(1,128)}) custom-call(s32[7]{0:T(128)} %pad_add_fusion.scalars, bf16[256,768]{1,0:T(8,128)(2,1)} %get-tuple-element.157.normed_ref, ...), custom_call_target="tpu_custom_call" | custom-call | flops 29899999232 | bytes 14168064 | tf_op jit(solution)/shard_map/feed_forward/pallas_call | solution.py:369
  248.7 13.7 %spatial_back.1 = (bf16[256,576]{1,0:T(8,128)(2,1)}, bf16[256,576]{1,0:T(8,128)(2,1)}, bf16[256,576]{1,0:T(8,128)(2,1)}, bf16[256,576]{1,0:T(8,128)(2,1)}, bf16[...) custom-call(s32[7]{0:T(128)} %pad_add_fusion.scalars, ...), custom_call_target="tpu_custom_call" | custom-call | flops 32199999488 | bytes 5234688 | tf_op jit(solution)/shard_map/spatial_back/pallas_call | solution.py:369
  268.4 4.9 %collective-permute-done.37 = bf16[4,192,768]{2,1,0:T(8,128)(2,1)} collective-permute-done((bf16[4,192,768]{2,1,0:T(8,128)(2,1)}, bf16[4,192,768]{2,1,0:T(8,128)(2,1)}, u32[]{:S(2)}, u32[]{:S(2)}) %collective-permute-start.37) | collective-permute-done | bytes 1179680 | tf_op jit(solution)/shard_map/ppermute | solution.py:46
  281.8 7.7 %collective-permute-done.35.refs_3_ = bf16[256,768]{1,0:T(8,128)(2,1)} collective-permute-done((bf16[256,768]{1,0:T(8,128)(2,1)}, bf16[256,768]{1,0:T(8,128)(2,1)}, u32[]{:S(2)}, u32[]{:S(2)}) %collective-permute-start.35) | collective-permute-done | bytes 393248 | tf_op jit(solution)/shard_map/ppermute | solution.py:46
  338.3 17.6 %collective-permute-done.43.refs_6_.refs_14_ = bf16[256,768]{1,0:T(8,128)(2,1)} collective-permute-done((bf16[256,768]{1,0:T(8,128)(2,1)S(1)}, bf16[256,768]{1,0:T(8,128)(2,1)}, u32[]{:S(2)}, u32[]{:S(2)}) %collective-permute-start.43) | collective-permute-done | bytes 393248 | tf_op jit(solution)/shard_map/ppermute | solution.py:46
  355.9 13.2 %temporal_back.1 = (bf16[256,576]{1,0:T(8,128)(2,1)}, bf16[256,576]{1,0:T(8,128)(2,1)}, bf16[256,576]{1,0:T(8,128)(2,1)}, bf16[256,576]{1,0:T(8,128)(2,1)}, bf16...) custom-call(s32[7]{0:T(128)} %pad_add_fusion.scalars, ...), custom_call_target="tpu_custom_call" | custom-call | flops 80499998720 | bytes 8544256 | tf_op jit(solution)/shard_map/temporal_back/pallas_call | solution.py:369
  369.1 9.0 %collective-permute-start.56 = (f32[8,768]{1,0:T(8,128)}, f32[8,768]{1,0:T(8,128)S(1)}, u32[]{:S(2)}, u32[]{:S(2)}) collective-permute-start(f32[8,768]{1,0:T(8,128)} %get-tuple-element.239), channel_id=1, source_target_pairs={{0,1},{1,0},{2,3},{3,2},{4,5},{5,4},{6,7},{7,6},{8,9},{9,8},{10,11... | collective-permute-start | bytes 73736 | tf_op jit(solution)/shard_map/ppermute | solution.py:46
  384.6 5.2 %collective-permute-start.59 = (bf16[608,384]{1,0:T(8,128)(2,1)}, bf16[608,384]{1,0:T(8,128)(2,1)}, u32[]{:S(2)}, u32[]{:S(2)}) collective-permute-start(bf16[608,384]{1,0:T(8,128)(2,1)} %add_convert_fusion.15.refs_17_), channel_id=1, source_target_pairs={{0,0},{1,1},{2,2},{3,3},{4,6},{5,7},{6,4},{7,5},{8,9},{9,8},{10,11... | collective-permute-start | bytes 1400840 | tf_op jit(solution)/shard_map/ppermute | solution.py:54
  390.5 5.0 %group_weights.3 = (bf16[800,384]{1,0:T(8,128)(2,1)}, bf16[800,384]{1,0:T(8,128)(2,1)}) custom-call(s32[7]{0:T(128)} %pad_add_fusion.scalars, bf16[256,576]{1,0:T(8,128)(2,1)} %get-tuple-element.227.refs_0_, bf16[256,576]{1,0:T(8,128)(2,1)} %get-tuple-element.228.refs_1_, bf16[256,576]{1,0:T(8,128)(2,1)} %get-tuple-element.229.refs_2_, ...), custom_call_target="tpu_custom_call" | custom-call | flops 230000000 | bytes 6561792 | tf_op jit(solution)/shard_map/group_weights/pallas_call | solution.py:369
  420.0 6.1 %collective-permute-done.55 = bf16[448,384]{1,0:T(8,128)(2,1)S(1)} collective-permute-done((bf16[448,384]{1,0:T(8,128)(2,1)S(1)}, bf16[448,384]{1,0:T(8,128)(2,1)S(1)}, u32[]{:S(2)}, u32[]{:S(2)}) %collective-permute-start.55) | collective-permute-done | bytes 344096 | tf_op jit(solution)/shard_map/ppermute | solution.py:46
  439.4 10.9 %collective-permute-done.67 = bf16[256,384]{1,0:T(8,128)(2,1)S(1)} collective-permute-done((bf16[256,384]{1,0:T(8,128)(2,1)S(1)}, bf16[256,384]{1,0:T(8,128)(2,1)S(1)}, u32[]{:S(2)}, u32[]{:S(2)}) %collective-permute-start.67) | collective-permute-done | bytes 196640 | tf_op jit(solution)/shard_map/ppermute | solution.py:46
  (468 shorter events, 247.4 us)
Async XLA Ops:
  3.4 29.1 %collective-permute-start.6 = (bf16[448,384]{1,0:T(8,128)(2,1)S(1)}, bf16[448,384]{1,0:T(8,128)(2,1)S(1)}, u32[]{:S(2)}, u32[]{:S(2)}) collective-permute-start(bf16[448,384]{1,0:T(8,128)(2,1)S(1)} %fusion.12), channel_id=1, source_target_pairs={{0,1},{1,0},{2,3},{3,2},{4,5},{5,4},{6,7},{7,6},{8,9},{9,8},{10,11... | collective-permute-start | bytes 1032200 | tf_op jit(solution)/shard_map/ppermute | solution.py:46
  6.5 26.6 %collective-permute-start.7 = (bf16[448,384]{1,0:T(8,128)(2,1)S(1)}, bf16[448,384]{1,0:T(8,128)(2,1)S(1)}, u32[]{:S(2)}, u32[]{:S(2)}) collective-permute-start(bf16[448,384]{1,0:T(8,128)(2,1)S(1)} %fusion.12), channel_id=1, source_target_pairs={{0,2},{1,3},{2,0},{3,1},{4,6},{5,7},{6,4},{7,5},{8,10},{9,11},{10,... | collective-permute-start | bytes 1032200 | tf_op jit(solution)/shard_map/ppermute | solution.py:46
  33.4 44.2 %collective-permute-start.9 = (bf16[4,448,384]{2,1,0:T(8,128)(2,1)S(1)}, bf16[4,448,384]{2,1,0:T(8,128)(2,1)}, u32[]{:S(2)}, u32[]{:S(2)}) collective-permute-start(bf16[4,448,384]{2,1,0:T(8,128)(2,1)S(1)} %pad_maximum_fusion.2), channel_id=1, source_target_pairs={{0,8},{4,12},{8,0},{12,4},{1,9},{5,13},{9,1},{13,5},{2,10},{6,14},... | collective-permute-start | bytes 4128776 | tf_op jit(solution)/shard_map/ppermute | solution.py:46
  35.0 33.2 %collective-permute-start.13 = (bf16[4,448,384]{2,1,0:T(8,128)(2,1)S(1)}, bf16[4,448,384]{2,1,0:T(8,128)(2,1)}, u32[]{:S(2)}, u32[]{:S(2)}) collective-permute-start(bf16[4,448,384]{2,1,0:T(8,128)(2,1)S(1)} %pad_maximum_fusion.2), channel_id=1, source_target_pairs={{0,16},{16,0},{1,17},{17,1},{2,18},{18,2},{3,19},{19,3},{4,20},{20... | collective-permute-start | bytes 4128776 | tf_op jit(solution)/shard_map/ppermute | solution.py:46
  45.0 32.6 %collective-permute-start.4 = (bf16[768,384]{1,0:T(8,128)(2,1)S(1)}, bf16[768,384]{1,0:T(8,128)(2,1)}, u32[]{:S(2)}, u32[]{:S(2)}) collective-permute-start(bf16[768,384]{1,0:T(8,128)(2,1)S(1)} %pad_maximum_fusion.5.refs_4_.refs_12_), channel_id=1, source_target_pairs={{0,16},{16,0},{1,17},{17,1},{2,18},{18,2},{3,19},{19,3},{4,20},{20... | collective-permute-start | bytes 1769480 | tf_op jit(solution)/shard_map/ppermute | solution.py:46
  45.8 28.9 %collective-permute-start.2 = (bf16[256,768]{1,0:T(8,128)(2,1)S(1)}, bf16[256,768]{1,0:T(8,128)(2,1)S(1)}, u32[]{:S(2)}, u32[]{:S(2)}) collective-permute-start(bf16[256,768]{1,0:T(8,128)(2,1)S(1)} %copy-done.55), channel_id=1, source_target_pairs={{0,2},{1,3},{2,0},{3,1},{4,6},{5,7},{6,4},{7,5},{8,10},{9,11},{10,... | collective-permute-start | bytes 1179656 | tf_op jit(solution)/shard_map/ppermute | solution.py:46
  68.2 56.3 %collective-permute-start.14 = (bf16[4,448,384]{2,1,0:T(8,128)(2,1)}, bf16[4,448,384]{2,1,0:T(8,128)(2,1)}, u32[]{:S(2)}, u32[]{:S(2)}) collective-permute-start(bf16[4,448,384]{2,1,0:T(8,128)(2,1)} %collective-permute-done.13), channel_id=1, source_target_pairs={{0,8},{4,12},{8,0},{12,4},{1,9},{5,13},{9,1},{13,5},{2,10},{6,14},... | collective-permute-start | bytes 4128776 | tf_op jit(solution)/shard_map/ppermute | solution.py:46
  94.5 30.0 %collective-permute-start.11 = (bf16[256,768]{1,0:T(8,128)(2,1)}, bf16[256,768]{1,0:T(8,128)(2,1)S(1)}, u32[]{:S(2)}, u32[]{:S(2)}) collective-permute-start(bf16[256,768]{1,0:T(8,128)(2,1)} %get-tuple-element.138), channel_id=1, source_target_pairs={{0,2},{1,3},{2,0},{3,1},{4,6},{5,7},{6,4},{7,5},{8,10},{9,11},{10,... | collective-permute-start | bytes 1179656 | tf_op jit(solution)/shard_map/ppermute | solution.py:46
  95.6 28.9 %collective-permute-start.12 = (bf16[256,768]{1,0:T(8,128)(2,1)}, bf16[256,768]{1,0:T(8,128)(2,1)}, u32[]{:S(2)}, u32[]{:S(2)}) collective-permute-start(bf16[256,768]{1,0:T(8,128)(2,1)} %get-tuple-element.139), channel_id=1, source_target_pairs={{0,3},{1,2},{2,1},{3,0},{4,7},{5,6},{6,5},{7,4},{8,11},{9,10},{10,... | collective-permute-start | bytes 1179656 | tf_op jit(solution)/shard_map/ppermute | solution.py:46
  98.0 31.3 %collective-permute-start.16 = (bf16[2,3,49,768]{3,2,1,0:T(8,128)(2,1)}, bf16[2,3,49,768]{3,2,1,0:T(8,128)(2,1)S(1)}, u32[]{:S(2)}, u32[]{:S(2)}) collective-permute-start(bf16[2,3,49,768]{3,2,1,0:T(8,128)(2,1)} %get-tuple-element.143), channel_id=1, source_target_pairs={{0,16},{16,0},{1,17},{17,1},{2,18},{18,2},{3,19},{19,3},{4,20},{20... | collective-permute-start | bytes 1354760 | tf_op jit(solution)/shard_map/ppermute | solution.py:46
  107.9 35.7 %collective-permute-start.17 = (bf16[384,768]{1,0:T(8,128)(2,1)}, bf16[384,768]{1,0:T(8,128)(2,1)S(1)}, u32[]{:S(2)}, u32[]{:S(2)}) collective-permute-start(bf16[384,768]{1,0:T(8,128)(2,1)} %refs_7_), channel_id=1, source_target_pairs={{0,16},{16,0},{1,17},{17,1},{2,18},{18,2},{3,19},{19,3},{4,20},{20... | collective-permute-start | bytes 1769480 | tf_op jit(solution)/shard_map/ppermute | solution.py:46
  132.8 32.1 %collective-permute-start.21 = (bf16[592,384]{1,0:T(8,128)(2,1)S(1)}, bf16[592,384]{1,0:T(8,128)(2,1)S(1)}, u32[]{:S(2)}, u32[]{:S(2)}) collective-permute-start(bf16[592,384]{1,0:T(8,128)(2,1)S(1)} %fusion.11), channel_id=1, source_target_pairs={{0,0},{1,1},{2,2},{3,3},{4,6},{5,7},{6,4},{7,5},{8,9},{9,8},{10,11... | collective-permute-start | bytes 1363976 | tf_op jit(solution)/shard_map/ppermute | solution.py:54
  164.4 33.4 %collective-permute-start.27 = (bf16[4,448,768]{2,1,0:T(8,128)(2,1)}, bf16[4,448,768]{2,1,0:T(8,128)(2,1)}, u32[]{:S(2)}, u32[]{:S(2)}) collective-permute-start(bf16[4,448,768]{2,1,0:T(8,128)(2,1)} %constant_dynamic-update-slice_fusion.2.refs_6_.refs_1_), channel_id=1, source_target_pairs={{0,4},{4,0},{8,12},{12,8},{1,5},{5,1},{9,13},{13,9},{2,6},{6,2},{1... | collective-permute-start | bytes 8257544 | tf_op jit(solution)/shard_map/ppermute | solution.py:46
  168.9 28.9 %collective-permute-start.26 = (bf16[4,448,768]{2,1,0:T(8,128)(2,1)}, bf16[4,448,768]{2,1,0:T(8,128)(2,1)}, u32[]{:S(2)}, u32[]{:S(2)}) collective-permute-start(bf16[4,448,768]{2,1,0:T(8,128)(2,1)} %constant_dynamic-update-slice_fusion.refs_4_.refs_0_), channel_id=1, source_target_pairs={{0,4},{4,0},{8,12},{12,8},{1,5},{5,1},{9,13},{13,9},{2,6},{6,2},{1... | collective-permute-start | bytes 8257544 | tf_op jit(solution)/shard_map/ppermute | solution.py:46
  244.2 29.1 %collective-permute-start.37 = (bf16[4,192,768]{2,1,0:T(8,128)(2,1)}, bf16[4,192,768]{2,1,0:T(8,128)(2,1)}, u32[]{:S(2)}, u32[]{:S(2)}) collective-permute-start(bf16[4,192,768]{2,1,0:T(8,128)(2,1)} %add_convert_fusion.1.refs_11_), channel_id=1, source_target_pairs={{0,8},{4,12},{8,0},{12,4},{1,9},{5,13},{9,1},{13,5},{2,10},{6,14},... | collective-permute-start | bytes 3538952 | tf_op jit(solution)/shard_map/ppermute | solution.py:46
  247.8 29.2 %collective-permute-start.36 = (bf16[2,4,192,384]{3,2,1,0:T(8,128)(2,1)}, bf16[2,4,192,384]{3,2,1,0:T(8,128)(2,1)}, u32[]{:S(2)}, u32[]{:S(2)}) collective-permute-start(bf16[2,4,192,384]{3,2,1,0:T(8,128)(2,1)} %pad_maximum_fusion.3.refs_10_), channel_id=1, source_target_pairs={{0,16},{16,0},{1,17},{17,1},{2,18},{18,2},{3,19},{19,3},{4,20},{20... | collective-permute-start | bytes 3538952 | tf_op jit(solution)/shard_map/ppermute | solution.py:46
  273.3 44.0 %collective-permute-start.47 = (bf16[608,384]{1,0:T(8,128)(2,1)}, bf16[608,384]{1,0:T(8,128)(2,1)}, u32[]{:S(2)}, u32[]{:S(2)}) collective-permute-start(bf16[608,384]{1,0:T(8,128)(2,1)} %get-tuple-element.215), channel_id=1, source_target_pairs={{0,16},{16,0},{1,17},{17,1},{2,18},{18,2},{3,19},{19,3},{4,20},{20... | collective-permute-start | bytes 1400840 | tf_op jit(solution)/shard_map/ppermute | solution.py:46
  312.4 43.5 %collective-permute-start.43 = (bf16[256,768]{1,0:T(8,128)(2,1)S(1)}, bf16[256,768]{1,0:T(8,128)(2,1)}, u32[]{:S(2)}, u32[]{:S(2)}) collective-permute-start(bf16[256,768]{1,0:T(8,128)(2,1)S(1)} %copy-done.4), channel_id=1, source_target_pairs={{0,2},{1,3},{2,0},{3,1},{4,6},{5,7},{6,4},{7,5},{8,10},{9,11},{10,... | collective-permute-start | bytes 1179656 | tf_op jit(solution)/shard_map/ppermute | solution.py:46
  317.3 38.6 %collective-permute-start.44 = (bf16[256,768]{1,0:T(8,128)(2,1)S(1)}, bf16[256,768]{1,0:T(8,128)(2,1)}, u32[]{:S(2)}, u32[]{:S(2)}) collective-permute-start(bf16[256,768]{1,0:T(8,128)(2,1)S(1)} %copy-done.4), channel_id=1, source_target_pairs={{0,3},{1,2},{2,1},{3,0},{4,7},{5,6},{6,5},{7,4},{8,11},{9,10},{10,... | collective-permute-start | bytes 1179656 | tf_op jit(solution)/shard_map/ppermute | solution.py:46
  324.8 65.0 %collective-permute-start.52 = (bf16[384,384]{1,0:T(8,128)(2,1)}, bf16[384,384]{1,0:T(8,128)(2,1)S(1)}, u32[]{:S(2)}, u32[]{:S(2)}) collective-permute-start(bf16[384,384]{1,0:T(8,128)(2,1)} %get-tuple-element.301), channel_id=1, source_target_pairs={{0,1},{1,0},{2,3},{3,2},{4,5},{5,4},{6,7},{7,6},{8,9},{9,8},{10,11... | collective-permute-start | bytes 884744 | tf_op jit(solution)/shard_map/ppermute | solution.py:46
  330.6 59.2 %collective-permute-start.53 = (bf16[384,384]{1,0:T(8,128)(2,1)}, bf16[384,384]{1,0:T(8,128)(2,1)S(1)}, u32[]{:S(2)}, u32[]{:S(2)}) collective-permute-start(bf16[384,384]{1,0:T(8,128)(2,1)} %get-tuple-element.302), channel_id=1, source_target_pairs={{0,2},{1,3},{2,0},{3,1},{4,6},{5,7},{6,4},{7,5},{8,10},{9,11},{10,... | collective-permute-start | bytes 884744 | tf_op jit(solution)/shard_map/ppermute | solution.py:46
  334.6 55.1 %collective-permute-start.54 = (bf16[384,384]{1,0:T(8,128)(2,1)S(1)}, bf16[384,384]{1,0:T(8,128)(2,1)S(1)}, u32[]{:S(2)}, u32[]{:S(2)}) collective-permute-start(bf16[384,384]{1,0:T(8,128)(2,1)S(1)} %copy-done.32), channel_id=1, source_target_pairs={{0,3},{1,2},{2,1},{3,0},{4,7},{5,6},{6,5},{7,4},{8,11},{9,10},{10,... | collective-permute-start | bytes 884744 | tf_op jit(solution)/shard_map/ppermute | solution.py:46
  403.0 30.1 %collective-permute-start.49 = (bf16[256,768]{1,0:T(8,128)(2,1)}, bf16[256,768]{1,0:T(8,128)(2,1)S(1)}, u32[]{:S(2)}, u32[]{:S(2)}) collective-permute-start(bf16[256,768]{1,0:T(8,128)(2,1)} %get-tuple-element.219), channel_id=1, source_target_pairs={{0,2},{1,3},{2,0},{3,1},{4,6},{5,7},{6,4},{7,5},{8,10},{9,11},{10,... | collective-permute-start | bytes 1179656 | tf_op jit(solution)/shard_map/ppermute | solution.py:46
  407.8 26.0 %collective-permute-start.50 = (bf16[256,768]{1,0:T(8,128)(2,1)}, bf16[256,768]{1,0:T(8,128)(2,1)S(1)}, u32[]{:S(2)}, u32[]{:S(2)}) collective-permute-start(bf16[256,768]{1,0:T(8,128)(2,1)} %get-tuple-element.220), channel_id=1, source_target_pairs={{0,3},{1,2},{2,1},{3,0},{4,7},{5,6},{6,5},{7,4},{8,11},{9,10},{10,... | collective-permute-start | bytes 1179656 | tf_op jit(solution)/shard_map/ppermute | solution.py:46
  (117 other events, 1100.8 us)
